TPU v7x, 32 devices: a whole 2x2x4 slice. The times are simulated.
32 devices in a mesh: dp: 4 (over y, x), tensor: 8 (over z, core).
Axes of the slice: x: 2, y: 2, z: 4, core: 2. Of those that a mesh axis runs over, the one named last changes fastest.
Arguments:
- tokens: bfloat16 [8192, 2048], P(('dp', 'tensor')), may hold values from -6 to 6
- cotangent: bfloat16 [8192, 2048], P(('dp', 'tensor'))
- kv_later: bfloat16 [8192, 256], P(('dp', 'tensor')), may hold values from -6 to 6
- lengths: int32 [4, 4], P('dp'), may hold values from 1 to 1984, as said below
- query_weight: float32 [2048, 2048], P('dp', 'tensor'), may hold values from -0.125 to 0.125
- query_moment: float32 [2048, 2048], P('dp', 'tensor'), may hold values from -0.0009765625 to 0.0009765625
- query_average: float32 [2048, 2048], P('dp', 'tensor'), may hold values from -0.125 to 0.125
- keyvalue_weight: float32 [2048, 256], P('dp'), may hold values from -0.125 to 0.125
- keyvalue_moment: float32 [2048, 256], P('dp'), may hold values from -0.0009765625 to 0.0009765625
- keyvalue_average: float32 [2048, 256], P('dp'), may hold values from -0.125 to 0.125
- output_weight: float32 [2048, 2048], P('tensor', 'dp')
- output_moment: float32 [2048, 2048], P('tensor', 'dp'), may hold values from -0.0009765625 to 0.0009765625
- output_average: float32 [2048, 2048], P('tensor', 'dp'), may hold values from -1 to 1
- gateup_weight: float32 [2, 2048, 5632], P(None, 'dp', 'tensor'), may hold values from -0.125 to 0.125
- gateup_moment: float32 [2, 2048, 5632], P(None, 'dp', 'tensor'), may hold values from -0.0009765625 to 0.0009765625
- gateup_average: float32 [2, 2048, 5632], P(None, 'dp', 'tensor'), may hold values from -0.125 to 0.125
- down_weight: float32 [5632, 2048], P('tensor', 'dp')
- down_moment: float32 [5632, 2048], P('tensor', 'dp'), may hold values from -0.0009765625 to 0.0009765625
- down_average: float32 [5632, 2048], P('tensor', 'dp'), may hold values from -0.078125 to 0.078125
- norm_gains: float32 [2, 2048], P(None, 'dp')
- gains_moment: float32 [2, 2048], P(None, 'dp'), may hold values from -0.0009765625 to 0.0009765625
- gains_average: float32 [2, 2048], P(None, 'dp'), may hold values from 0.5 to 1.5
Outputs:
- mixed: float32 [8192, 2048], P(('dp', 'tensor'))
- mixed_low: bfloat16 [8192, 2048], P(('dp', 'tensor'))
- tokens_grad: float32 [8192, 2048], P(('dp', 'tensor'))
- grad_norm: float32 [], replicated
- query_grad: float32 [2048, 2048], P('dp', 'tensor')
- query_moment_new: float32 [2048, 2048], P('dp', 'tensor')
- query_average_new: float32 [2048, 2048], P('dp', 'tensor')
- query_new: float32 [2048, 2048], P('dp', 'tensor')
- query_new_low: bfloat16 [2048, 2048], P('dp', 'tensor')
- keyvalue_grad: float32 [2048, 256], P('dp')
- keyvalue_moment_new: float32 [2048, 256], P('dp')
- keyvalue_average_new: float32 [2048, 256], P('dp')
- keyvalue_new: float32 [2048, 256], P('dp')
- keyvalue_new_low: bfloat16 [2048, 256], P('dp')
- output_grad: float32 [2048, 2048], P('tensor', 'dp')
- output_moment_new: float32 [2048, 2048], P('tensor', 'dp')
- output_average_new: float32 [2048, 2048], P('tensor', 'dp')
- output_new: float32 [2048, 2048], P('tensor', 'dp')
- output_new_low: bfloat16 [2048, 2048], P('tensor', 'dp')
- gateup_grad: float32 [2, 2048, 5632], P(None, 'dp', 'tensor')
- gateup_moment_new: float32 [2, 2048, 5632], P(None, 'dp', 'tensor')
- gateup_average_new: float32 [2, 2048, 5632], P(None, 'dp', 'tensor')
- gateup_new: float32 [2, 2048, 5632], P(None, 'dp', 'tensor')
- gateup_new_low: bfloat16 [2, 2048, 5632], P(None, 'dp', 'tensor')
- down_grad: float32 [5632, 2048], P('tensor', 'dp')
- down_moment_new: float32 [5632, 2048], P('tensor', 'dp')
- down_average_new: float32 [5632, 2048], P('tensor', 'dp')
- down_new: float32 [5632, 2048], P('tensor', 'dp')
- down_new_low: bfloat16 [5632, 2048], P('tensor', 'dp')
- gains_grad: float32 [2, 2048], P(None, 'dp')
- gains_moment_new: float32 [2, 2048], P(None, 'dp')
- gains_average_new: float32 [2, 2048], P(None, 'dp')
- gains_new: float32 [2, 2048], P(None, 'dp')
- gains_new_low: bfloat16 [2, 2048], P(None, 'dp')
Inputs may be any that keep to these rules, and one draw needn't show every extreme that they name: `lengths`: each row sums to 2048; one document of each row has exactly 1984 tokens and the others share the rest.
All inputs are finite; a program needn't handle non-finite values.
Results may differ from a plain program's by a relative error of at most 0.025.
Values may be sent and summed in bfloat16 or wider, within the bound.
A program may use at most 256 MiB of HBM per device.

v0:
```python
import math

import jax
import jax.numpy as jnp
from jax import lax
from jax.sharding import PartitionSpec as P

HD = 128
STEP = 10


EPSILON = 1e-05
MASKED = -1000000000.0
CLIP = 1.0
MOMENTUM = 0.9
LEARNING_RATES = (12.0, 12.0, 480.0, 48.0, 12.0, 960.0)
AVERAGE_TOP = 0.999
ROPE_BASE = 10000.0


def rms_normed(field, gain_row):
    return field * lax.rsqrt(jnp.mean(field * field, axis=-1, keepdims=True) + EPSILON) * gain_row


def doc_layout(doc_lengths, length):
    endings = jnp.cumsum(doc_lengths)
    beginnings = endings - doc_lengths
    places = jnp.arange(length, dtype=jnp.int32)
    segment = jnp.sum((places[:, None] >= endings[None, :]).astype(jnp.int32), axis=1)
    picked = segment[:, None] == jnp.arange(doc_lengths.shape[0], dtype=jnp.int32)[None, :]
    position = places - jnp.sum(jnp.where(picked, beginnings[None, :], 0), axis=1)
    return (segment, position)


def rotary_tables(position):
    half_size = HD // 2
    frequency = jnp.exp(
        jnp.arange(half_size, dtype=jnp.float32) * (-2.0 * math.log(ROPE_BASE) / HD)
    )
    angles = position.astype(jnp.float32)[:, None] * frequency[None, :]
    return (jnp.cos(angles), jnp.sin(angles))


def rotate(field, cosine, sine):
    half_size = field.shape[-1] // 2
    front_part = field[..., :half_size]
    back_part = field[..., half_size:]
    return jnp.concatenate(
        [front_part * cosine - back_part * sine, front_part * sine + back_part * cosine], axis=-1
    )


def visible(begin_row, block_size, segment):
    length = segment.shape[0]
    query_places = begin_row + jnp.arange(block_size, dtype=jnp.int32)
    key_places = jnp.arange(length, dtype=jnp.int32)
    query_segment = lax.dynamic_slice_in_dim(segment, begin_row, block_size)
    return (query_segment[:, None] == segment[None, :]) & (
        key_places[None, :] <= query_places[:, None]
    )


def inner_rows(left_side, right_side):
    return lax.dot_general(
        left_side, right_side, (((0,), (0,)), ((), ())), preferred_element_type=jnp.float32
    )


def outer_cols(left_side, right_side):
    return lax.dot_general(
        left_side, right_side, (((1,), (1,)), ((), ())), preferred_element_type=jnp.float32
    )


def advance(grad_raw, weight, moment, average, factor, rate):
    average_decay = min(AVERAGE_TOP, (1.0 + STEP) / (10.0 + STEP))
    clipped = grad_raw * factor
    moment_new = MOMENTUM * moment + clipped
    weight_new = weight - rate * (clipped + MOMENTUM * moment_new)
    average_new = average_decay * average + (1.0 - average_decay) * weight_new
    return (clipped, moment_new, average_new, weight_new, weight_new.astype(jnp.bfloat16))


def local(
    tokens,
    cotangent,
    kv_later,
    lengths,
    query_weight,
    query_moment,
    query_average,
    keyvalue_weight,
    keyvalue_moment,
    keyvalue_average,
    output_weight,
    output_moment,
    output_average,
    gateup_weight,
    gateup_moment,
    gateup_average,
    down_weight,
    down_moment,
    down_average,
    norm_gains,
    gains_moment,
    gains_average,
):
    masters = (query_weight, keyvalue_weight, output_weight, gateup_weight, down_weight, norm_gains)
    lowered = tuple((weight.astype(jnp.bfloat16) for weight in masters))
    full_query, full_kv, full_output, full_gateup, full_down, full_gains = (
        lax.all_gather(lowered[0], "dp", axis=0, tiled=True),
        lax.all_gather(lowered[1], "dp", axis=0, tiled=True),
        lax.all_gather(lowered[2], "dp", axis=1, tiled=True),
        lax.all_gather(lowered[3], "dp", axis=1, tiled=True),
        lax.all_gather(lowered[4], "dp", axis=1, tiled=True),
        lax.all_gather(lowered[5], "dp", axis=1, tiled=True),
    )
    gain_rows = full_gains.astype(jnp.float32)
    row_count = tokens.shape[0]
    seq_len = row_count * lax.axis_size("tensor")
    own_begin = lax.axis_index("tensor") * row_count
    head_count = full_query.shape[1] // HD
    block_size = min(512, seq_len)
    block_count = seq_len // block_size
    scale_factor = 1.0 / math.sqrt(HD)
    segment, position = doc_layout(lengths[0], seq_len)
    cosine, sine = rotary_tables(position)
    own_cosine = lax.dynamic_slice_in_dim(cosine, own_begin, row_count, 0)
    own_sine = lax.dynamic_slice_in_dim(sine, own_begin, row_count, 0)
    own_tokens = tokens.astype(jnp.float32)
    normed_one = rms_normed(own_tokens, gain_rows[0]).astype(jnp.bfloat16)
    normed_all = lax.all_gather(normed_one, "tensor", axis=0, tiled=True)
    query_pre = jnp.dot(normed_all, full_query, preferred_element_type=jnp.float32)
    kv_pre = jnp.dot(normed_all, full_kv, preferred_element_type=jnp.float32)
    queries = rotate(
        query_pre.reshape(seq_len, head_count, HD).transpose(1, 0, 2), cosine, sine
    ).astype(jnp.bfloat16)
    keys_low = rotate(kv_pre[:, :HD], cosine, sine).astype(jnp.bfloat16)
    values_low = kv_pre[:, HD:].astype(jnp.bfloat16)
    query_blocks = queries.reshape(head_count, block_count, block_size, HD).transpose(1, 0, 2, 3)
    starts = jnp.arange(block_count, dtype=jnp.int32) * block_size

    def block_scores(query_block, begin_row):
        scores = (
            jnp.einsum("hqd,kd->hqk", query_block, keys_low, preferred_element_type=jnp.float32)
            * scale_factor
        )
        return jnp.where(visible(begin_row, block_size, segment)[None], scores, MASKED)

    def forward_block(block_item):
        query_block, begin_row = block_item
        scores = block_scores(query_block, begin_row)
        row_max = jnp.max(scores, axis=-1, keepdims=True)
        log_total = row_max + jnp.log(jnp.sum(jnp.exp(scores - row_max), axis=-1, keepdims=True))
        attn_probs = jnp.exp(scores - log_total)
        mixed_block = jnp.einsum(
            "hqk,kd->hqd",
            attn_probs.astype(jnp.bfloat16),
            values_low,
            preferred_element_type=jnp.float32,
        ).astype(jnp.bfloat16)
        result = (mixed_block, log_total)
        return result

    attended, saved = lax.map(forward_block, (query_blocks, starts))
    attn_rows = attended.transpose(0, 2, 1, 3).reshape(seq_len, head_count * HD)
    hidden_one = own_tokens + lax.psum_scatter(
        jnp.dot(attn_rows, full_output, preferred_element_type=jnp.float32).astype(jnp.bfloat16),
        "tensor",
        scatter_dimension=0,
        tiled=True,
    ).astype(jnp.float32)
    normed_two = rms_normed(hidden_one, gain_rows[1]).astype(jnp.bfloat16)
    normed_mlp = lax.all_gather(normed_two, "tensor", axis=0, tiled=True)
    gate = jnp.dot(normed_mlp, full_gateup[0], preferred_element_type=jnp.float32)
    up_part = jnp.dot(normed_mlp, full_gateup[1], preferred_element_type=jnp.float32)
    middle = (jax.nn.silu(gate) * up_part).astype(jnp.bfloat16)
    mixed = hidden_one + lax.psum_scatter(
        jnp.dot(middle, full_down, preferred_element_type=jnp.float32).astype(jnp.bfloat16),
        "tensor",
        scatter_dimension=0,
        tiled=True,
    ).astype(jnp.float32)
    grad_rows = lax.all_gather(cotangent, "tensor", axis=0, tiled=True)
    grad_down = inner_rows(middle, grad_rows)
    grad_middle = outer_cols(grad_rows, full_down)
    _, silu_pull = jax.vjp(lambda gate_in, up_in: jax.nn.silu(gate_in) * up_in, gate, up_part)
    grad_gate_full, grad_up_full = silu_pull(grad_middle)
    grad_gate = grad_gate_full.astype(jnp.bfloat16)
    grad_up = grad_up_full.astype(jnp.bfloat16)
    grad_gateup = jnp.stack([inner_rows(normed_mlp, grad_gate), inner_rows(normed_mlp, grad_up)])
    grad_normed_two = lax.psum_scatter(
        (outer_cols(grad_gate, full_gateup[0]) + outer_cols(grad_up, full_gateup[1])).astype(
            jnp.bfloat16
        ),
        "tensor",
        scatter_dimension=0,
        tiled=True,
    ).astype(jnp.float32)
    _, second_pull = jax.vjp(rms_normed, hidden_one, gain_rows[1])
    grad_hidden_norm, gain_grad_two = second_pull(grad_normed_two)
    grad_hidden = cotangent.astype(jnp.float32) + grad_hidden_norm
    grad_branch = lax.all_gather(grad_hidden.astype(jnp.bfloat16), "tensor", axis=0, tiled=True)
    grad_output = inner_rows(attn_rows, grad_branch)
    grad_attended = outer_cols(grad_branch, full_output).astype(jnp.bfloat16)
    grad_blocks = grad_attended.reshape(block_count, block_size, head_count, HD).transpose(
        0, 2, 1, 3
    )

    def backward_block(running, block_item):
        key_grad, value_grad = running
        query_block, grad_block, saved_item, begin_row = block_item
        attn_probs = jnp.exp(block_scores(query_block, begin_row) - saved_item)
        value_grad = value_grad + jnp.einsum(
            "hqk,hqd->kd",
            attn_probs.astype(jnp.bfloat16),
            grad_block,
            preferred_element_type=jnp.float32,
        )
        prob_grad = jnp.einsum(
            "hqd,kd->hqk", grad_block, values_low, preferred_element_type=jnp.float32
        )
        score_grad = (
            attn_probs * (prob_grad - jnp.sum(prob_grad * attn_probs, axis=-1, keepdims=True))
        ).astype(jnp.bfloat16)
        query_grad = (
            jnp.einsum("hqk,kd->hqd", score_grad, keys_low, preferred_element_type=jnp.float32)
            * scale_factor
        )
        key_grad = (
            key_grad
            + jnp.einsum("hqk,hqd->kd", score_grad, query_block, preferred_element_type=jnp.float32)
            * scale_factor
        )
        return ((key_grad, value_grad), query_grad)

    zero_rows = jnp.zeros((seq_len, HD), jnp.float32)
    (key_grad, value_grad), query_grads = lax.scan(
        backward_block, (zero_rows, zero_rows), (query_blocks, grad_blocks, saved, starts)
    )
    query_grads = query_grads.transpose(1, 0, 2, 3).reshape(head_count, seq_len, HD)
    grad_query_pre = (
        rotate(query_grads, cosine, -sine)
        .transpose(1, 0, 2)
        .reshape(seq_len, head_count * HD)
        .astype(jnp.bfloat16)
    )
    grad_query = inner_rows(normed_all, grad_query_pre)
    normed_part = outer_cols(grad_query_pre, full_query)
    summed_normed, summed_keys, summed_values = (
        lax.psum_scatter(
            normed_part.astype(jnp.bfloat16), "tensor", scatter_dimension=0, tiled=True
        ).astype(jnp.float32),
        lax.psum_scatter(
            key_grad.astype(jnp.bfloat16), "tensor", scatter_dimension=0, tiled=True
        ).astype(jnp.float32),
        lax.psum_scatter(
            value_grad.astype(jnp.bfloat16), "tensor", scatter_dimension=0, tiled=True
        ).astype(jnp.float32),
    )
    later_rows = kv_later.astype(jnp.float32)
    key_total = summed_keys + later_rows[:, :HD]
    value_total = summed_values + later_rows[:, HD:]
    grad_kv_pre = jnp.concatenate(
        [rotate(key_total, own_cosine, -own_sine), value_total], axis=-1
    ).astype(jnp.bfloat16)
    grad_normed_one = summed_normed + outer_cols(grad_kv_pre, full_kv)
    grad_keyvalue_part = inner_rows(normed_one, grad_kv_pre)
    _, first_pull = jax.vjp(rms_normed, own_tokens, gain_rows[0])
    grad_token_norm, gain_grad_one = first_pull(grad_normed_one)
    tokens_grad = grad_hidden + grad_token_norm
    kv_total, gains_total = lax.psum(
        (grad_keyvalue_part, jnp.stack([gain_grad_one, gain_grad_two])), ("dp", "tensor")
    )
    dp_index = lax.axis_index("dp")
    kv_shard = keyvalue_weight.shape[0]
    gains_shard = norm_gains.shape[1]
    grad_keyvalue = lax.dynamic_slice_in_dim(kv_total, dp_index * kv_shard, kv_shard, 0)
    grad_gains = lax.dynamic_slice_in_dim(gains_total, dp_index * gains_shard, gains_shard, 1)
    local_grads = (grad_query, grad_output, grad_gateup, grad_down)
    whole_query, whole_output, whole_gateup, whole_down = (
        lax.psum(local_grads[0].astype(jnp.bfloat16), "dp").astype(jnp.float32),
        lax.psum(local_grads[1].astype(jnp.bfloat16), "dp").astype(jnp.float32),
        lax.psum(local_grads[2].astype(jnp.bfloat16), "dp").astype(jnp.float32),
        lax.psum(local_grads[3].astype(jnp.bfloat16), "dp").astype(jnp.float32),
    )
    own_query = lax.dynamic_slice_in_dim(
        whole_query, dp_index * query_weight.shape[0], query_weight.shape[0], 0
    )
    own_output = lax.dynamic_slice_in_dim(
        whole_output, dp_index * output_weight.shape[1], output_weight.shape[1], 1
    )
    own_gateup = lax.dynamic_slice_in_dim(
        whole_gateup, dp_index * gateup_weight.shape[1], gateup_weight.shape[1], 1
    )
    own_down = lax.dynamic_slice_in_dim(
        whole_down, dp_index * down_weight.shape[1], down_weight.shape[1], 1
    )
    split_squares = (
        jnp.sum(own_query * own_query)
        + jnp.sum(own_output * own_output)
        + jnp.sum(own_gateup * own_gateup)
        + jnp.sum(own_down * own_down)
    )
    shared_squares = jnp.sum(grad_keyvalue * grad_keyvalue) + jnp.sum(grad_gains * grad_gains)
    local_squares = split_squares + shared_squares / lax.axis_size("tensor")
    grad_norm = jnp.sqrt(lax.psum(local_squares, ("dp", "tensor")))
    factor = jnp.minimum(1.0, CLIP / (grad_norm + 1e-06))
    query_set = advance(
        own_query, query_weight, query_moment, query_average, factor, LEARNING_RATES[0]
    )
    keyvalue_set = advance(
        grad_keyvalue, keyvalue_weight, keyvalue_moment, keyvalue_average, factor, LEARNING_RATES[1]
    )
    output_set = advance(
        own_output, output_weight, output_moment, output_average, factor, LEARNING_RATES[2]
    )
    gateup_set = advance(
        own_gateup, gateup_weight, gateup_moment, gateup_average, factor, LEARNING_RATES[3]
    )
    down_set = advance(own_down, down_weight, down_moment, down_average, factor, LEARNING_RATES[4])
    gains_set = advance(
        grad_gains, norm_gains, gains_moment, gains_average, factor, LEARNING_RATES[5]
    )
    return (
        mixed,
        mixed.astype(jnp.bfloat16),
        tokens_grad,
        grad_norm,
        query_set[0],
        query_set[1],
        query_set[2],
        query_set[3],
        query_set[4],
        keyvalue_set[0],
        keyvalue_set[1],
        keyvalue_set[2],
        keyvalue_set[3],
        keyvalue_set[4],
        output_set[0],
        output_set[1],
        output_set[2],
        output_set[3],
        output_set[4],
        gateup_set[0],
        gateup_set[1],
        gateup_set[2],
        gateup_set[3],
        gateup_set[4],
        down_set[0],
        down_set[1],
        down_set[2],
        down_set[3],
        down_set[4],
        gains_set[0],
        gains_set[1],
        gains_set[2],
        gains_set[3],
        gains_set[4],
    )


def solution(mesh):
    return jax.shard_map(
        local,
        mesh=mesh,
        in_specs=(
            P(("dp", "tensor"), None),
            P(("dp", "tensor"), None),
            P(("dp", "tensor"), None),
            P("dp", None),
            P("dp", "tensor"),
            P("dp", "tensor"),
            P("dp", "tensor"),
            P("dp", None),
            P("dp", None),
            P("dp", None),
            P("tensor", "dp"),
            P("tensor", "dp"),
            P("tensor", "dp"),
            P(None, "dp", "tensor"),
            P(None, "dp", "tensor"),
            P(None, "dp", "tensor"),
            P("tensor", "dp"),
            P("tensor", "dp"),
            P("tensor", "dp"),
            P(None, "dp"),
            P(None, "dp"),
            P(None, "dp"),
        ),
        out_specs=(
            P(("dp", "tensor"), None),
            P(("dp", "tensor"), None),
            P(("dp", "tensor"), None),
            P(),
            P("dp", "tensor"),
            P("dp", "tensor"),
            P("dp", "tensor"),
            P("dp", "tensor"),
            P("dp", "tensor"),
            P("dp", None),
            P("dp", None),
            P("dp", None),
            P("dp", None),
            P("dp", None),
            P("tensor", "dp"),
            P("tensor", "dp"),
            P("tensor", "dp"),
            P("tensor", "dp"),
            P("tensor", "dp"),
            P(None, "dp", "tensor"),
            P(None, "dp", "tensor"),
            P(None, "dp", "tensor"),
            P(None, "dp", "tensor"),
            P(None, "dp", "tensor"),
            P("tensor", "dp"),
            P("tensor", "dp"),
            P("tensor", "dp"),
            P("tensor", "dp"),
            P("tensor", "dp"),
            P(None, "dp"),
            P(None, "dp"),
            P(None, "dp"),
            P(None, "dp"),
            P(None, "dp"),
        ),
        check_vma=False,
    )
```

profile of v0, /device:TPU:0, one launch (start us, length us, event | category | flops | bytes accessed | tf_op | source)
XLA Modules:
  0.0 1543.7 jit_solution(17135785860693606377)
XLA Ops:
  9.9 9.5 all_gather.30
  26.2 13.7 all-gather.14.cloned.1.call-done
  39.9 84.3 %all-gather.10.cloned.1.call-done = bf16[2048,2048]{1,0:T(8,128)(2,1)} async-done(((bf16[256,2048]{1,0:T(8,128)(2,1)}), bf16[2048,2048]{1,0:T(8,128)(2,1)}) %all-gather.10.cloned.1.call-update) | async-done | bytes 8388624 | tf_op jit(solution)/shard_map/all_gather | solution.py:132
  139.5 12.3 all-gather.12.cloned.1.call-done
  151.8 7.3 fusion.101
  169.6 49.8 %while.27 = (s32[]{:T(128)}, bf16[4,2,512,128]{3,2,1,0:T(8,128)(2,1)}, f32[4,2,512,1]{2,1,3,0:T(2,128)S(1)}, s32[4]{0:T(128)S(1)}, s32[2048]{0:T(1024)S(1)}, /*i...) while((s32[]{:T(128)}, ...), condition=%wide.region_7.8_spmd, body=%wide.region_4.7_spmd.sunk | while | flops 1100086784 | bytes 30984376 | solution.py:165
  222.7 7.2 convolution_convert_fusion.2
  233.3 86.4 %reduce-scatter.7.cloned.1.call-done = bf16[256,2048]{1,0:T(8,128)(2,1)} async-done(((bf16[2048,2048]{1,0:T(8,128)(2,1)}), bf16[256,2048]{1,0:T(8,128)(2,1)}) %reduce-scatter.7.cloned.1.call-update) | async-done | bytes 1048592 | tf_op jit(solution)/shard_map/reduce_scatter | solution.py:167
  325.8 60.2 %all-gather.20.cloned.1.call-done = bf16[2,2048,704]{1,2,0:T(8,128)(2,1)} async-done(((bf16[2,512,704]{1,2,0:T(8,128)(2,1)}), bf16[2,2048,704]{1,2,0:T(8,128)(2,1)}) %all-gather.20.cloned.1.call-update) | async-done | bytes 5767184 | tf_op jit(solution)/shard_map/all_gather | solution.py:114
  386.0 84.3 %all-gather.18.cloned.1.call-done = bf16[2048,2048]{1,0:T(8,128)(2,1)} async-done(((bf16[256,2048]{1,0:T(8,128)(2,1)}), bf16[2048,2048]{1,0:T(8,128)(2,1)}) %all-gather.18.cloned.1.call-update) | async-done | bytes 8388624 | tf_op jit(solution)/shard_map/all_gather | solution.py:174
  470.3 12.1 fusion.58
  482.4 8.0 fusion.57
  490.4 22.5 %all-gather.22.cloned.1.call-done = bf16[704,2048]{1,0:T(8,128)(2,1)} async-done(((bf16[704,512]{1,0:T(8,128)(2,1)}), bf16[704,2048]{1,0:T(8,128)(2,1)}) %all-gather.22.cloned.1.call-update) | async-done | bytes 2883600 | tf_op jit(solution)/shard_map/all_gather | solution.py:115
  512.9 83.7 %all-gather.24.cloned.1.call-done = bf16[2048,2048]{1,0:T(8,128)(2,1)} async-done(((bf16[256,2048]{1,0:T(8,128)(2,1)}), bf16[2048,2048]{1,0:T(8,128)(2,1)}) %all-gather.24.cloned.1.call-update) | async-done | bytes 8388624 | tf_op jit(solution)/shard_map/all_gather | solution.py:184
  596.6 15.1 multiply_convert_fusion.1
  611.7 14.2 fusion.56
  625.9 13.2 add_convert_fusion
  639.1 88.3 %reduce-scatter.11.cloned.1.call-done = bf16[256,2048]{1,0:T(8,128)(2,1)} async-done(((bf16[2048,2048]{1,0:T(8,128)(2,1)}), bf16[256,2048]{1,0:T(8,128)(2,1)}) %reduce-scatter.11.cloned.1.call-update) | async-done | bytes 1048592 | tf_op jit(solution)/shard_map/reduce_scatter | solution.py:192
  735.2 11.1 fusion.54
  746.3 10.9 fusion.53
  757.2 56.3 %all-gather.26.cloned.1.call-done = bf16[2048,2048]{1,0:T(8,128)(2,1)} async-done(((bf16[256,2048]{1,0:T(8,128)(2,1)}), bf16[2048,2048]{1,0:T(8,128)(2,1)}) %all-gather.26.cloned.1.call-update) | async-done | bytes 8388624 | tf_op jit(solution)/shard_map/all_gather | solution.py:203
  813.6 6.7 convolution_convert_fusion.8
  824.9 80.0 %while.28 = (s32[]{:T(128)}, f32[2048,128]{1,0:T(8,128)S(1)}, f32[2048,128]{1,0:T(8,128)}, f32[4,2,512,128]{3,2,0,1:T(8,128)}, s32[4]{0:T(128)S(1)}, /*index=5*/...) while((s32[]{:T(128)}, f32[2048,128]{1,0:T(8,128)S(1)}, ...), condition=%wide.region_15.16_spmd.clone, body=%wide.region_13.15_spmd.clone.sunk | while | flops 2720398848 | bytes 78690552 | solution.py:238
  905.9 11.0 convolution_convert_fusion.5
  935.5 32.1 %reduce-scatter.17.cloned.1.call-done = bf16[256,128]{0,1:T(8,128)(2,1)} async-done(((bf16[2048,128]{0,1:T(8,128)(2,1)}), bf16[256,128]{0,1:T(8,128)(2,1)}) %reduce-scatter.17.cloned.1.call-update) | async-done | bytes 65552 | tf_op jit(solution)/shard_map/reduce_scatter | solution.py:257
  975.5 7.2 convolution_convert_fusion.7
  991.5 10.9 convolution_convert_fusion.1
  1002.4 102.9 %all-reduce.4.cloned.1.call-done = f32[2048,256]{1,0:T(8,128)} async-done(((f32[2048,256]{1,0:T(8,128)}), f32[2048,256]{1,0:T(8,128)}) %all-reduce.4.cloned.1.call-update) | async-done | bytes 2097168 | tf_op jit(solution)/shard_map/psum | solution.py:272
  1107.1 215.3 %all-reduce.6.cloned.1.call-done = (bf16[2048,256]{1,0:T(8,128)(2,1)}, bf16[256,2048]{1,0:T(8,128)(2,1)}, bf16[2,2048,704]{1,2,0:T(8,128)(2,1)}, bf16[704,2048]{1,0:T(8,128)(2,1)}) async-done(((bf16[2048,256]{1,0:T(8,128)(2,1)}, bf16[256,2048]{1,0:T(8,128)(2,1)}, bf16[2,2048,704]{1,2,0:T(8,128)(2,1)}, bf16[704,2048]{1,0:T(8,128)(2,1)}), (bf16[2048,256]{1,0:T(8,128)(2,1)}, bf16[256,2048]{1,0:T(8,128)(2,1)}, ...) | async-done | bytes 10747920 | tf_op jit(solution)/shard_map/psum | solution.py:282
  1333.5 81.4 %reduce-scatter.13.cloned.1.call-done = bf16[256,2048]{1,0:T(8,128)(2,1)} async-done(((bf16[2048,2048]{1,0:T(8,128)(2,1)}), bf16[256,2048]{1,0:T(8,128)(2,1)}) %reduce-scatter.13.cloned.1.call-update) | async-done | bytes 1048592 | tf_op jit(solution)/shard_map/reduce_scatter | solution.py:251
  1418.7 39.6 %psum.54 = f32[2,2048]{1,0:T(2,128)S(1)} all-reduce(f32[2,2048]{1,0:T(2,128)S(1)} %pad_maximum_fusion.5), channel_id=1, replica_groups=mesh['dp'=4,'tensor'=8] {'dp','tensor'}, use_global_device_ids=true, to_apply=%region_32.33 | all-reduce | flops 4096 | bytes 32768 | tf_op jit(solution)/shard_map/psum | solution.py:272
  1460.2 43.2 %psum.55 = f32[]{:T(128)} all-reduce(f32[]{:T(128)S(6)} %add.251), channel_id=1, replica_groups=mesh['dp'=4,'tensor'=8] {'dp','tensor'}, use_global_device_ids=true, to_apply=%region_34.35 | all-reduce | flops 1 | bytes 8 | tf_op jit(solution)/shard_map/psum | solution.py:307
  (345 shorter events, 255.8 us)
Async XLA Ops:
  7.2 32.7 %all-gather.14.cloned.1.call-start = ((), (), s32[]{:S(2)}) async-start(), calls=%async_computation.8 | async-start | bytes 1310720 | tf_op jit(solution)/shard_map/all_gather | solution.py:112
  9.1 115.0 %all-gather.10.cloned.1.call-start = ((), (), s32[]{:S(2)}) async-start(), calls=%async_computation.6 | async-start | bytes 9437184 | tf_op jit(solution)/shard_map/all_gather | solution.py:132
  21.6 708.8 %copy-start.48 = (f32[1,2048]{1,0:T(1,128)}, f32[1,2048]{1,0:T(1,128)S(1)}, u32[]{:S(2)}) copy-start(f32[1,2048]{1,0:T(1,128)S(1)} %get-tuple-element.350) | copy-start | bytes 24580
  24.1 127.7 %all-gather.12.cloned.1.call-start = ((), (), s32[]{:S(2)}) async-start(), calls=%async_computation.7 | async-start | bytes 1310720 | tf_op jit(solution)/shard_map/all_gather | solution.py:111
  24.9 197.7 %all-gather.16.cloned.1.call-start = ((), (), s32[]{:S(2)}) async-start(), calls=%async_computation.9 | async-start | bytes 1310720 | tf_op jit(solution)/shard_map/all_gather | solution.py:113
  25.7 294.0 %reduce-scatter.7.cloned.1.call-start = ((), (), s32[]{:S(2)}) async-start(), calls=%async_computation.10 | async-start | bytes 9437184 | tf_op jit(solution)/shard_map/reduce_scatter | solution.py:167
  229.9 89.8 %copy-start = (bf16[256,2048]{1,0:T(8,128)(2,1)S(1)}, bf16[256,2048]{1,0:T(8,128)(2,1)}, u32[]{:S(2)}) copy-start(bf16[256,2048]{1,0:T(8,128)(2,1)} %param.26) | copy-start | bytes 3145732
  229.9 156.0 %all-gather.20.cloned.1.call-start = ((), (), s32[]{:S(2)}) async-start(), calls=%async_computation.12 | async-start | bytes 7208960 | tf_op jit(solution)/shard_map/all_gather | solution.py:114
  233.2 90.8 %copy-start.18 = (f32[704,512]{1,0:T(8,128)S(1)}, f32[704,512]{1,0:T(8,128)}, u32[]{:S(2)}) copy-start(f32[704,512]{1,0:T(8,128)} %param.42) | copy-start | bytes 4325380
  233.2 237.1 %all-gather.18.cloned.1.call-start = ((), (), s32[]{:S(2)}) async-start(), calls=%async_computation.11 | async-start | bytes 9437184 | tf_op jit(solution)/shard_map/all_gather | solution.py:174
  321.4 409.0 %copy-start.54 = (f32[256]{0:T(256)}, f32[256]{0:T(256)S(1)}, u32[]{:S(2)}) copy-start(f32[256]{0:T(256)S(1)} %fusion.88) | copy-start | bytes 3076
  324.0 188.9 %all-gather.22.cloned.1.call-start = ((), (), s32[]{:S(2)}) async-start(), calls=%async_computation.13 | async-start | bytes 3604480 | tf_op jit(solution)/shard_map/all_gather | solution.py:115
  325.0 271.6 %all-gather.24.cloned.1.call-start = ((), (), s32[]{:S(2)}) async-start(), calls=%async_computation.15 | async-start | bytes 9437184 | tf_op jit(solution)/shard_map/all_gather | solution.py:184
  325.8 401.6 %reduce-scatter.11.cloned.1.call-start = ((), (), s32[]{:S(2)}) async-start(), calls=%async_computation.16 | async-start | bytes 9437184 | tf_op jit(solution)/shard_map/reduce_scatter | solution.py:192
  639.1 174.5 %all-gather.26.cloned.1.call-start = ((), (), s32[]{:S(2)}) async-start(), calls=%async_computation.17 | async-start | bytes 9437184 | tf_op jit(solution)/shard_map/all_gather | solution.py:203
  733.0 202.5 %reduce-scatter.15.cloned.1.call-start = ((), (), s32[]{:S(2)}) async-start(), calls=%async_computation.19 | async-start | bytes 589824 | tf_op jit(solution)/shard_map/reduce_scatter | solution.py:254
  905.9 61.7 %reduce-scatter.17.cloned.1.call-start = ((), (), s32[]{:S(2)}) async-start(), calls=%async_computation.20 | async-start | bytes 589824 | tf_op jit(solution)/shard_map/reduce_scatter | solution.py:257
  919.2 186.1 %all-reduce.4.cloned.1.call-start = ((), (), s32[]{:S(2)}) async-start(), calls=%async_computation.21 | async-start | bytes 4194304 | tf_op jit(solution)/shard_map/psum | solution.py:272
  971.4 351.0 %all-reduce.6.cloned.1.call-start = ((), (), s32[]{:S(2)}) async-start(), calls=%async_computation.22 | async-start | bytes 21495808 | tf_op jit(solution)/shard_map/psum | solution.py:282
  982.7 432.1 %reduce-scatter.13.cloned.1.call-start = ((), (), s32[]{:S(2)}) async-start(), calls=%async_computation.18 | async-start | bytes 9437184 | tf_op jit(solution)/shard_map/reduce_scatter | solution.py:251
  989.7 540.0 %reduce-scatter.9.cloned.1.call-start = ((), (), s32[]{:S(2)}) async-start(), calls=%async_computation.14 | async-start | bytes 9437184 | tf_op jit(solution)/shard_map/reduce_scatter | solution.py:178
  1002.4 412.5 %copy-start.1 = (bf16[256,2048]{1,0:T(8,128)(2,1)S(1)}, bf16[256,2048]{1,0:T(8,128)(2,1)}, u32[]{:S(2)}) copy-start(bf16[256,2048]{1,0:T(8,128)(2,1)} %param.26) | copy-start | bytes 3145732
  1002.4 412.5 %copy-start.52 = (f32[1,2048]{1,0:T(1,128)S(1)}, f32[1,2048]{1,0:T(1,128)}, u32[]{:S(2)}) copy-start(f32[1,2048]{1,0:T(1,128)} %copy-done.51) | copy-start | bytes 24580
  1002.4 412.4 %copy-start.61 = (f32[256]{0:T(256)S(1)}, f32[256]{0:T(256)}, u32[]{:S(2)}) copy-start(f32[256]{0:T(256)} %copy-done.60) | copy-start | bytes 3076
  1333.4 170.7 %copy-start.63 = (f32[256]{0:T(256)S(1)}, f32[256]{0:T(256)}, u32[]{:S(2)}) copy-start(f32[256]{0:T(256)} %copy-done.62) | copy-start | bytes 3076
  1333.4 170.8 %copy-start.57 = (f32[2,512]{1,0:T(2,128)S(1)}, f32[2,512]{1,0:T(2,128)}, u32[]{:S(2)}) copy-start(f32[2,512]{1,0:T(2,128)} %param.45) | copy-start | bytes 12292
  1333.4 170.8 %copy-start.64 = (f32[2,512]{1,0:T(2,128)S(1)}, f32[2,512]{1,0:T(2,128)}, u32[]{:S(2)}) copy-start(f32[2,512]{1,0:T(2,128)} %param.46) | copy-start | bytes 12292
  1333.4 171.4 %copy-start.65 = (f32[2,512]{1,0:T(2,128)S(1)}, f32[2,512]{1,0:T(2,128)}, u32[]{:S(2)}) copy-start(f32[2,512]{1,0:T(2,128)} %param.47) | copy-start | bytes 12292
  1333.4 172.0 %copy-start.33 = (f32[512,256]{1,0:T(8,128)S(1)}, f32[512,256]{1,0:T(8,128)}, u32[]{:S(2)}) copy-start(f32[512,256]{1,0:T(8,128)} %param.33) | copy-start | bytes 1572868
  1333.5 171.9 %copy-start.35 = (f32[512,256]{1,0:T(8,128)S(1)}, f32[512,256]{1,0:T(8,128)}, u32[]{:S(2)}) copy-start(f32[512,256]{1,0:T(8,128)} %param.30) | copy-start | bytes 1572868
  1333.5 171.9 %copy-start.46 = (f32[512,256]{1,0:T(8,128)S(1)}, f32[512,256]{1,0:T(8,128)}, u32[]{:S(2)}) copy-start(f32[512,256]{1,0:T(8,128)} %param.34) | copy-start | bytes 1572868
  1333.5 171.9 %copy-start.47 = (f32[512,256]{1,0:T(8,128)S(1)}, f32[512,256]{1,0:T(8,128)}, u32[]{:S(2)}) copy-start(f32[512,256]{1,0:T(8,128)} %param.31) | copy-start | bytes 1572868
  (61 other events, 637.0 us)
Sparse Core Ops, SparseCore 0:
  10.5 29.3 all-gather.13
  42.1 82.0 all-gather.9
  126.6 25.1 all-gather.11
  154.0 26.4 all-gather.15
  230.1 89.5 reduce-scatter.6
  322.0 63.9 all-gather.19
  388.2 82.0 all-gather.17
  472.7 40.1 all-gather.21
  514.5 82.0 all-gather.23
  639.2 88.1 reduce-scatter.10
  733.1 80.4 all-gather.25
  906.0 29.4 reduce-scatter.14
  938.4 29.0 reduce-scatter.16
  973.3 131.9 all-reduce.3
  1111.4 210.9 all-reduce.5
  1324.5 90.2 reduce-scatter.12
  1417.0 90.0 reduce-scatter.8
where the time goes:
time: 1550 us; the launch traced here: 1540 us
  waiting for transfers between devices  1030 us (66%)
  matrix products  228 us (15%)
  other arithmetic  117 us (8%)
  blocking collectives  92.3 us (6%)
  local copies, waits for them, and re-layouts  37.8 us (2%)
  between operations  20.7 us (1%)
  loops' own time  16.5 us (1%)
    psum x1, waiting for transfers between devices, local(): lax.psum(local_grads[0].astype(jnp.bfloat16), 'dp').astype(jnp.float32)  215 us
    psum x1, waiting for transfers between devices, local(): lax.psum((grad_keyvalue_part, jnp.stack([gain_grad_one, gain_grad_two])),...  103 us
    reduce_scatter x1, waiting for transfers between devices, local(): lax.psum_scatter((outer_cols(grad_gate, full_gateup[0]) + outer_cols(grad...  88.3 us
    reduce_scatter x1, waiting for transfers between devices, local(): lax.psum_scatter(jnp.dot(attn_rows, full_output, preferred_element_type=j...  86.4 us
    all_gather x1, waiting for transfers between devices, local(): normed_mlp = lax.all_gather(normed_two, 'tensor', axis=0, tiled=True)  84.3 us
    all_gather x1, waiting for transfers between devices, local(): normed_all = lax.all_gather(normed_one, 'tensor', axis=0, tiled=True)  84.3 us
    all_gather x1, waiting for transfers between devices, local(): grad_rows = lax.all_gather(cotangent, 'tensor', axis=0, tiled=True)  83.7 us
    reduce_scatter x1, waiting for transfers between devices, local(): lax.psum_scatter(normed_part.astype(jnp.bfloat16), 'tensor', scatter_dime...  81.4 us
  transfers between devices with their start and end apart: 17, of which 15 were waited for; matrix products, arithmetic and copies ran while one was open for 14% of the time, Pallas kernels for 0%

commit v1 on v0

--- a/solution.py
+++ b/solution.py
@@ -1,8 +1,11 @@
+import functools
 import math
 
 import jax
 import jax.numpy as jnp
 from jax import lax
+from jax.experimental import pallas as pl
+from jax.experimental.pallas import tpu as pltpu
 from jax.sharding import PartitionSpec as P
 
 HD = 128
@@ -16,6 +19,400 @@
 LEARNING_RATES = (12.0, 12.0, 480.0, 48.0, 12.0, 960.0)
 AVERAGE_TOP = 0.999
 ROPE_BASE = 10000.0
+
+MESH = pl.DeviceIdType.MESH
+LOW = jnp.bfloat16
+F32 = jnp.float32
+
+
+def dot_nn(a, b):
+    return jnp.dot(a, b, preferred_element_type=F32)
+
+
+def dot_nt(a, b):
+    return lax.dot_general(a, b, (((1,), (1,)), ((), ())), preferred_element_type=F32)
+
+
+def dot_tn(a, b):
+    return lax.dot_general(a, b, (((0,), (0,)), ((), ())), preferred_element_type=F32)
+
+
+class Place:
+    def __init__(self, nd, nt):
+        self.nd, self.nt = nd, nt
+        self.nx = 2 if nd % 2 == 0 else 1
+        self.ny = nd // self.nx
+        self.nz = nt // 2
+        self.dp = lax.axis_index("dp")
+        self.t = lax.axis_index("tensor")
+        self.y = self.dp // self.nx
+        self.x = lax.rem(self.dp, self.nx)
+        self.z = self.t // 2
+        self.c = lax.rem(self.t, 2)
+
+    def x_peer(self):
+        return self.y * self.nx + (1 - self.x)
+
+    def y_peer(self, step):
+        return lax.rem(self.y + step, self.ny) * self.nx + self.x
+
+    def xy_peer(self, step):
+        return lax.rem(self.y + step, self.ny) * self.nx + (1 - self.x)
+
+    def sibling(self):
+        return self.z * 2 + (1 - self.c)
+
+
+def remote(src, dst, send, recv, dp, t):
+    return pltpu.make_async_remote_copy(src, dst, send, recv, device_id=(dp, t), device_id_type=MESH)
+
+
+def greet(at, dps=True, zs=True, core=True):
+    bar = pltpu.get_barrier_semaphore()
+    count = 0
+    targets = []
+    if dps:
+        targets.append((at.x_peer(), at.t))
+        targets += [(at.y_peer(s), at.t) for s in range(1, at.ny)]
+    if core:
+        targets.append((at.dp, at.sibling()))
+    for target in targets:
+        pl.semaphore_signal(bar, inc=1, device_id=target, device_id_type=MESH)
+        count += 1
+    if zs:
+        @pl.when(at.z > 0)
+        def _():
+            pl.semaphore_signal(bar, inc=1, device_id=(at.dp, at.t - 2), device_id_type=MESH)
+
+        @pl.when(at.z < at.nz - 1)
+        def _():
+            pl.semaphore_signal(bar, inc=1, device_id=(at.dp, at.t + 2), device_id_type=MESH)
+
+        count = count + (at.z > 0).astype(jnp.int32) + (at.z < at.nz - 1).astype(jnp.int32)
+    pl.semaphore_wait(bar, count)
+
+
+def far_first(k, z, nz):
+    j = nz - 1 - k
+    m = jnp.minimum(z, nz - 1 - z)
+    s = (j + 1) // 2
+    two = jnp.where(lax.rem(j, 2) == 1, z - s, z + s)
+    one = jnp.where(z < nz - 1 - z, j, nz - 1 - j)
+    return jnp.where(j <= 2 * m, two, one)
+
+
+class Gather:
+    def __init__(self, at, src, dst, xs, ys, xf, yf, recv, kind):
+        self.at, self.src, self.dst, self.kind = at, src, dst, kind
+        self.xs, self.ys, self.xf, self.yf, self.recv = xs, ys, xf, yf, recv
+
+    def own(self):
+        at = self.at
+        out = [remote(self.src, self.dst(at.dp), self.xs, self.recv.at[at.dp], at.x_peer(), at.t)]
+        for s in range(1, at.ny):
+            out.append(remote(self.src, self.dst(at.dp), self.ys.at[s - 1], self.recv.at[at.dp], at.y_peer(s), at.t))
+        return out
+
+    def passed(self):
+        at = self.at
+        out = []
+        for s in range(1, at.ny):
+            if self.kind == 0:
+                o = at.x_peer()
+                out.append(remote(self.dst(o), self.dst(o), self.yf.at[s - 1], self.recv.at[o], at.y_peer(s), at.t))
+            else:
+                o = at.y_peer(s)
+                out.append(remote(self.dst(o), self.dst(o), self.xf.at[s - 1], self.recv.at[o], at.x_peer(), at.t))
+        return out
+
+    def arrived(self, o):
+        remote(self.src, self.dst(o), self.xs, self.recv.at[o], self.at.x_peer(), self.at.t).wait_recv()
+
+    def start(self):
+        for cp in self.own():
+            cp.start()
+
+    def forward(self):
+        at = self.at
+        if self.kind == 0:
+            self.arrived(at.x_peer())
+        else:
+            for s in range(1, at.ny):
+                self.arrived(at.y_peer(s))
+        for cp in self.passed():
+            cp.start()
+
+    def finish(self):
+        at = self.at
+        if self.kind == 0:
+            for s in range(1, at.ny):
+                self.arrived(at.y_peer(s))
+        else:
+            self.arrived(at.x_peer())
+        for s in range(1, at.ny):
+            self.arrived(at.xy_peer(s))
+
+    def drain(self):
+        for cp in self.own() + self.passed():
+            cp.wait_send()
+
+
+def mlp_kernel(nd, nt, xn_in, dy_in, wgu_in, wd_in,
+               dxn_out, dwgu_out, dwd_out, out_out,
+               xall, dyv, wgu, wd, mid, dg, du, psend, pown, precv, zrecv, stage,
+               lsem, wx, wy, wxf, wyf, wr, ar, ac, asr, asl, ps, pr, zs, zr, osem, wsem):
+    at = Place(nd, nt)
+    nz = at.nz
+    R, D = xn_in.shape
+    Dd = wgu_in.shape[1]
+    F = wgu_in.shape[2]
+    Fh = F // 2
+    rows = lambda t: pl.ds(pl.multiple_of(t * R, R), R)
+    dcols = lambda o: pl.ds(pl.multiple_of(o * Dd, Dd), Dd)
+
+    own_loads = [
+        pltpu.make_async_copy(xn_in, xall.at[rows(at.t)], lsem.at[0]),
+        pltpu.make_async_copy(dy_in, dyv, lsem.at[1]),
+        pltpu.make_async_copy(wgu_in, wgu.at[:, dcols(at.dp)], lsem.at[2]),
+        pltpu.make_async_copy(wd_in, wd.at[at.dp], lsem.at[3]),
+    ]
+    for cp in own_loads:
+        cp.start()
+    greet(at)
+
+    gathers = []
+    for p in range(2):
+        gathers.append(Gather(at, wgu_in.at[p], lambda o, p=p: wgu.at[p, dcols(o)],
+                              wx.at[p], wy.at[p], wxf.at[p], wyf.at[p], wr.at[p], p))
+    for p in range(2):
+        gathers.append(Gather(at, wd_in.at[pl.ds(p * Fh, Fh)], lambda o, p=p: wd.at[o, pl.ds(p * Fh, Fh)],
+                              wx.at[2 + p], wy.at[2 + p], wxf.at[2 + p], wyf.at[2 + p], wr.at[2 + p], p))
+
+    def right(o):
+        return remote(xall.at[rows(o)], xall.at[rows(o)], asr.at[o], ar.at[o], at.dp, at.t + 2)
+
+    def left(o):
+        return remote(xall.at[rows(o)], xall.at[rows(o)], asl.at[o], ar.at[o], at.dp, at.t - 2)
+
+    def across(o):
+        return remote(xall.at[rows(o)], xall.at[rows(o)], ac.at[o], ar.at[o], at.dp, at.sibling())
+
+    own_loads[0].wait()
+    across(at.t).start()
+    pl.when(at.z < nz - 1)(lambda: right(at.t).start())
+    pl.when(at.z > 0)(lambda: left(at.t).start())
+    for g in gathers[:2]:
+        g.start()
+    for g in gathers[2:]:
+        g.start()
+
+    def line_step(s):
+        @pl.when(at.z - s >= 0)
+        def _():
+            o = at.t - 2 * s
+            across(o).wait_recv()
+            pl.when(at.z < nz - 1)(lambda: right(o).start())
+            across(o).start()
+
+        @pl.when(at.z + s < nz)
+        def _():
+            o = at.t + 2 * s
+            across(o).wait_recv()
+            pl.when(at.z > 0)(lambda: left(o).start())
+            across(o).start()
+
+    for g in gathers[:2]:
+        g.forward()
+    line_step(1)
+    for g in gathers[2:]:
+        g.forward()
+    for s in range(2, nz):
+        line_step(s)
+    for cp in own_loads[1:]:
+        cp.wait()
+    for g in gathers:
+        g.finish()
+    for zz in range(nz):
+        across(2 * zz + (1 - at.c)).wait_recv()
+
+    def swap(d, slot):
+        return remote(psend.at[slot], precv.at[d], ps.at[slot], pr.at[d], at.dp, at.sibling())
+
+    def push_right(d):
+        return remote(pown.at[d], zrecv.at[d], zs.at[d], zr.at[d], at.dp, at.t + 2)
+
+    def push_left(d):
+        slot = jnp.where(d == at.z - 1, nz, d)
+        return remote(pown.at[d], zrecv.at[slot], zs.at[d], zr.at[slot], at.dp, at.t - 2)
+
+    def came(slot):
+        remote(pown.at[0], zrecv.at[slot], zs.at[0], zr.at[slot], at.dp, at.sibling()).wait_recv()
+
+    is_end = (at.z == 0) | (at.z == nz - 1)
+
+    def tile(tt, put):
+        r = rows(tt)
+        x = xall[r, :]
+        gate = dot_nn(x, wgu[0])
+        up = dot_nn(x, wgu[1])
+        dmid = dot_nt(dyv[r, dcols(0)], wd[0])
+        for o in range(1, nd):
+            dmid = dmid + dot_nt(dyv[r, pl.ds(o * Dd, Dd)], wd[o])
+        sig = 1.0 / (1.0 + jnp.exp(-gate))
+        silu = gate * sig
+        mid[r, :] = (silu * up).astype(LOW)
+        du[r, :] = (dmid * silu).astype(LOW)
+        dg[r, :] = (dmid * up * (sig * (1.0 + gate * (1.0 - sig)))).astype(LOW)
+        put((dot_nt(dg[r, :], wgu[0]) + dot_nt(du[r, :], wgu[1])).astype(LOW))
+
+    def chain(k):
+        d = far_first(k, at.z, nz)
+        swap(d, 0).wait_recv()
+
+        @pl.when(is_end)
+        def _():
+            pown[d] = (pown[d].astype(F32) + precv[d].astype(F32)).astype(LOW)
+
+        @pl.when(jnp.logical_not(is_end))
+        def _():
+            came(d)
+            pown[d] = (pown[d].astype(F32) + precv[d].astype(F32) + zrecv[d].astype(F32)).astype(LOW)
+
+        pl.when(d > at.z)(lambda: push_right(d).start())
+        pl.when(d < at.z)(lambda: push_left(d).start())
+
+    def half(i, _):
+        k, own = i // 2, lax.rem(i, 2)
+        d = far_first(k, at.z, nz)
+        slot = lax.rem(k, 2)
+        pl.when((own == 0) & (k >= 2))(lambda: swap(d, slot).wait_send())
+
+        def put(v):
+            @pl.when(own == 0)
+            def _():
+                psend[slot] = v
+                swap(d, slot).start()
+
+            @pl.when(own == 1)
+            def _():
+                pown[d] = v
+
+        tile(2 * d + jnp.where(own == 0, 1 - at.c, at.c), put)
+        late = jnp.where(is_end, k, k - 2)
+        pl.when((own == 1) & (late >= 0) & (late < nz - 1))(lambda: chain(late))
+        return 0
+
+    lax.fori_loop(0, 2 * nz, half, 0)
+    for k in range(max(0, nz - 2), nz):
+        swap(0, k % 2).wait_send()
+
+    W = min(256, D)
+
+    def out_copy(slot, dst):
+        return pltpu.make_async_copy(stage.at[slot], dst, osem.at[slot])
+
+    def wtile(i, g):
+        slot = lax.rem(i, 2)
+        cols = pl.ds(pl.multiple_of(i * W, W), W)
+        pl.when(i >= 2)(lambda: out_copy(slot, dwgu_out.at[g, cols]).wait())
+        stage[slot] = dot_tn(xall[:, cols], (dg if g == 0 else du)[...]).astype(LOW)
+        out_copy(slot, dwgu_out.at[g, cols]).start()
+
+    def wgrad(g):
+        n = D // W
+        lax.fori_loop(0, n, lambda i, _: (wtile(i, g), 0)[1], 0)
+        for s in range(2):
+            out_copy(s, dwgu_out.at[g, pl.ds(0, W)]).wait()
+
+    def dwd_copy(o):
+        return pltpu.make_async_copy(wd.at[o], dwd_out.at[o], wsem.at[o])
+
+    def otile(i, _):
+        slot = lax.rem(i, 2)
+        r = rows(i)
+        pl.when(i >= 2)(lambda: pltpu.make_async_copy(psend.at[slot], out_out.at[r], osem.at[slot]).wait())
+
+        def part(o, _):
+            psend[slot, :, dcols(o)] = dot_nn(mid[r, :], wd[o]).astype(LOW)
+            return 0
+
+        lax.fori_loop(0, nd, part, 0)
+        pltpu.make_async_copy(psend.at[slot], out_out.at[r], osem.at[slot]).start()
+        return 0
+
+    wgrad(0)
+    if nz >= 2:
+        pl.when(jnp.logical_not(is_end))(lambda: chain(jnp.int32(nz - 2)))
+    wgrad(1)
+    lax.fori_loop(0, nt, otile, 0)
+    for s in range(2):
+        pltpu.make_async_copy(psend.at[s], out_out.at[rows(0)], osem.at[s]).wait()
+    for g in gathers:
+        g.drain()
+    def dtile(o, _):
+        wd[o] = dot_tn(mid[...], dyv[:, dcols(o)]).astype(LOW)
+        dwd_copy(o).start()
+        return 0
+
+    lax.fori_loop(0, nd, dtile, 0)
+    for o in range(nd):
+        dwd_copy(o).wait()
+
+    swap(at.z, 0).wait_recv()
+    dxn_out[...] = pown[at.z].astype(F32) + precv[at.z].astype(F32)
+
+    @pl.when(at.z > 0)
+    def _():
+        came(at.z)
+        dxn_out[...] = dxn_out[...] + zrecv[at.z].astype(F32)
+
+    @pl.when(at.z < nz - 1)
+    def _():
+        came(nz)
+        dxn_out[...] = dxn_out[...] + zrecv[nz].astype(F32)
+
+    for zz in range(nz):
+        @pl.when(zz != at.z)
+        def _(zz=zz):
+            remote(pown.at[zz], zrecv.at[zz], zs.at[zz], zr.at[zz], at.dp, at.sibling()).wait_send()
+    for zz in range(nz):
+        o = 2 * zz + at.c
+        across(o).wait_send()
+        pl.when((at.z < nz - 1) & (zz <= at.z))(lambda o=o: right(o).wait_send())
+        pl.when((at.z > 0) & (zz >= at.z))(lambda o=o: left(o).wait_send())
+
+
+def mlp(nd, nt, xn, dy_all, wgu, wd):
+    R, D = xn.shape
+    S = dy_all.shape[0]
+    Dd, F = wgu.shape[1:]
+    nz = nt // 2
+    ny = nd // 2
+    dma = lambda *s: pltpu.SemaphoreType.DMA(s)
+    hbm = pl.BlockSpec(memory_space=pltpu.HBM)
+    vm = pl.BlockSpec(memory_space=pltpu.VMEM)
+    return pl.pallas_call(
+        functools.partial(mlp_kernel, nd, nt),
+        out_shape=(
+            jax.ShapeDtypeStruct((R, D), F32),
+            jax.ShapeDtypeStruct((2, D, F), LOW),
+            jax.ShapeDtypeStruct((nd, F, Dd), LOW),
+            jax.ShapeDtypeStruct((S, D), LOW),
+        ),
+        in_specs=[hbm] * 4,
+        out_specs=(vm, hbm, hbm, hbm),
+        scratch_shapes=[
+            pltpu.VMEM((S, D), LOW), pltpu.VMEM((S, D), LOW), pltpu.VMEM((2, D, F), LOW), pltpu.VMEM((nd, F, Dd), LOW),
+            pltpu.VMEM((S, F), LOW), pltpu.VMEM((S, F), LOW), pltpu.VMEM((S, F), LOW),
+            pltpu.VMEM((2, R, D), LOW), pltpu.VMEM((nz, R, D), LOW), pltpu.VMEM((nz, R, D), LOW), pltpu.VMEM((nz + 1, R, D), LOW),
+            pltpu.VMEM((2, min(256, D), F), LOW),
+            dma(4), dma(4), dma(4, ny - 1), dma(4, ny - 1), dma(4, ny - 1), dma(4, nd),
+            dma(nt), dma(nt), dma(nt), dma(nt), dma(2), dma(nz), dma(nz), dma(nz + 1), dma(2), dma(nd),
+        ],
+        compiler_params=pltpu.CompilerParams(collective_id=1, has_side_effects=True, vmem_limit_bytes=63 << 20),
+        cost_estimate=pl.CostEstimate(flops=12 * S * D * F, bytes_accessed=40 << 20, transcendentals=S * F),
+        name="mlp",
+    )(xn, dy_all, wgu, wd)
 
 
 def rms_normed(field, gain_row):
@@ -107,12 +504,10 @@
 ):
     masters = (query_weight, keyvalue_weight, output_weight, gateup_weight, down_weight, norm_gains)
     lowered = tuple((weight.astype(jnp.bfloat16) for weight in masters))
-    full_query, full_kv, full_output, full_gateup, full_down, full_gains = (
+    full_query, full_kv, full_output, full_gains = (
         lax.all_gather(lowered[0], "dp", axis=0, tiled=True),
         lax.all_gather(lowered[1], "dp", axis=0, tiled=True),
         lax.all_gather(lowered[2], "dp", axis=1, tiled=True),
-        lax.all_gather(lowered[3], "dp", axis=1, tiled=True),
-        lax.all_gather(lowered[4], "dp", axis=1, tiled=True),
         lax.all_gather(lowered[5], "dp", axis=1, tiled=True),
     )
     gain_rows = full_gains.astype(jnp.float32)
@@ -171,31 +566,13 @@
         tiled=True,
     ).astype(jnp.float32)
     normed_two = rms_normed(hidden_one, gain_rows[1]).astype(jnp.bfloat16)
-    normed_mlp = lax.all_gather(normed_two, "tensor", axis=0, tiled=True)
-    gate = jnp.dot(normed_mlp, full_gateup[0], preferred_element_type=jnp.float32)
-    up_part = jnp.dot(normed_mlp, full_gateup[1], preferred_element_type=jnp.float32)
-    middle = (jax.nn.silu(gate) * up_part).astype(jnp.bfloat16)
+    grad_rows = lax.all_gather(cotangent, "tensor", axis=0, tiled=True)
+    nd, nt = lax.axis_size("dp"), lax.axis_size("tensor")
+    grad_normed_two, part_gateup, part_down, mlp_rows = mlp(
+        nd, nt, normed_two, grad_rows, lowered[3], lowered[4]
+    )
     mixed = hidden_one + lax.psum_scatter(
-        jnp.dot(middle, full_down, preferred_element_type=jnp.float32).astype(jnp.bfloat16),
-        "tensor",
-        scatter_dimension=0,
-        tiled=True,
-    ).astype(jnp.float32)
-    grad_rows = lax.all_gather(cotangent, "tensor", axis=0, tiled=True)
-    grad_down = inner_rows(middle, grad_rows)
-    grad_middle = outer_cols(grad_rows, full_down)
-    _, silu_pull = jax.vjp(lambda gate_in, up_in: jax.nn.silu(gate_in) * up_in, gate, up_part)
-    grad_gate_full, grad_up_full = silu_pull(grad_middle)
-    grad_gate = grad_gate_full.astype(jnp.bfloat16)
-    grad_up = grad_up_full.astype(jnp.bfloat16)
-    grad_gateup = jnp.stack([inner_rows(normed_mlp, grad_gate), inner_rows(normed_mlp, grad_up)])
-    grad_normed_two = lax.psum_scatter(
-        (outer_cols(grad_gate, full_gateup[0]) + outer_cols(grad_up, full_gateup[1])).astype(
-            jnp.bfloat16
-        ),
-        "tensor",
-        scatter_dimension=0,
-        tiled=True,
+        mlp_rows, "tensor", scatter_dimension=0, tiled=True
     ).astype(jnp.float32)
     _, second_pull = jax.vjp(rms_normed, hidden_one, gain_rows[1])
     grad_hidden_norm, gain_grad_two = second_pull(grad_normed_two)
@@ -277,25 +654,10 @@
     gains_shard = norm_gains.shape[1]
     grad_keyvalue = lax.dynamic_slice_in_dim(kv_total, dp_index * kv_shard, kv_shard, 0)
     grad_gains = lax.dynamic_slice_in_dim(gains_total, dp_index * gains_shard, gains_shard, 1)
-    local_grads = (grad_query, grad_output, grad_gateup, grad_down)
-    whole_query, whole_output, whole_gateup, whole_down = (
-        lax.psum(local_grads[0].astype(jnp.bfloat16), "dp").astype(jnp.float32),
-        lax.psum(local_grads[1].astype(jnp.bfloat16), "dp").astype(jnp.float32),
-        lax.psum(local_grads[2].astype(jnp.bfloat16), "dp").astype(jnp.float32),
-        lax.psum(local_grads[3].astype(jnp.bfloat16), "dp").astype(jnp.float32),
-    )
-    own_query = lax.dynamic_slice_in_dim(
-        whole_query, dp_index * query_weight.shape[0], query_weight.shape[0], 0
-    )
-    own_output = lax.dynamic_slice_in_dim(
-        whole_output, dp_index * output_weight.shape[1], output_weight.shape[1], 1
-    )
-    own_gateup = lax.dynamic_slice_in_dim(
-        whole_gateup, dp_index * gateup_weight.shape[1], gateup_weight.shape[1], 1
-    )
-    own_down = lax.dynamic_slice_in_dim(
-        whole_down, dp_index * down_weight.shape[1], down_weight.shape[1], 1
-    )
+    own_query = lax.psum_scatter(grad_query.astype(LOW), "dp", scatter_dimension=0, tiled=True).astype(F32)
+    own_output = lax.psum_scatter(grad_output.astype(LOW), "dp", scatter_dimension=1, tiled=True).astype(F32)
+    own_gateup = lax.psum_scatter(part_gateup, "dp", scatter_dimension=1, tiled=True).astype(F32)
+    own_down = lax.psum_scatter(part_down, "dp", scatter_dimension=0, tiled=False).astype(F32)
     split_squares = (
         jnp.sum(own_query * own_query)
         + jnp.sum(own_output * own_output)

time: 1550 us -> 1420 us (0.916)
  waiting for transfers between devices: 1030 us -> 784 us
  Pallas kernels: 0 us -> 174 us
  matrix products: 228 us -> 137 us
  local copies, waits for them, and re-layouts: 37.8 us -> 67.2 us
    psum x1 -> x0, waiting for transfers between devices: 215 us -> none  [local(): lax.psum(local_grads[0].astype(jnp.bfloat16), 'dp').astype(jnp.float32)]
    pallas_call x0 -> x1, Pallas kernels: none -> 174 us  [mlp(): pl.pallas_call(functools.partial(mlp_kernel, nd, nt), out_shape=(jax.Shap...]
    all_gather x3 -> x0, waiting for transfers between devices: 167 us -> none  [the longest x1 84.3 us: local(): normed_mlp = lax.all_gather(normed_two, 'tensor', axis=0, tiled=True)]
    dot_general x6 -> x3, matrix products: 58.7 us -> 15.9 us  [outer_cols(): lax.dot_general(left_side, right_side, (((1,), (1,)), ((), ())), preferre...]
    reduce_scatter x2 -> x4, waiting for transfers between devices: 88.3 us -> 129 us  [the longest x1 71.1 us: local(): lax.psum_scatter(part_gateup, 'dp', scatter_dimension=1, tiled=True)]
    all_gather x1, waiting for transfers between devices: 56.3 us -> 93.5 us  [local(): lax.all_gather(grad_hidden.astype(jnp.bfloat16), 'tensor', axis=0, tiled=...]
    psum x1, waiting for transfers between devices: 103 us -> 137 us  [local(): lax.psum((grad_keyvalue_part, jnp.stack([gain_grad_one, gain_grad_two])),...]
    dot_general x3 -> x0, matrix products: 31 us -> none  [the longest x1 12.1 us: local(): jnp.dot(normed_mlp, full_gateup[1], preferred_element_type=jnp.float32)]
  transfers between devices with their start and end apart: 17 -> 16, of which waited for: 15 -> 14; matrix products, arithmetic and copies ran while one was open for 14% -> 14% of each run, Pallas kernels for 0% -> 0%
where the time goes in v1:
time: 1420 us; the launch traced here: 1410 us
  waiting for transfers between devices  784 us (55%)
  Pallas kernels  174 us (12%)
  matrix products  137 us (10%)
  other arithmetic  115 us (8%)
  blocking collectives  92.2 us (6%)
  local copies, waits for them, and re-layouts  67.2 us (5%)
  between operations  20.9 us (1%)
  loops' own time  16.1 us (1%)
    pallas_call x1, Pallas kernels, mlp(): pl.pallas_call(functools.partial(mlp_kernel, nd, nt), out_shape=(jax.Shap...  174 us
    psum x1, waiting for transfers between devices, local(): lax.psum((grad_keyvalue_part, jnp.stack([gain_grad_one, gain_grad_two])),...  137 us
    all_gather x1, waiting for transfers between devices, local(): lax.all_gather(grad_hidden.astype(jnp.bfloat16), 'tensor', axis=0, tiled=...  93.5 us
    reduce_scatter x1, waiting for transfers between devices, local(): lax.psum_scatter(normed_part.astype(jnp.bfloat16), 'tensor', scatter_dime...  87.6 us
    all_gather x1, waiting for transfers between devices, local(): normed_all = lax.all_gather(normed_one, 'tensor', axis=0, tiled=True)  84.3 us
    reduce_scatter x1, waiting for transfers between devices, local(): lax.psum_scatter(jnp.dot(attn_rows, full_output, preferred_element_type=j...  84.1 us
    all_gather x1, waiting for transfers between devices, local(): grad_rows = lax.all_gather(cotangent, 'tensor', axis=0, tiled=True)  78.7 us
    reduce_scatter x1, waiting for transfers between devices, local(): lax.psum_scatter(part_gateup, 'dp', scatter_dimension=1, tiled=True)  71.1 us
  transfers between devices with their start and end apart: 16, of which 14 were waited for; matrix products, arithmetic and copies ran while one was open for 14% of the time, Pallas kernels for 0%

profile of v1, /device:TPU:0, one launch (start us, length us, event | category | flops | bytes accessed | tf_op | source)
XLA Modules:
  0.0 1407.2 jit_solution(10462542951568218628)
XLA Ops:
  9.9 9.5 all_gather.21
  25.1 14.7 %all-gather.11.cloned.1.call-done = bf16[2048,256]{1,0:T(8,128)(2,1)} async-done(((bf16[512,256]{1,0:T(8,128)(2,1)}), bf16[2048,256]{1,0:T(8,128)(2,1)}) %all-gather.11.cloned.1.call-update) | async-done | bytes 1048592 | tf_op jit(solution)/shard_map/all_gather | solution.py:509
  39.8 84.3 %all-gather.7.cloned.1.call-done = bf16[2048,2048]{1,0:T(8,128)(2,1)} async-done(((bf16[256,2048]{1,0:T(8,128)(2,1)}), bf16[2048,2048]{1,0:T(8,128)(2,1)}) %all-gather.7.cloned.1.call-update) | async-done | bytes 8388624 | tf_op jit(solution)/shard_map/all_gather | solution.py:527
  124.1 6.0 fusion.91
  141.6 10.1 all-gather.9.cloned.1.call-done
  151.7 7.3 fusion.90
  176.0 53.4 %while.27 = (s32[]{:T(128)}, bf16[4,2,512,128]{3,2,1,0:T(8,128)(2,1)}, f32[4,2,512,1]{2,1,3,0:T(2,128)S(1)}, s32[4]{0:T(128)S(1)}, s32[2048]{0:T(1024)S(1)}, /*i...) while((s32[]{:T(128)}, ...), condition=%wide.region_7.8_spmd, body=%wide.region_4.7_spmd.sunk | while | flops 1100086784 | bytes 30984376 | solution.py:560
  232.9 7.2 convolution_convert_fusion.1
  245.9 84.1 %reduce-scatter.12.cloned.1.call-done = bf16[256,2048]{1,0:T(8,128)(2,1)} async-done(((bf16[2048,2048]{1,0:T(8,128)(2,1)}), bf16[256,2048]{1,0:T(8,128)(2,1)}) %reduce-scatter.12.cloned.1.call-update) | async-done | bytes 1048592 | tf_op jit(solution)/shard_map/reduce_scatter | solution.py:562
  333.2 78.7 %all-gather.15.cloned.1.call-done.dy_in = bf16[2048,2048]{1,0:T(8,128)(2,1)} async-done(((bf16[256,2048]{1,0:T(8,128)(2,1)}), bf16[2048,2048]{1,0:T(8,128)(2,1)}) %all-gather.15.cloned.1.call-update) | async-done | bytes 8388624 | tf_op jit(solution)/shard_map/all_gather | solution.py:569
  411.9 174.2 %mlp.1 = (f32[256,2048]{1,0:T(8,128)}, bf16[2,2048,704]{2,1,0:T(8,128)(2,1)}, bf16[4,704,512]{2,1,0:T(8,128)(2,1)}, bf16[2048,2048]{1,0:T(8,128)(2,1)}) custom-call(bf16[256,2048]{1,0:T(8,128)(2,1)} %multiply_convert_fusion.1.xn_in, bf16[2048,2048]{1,0:T(8,128)(2,1)} %all-gather.15.cloned.1.call-done.dy_in, bf16[2,512,704]{2,1,0:T(8,128)(2,1)} %copy.205.wgu_in, ...), custom_call_target="tpu_custom_call" | custom-call | flops 35433480192 | bytes 41943040 | tf_op jit(solution)/shard_map/mlp/pallas_call | solution.py:394
  593.2 93.5 %all-gather.17.cloned.1.call-done = bf16[2048,2048]{1,0:T(8,128)(2,1)} async-done(((bf16[256,2048]{1,0:T(8,128)(2,1)}), bf16[2048,2048]{1,0:T(8,128)(2,1)}) %all-gather.17.cloned.1.call-update) | async-done | bytes 8388624 | tf_op jit(solution)/shard_map/all_gather | solution.py:580
  686.7 6.7 convolution_convert_fusion.4
  698.1 87.8 %while.28 = (s32[]{:T(128)}, f32[2048,128]{1,0:T(8,128)S(1)}, f32[2048,128]{1,0:T(8,128)}, f32[4,2,512,128]{3,2,0,1:T(8,128)}, s32[4]{0:T(128)S(1)}, /*index=5*/...) while((s32[]{:T(128)}, f32[2048,128]{1,0:T(8,128)S(1)}, ...), condition=%wide.region_14.15_spmd.clone, body=%wide.region_12.14_spmd.clone.sunk | while | flops 2720398848 | bytes 78690552 | solution.py:615
  725.9 4.9 fusion.140
  748.1 4.9 fusion.140
  791.3 25.3 %reduce-scatter.18.cloned.1.call-done = bf16[256,128]{0,1:T(8,128)(2,1)} async-done(((bf16[2048,128]{0,1:T(8,128)(2,1)}), bf16[256,128]{0,1:T(8,128)(2,1)}) %reduce-scatter.18.cloned.1.call-update) | async-done | bytes 65552 | tf_op jit(solution)/shard_map/reduce_scatter | solution.py:631
  816.5 32.1 %reduce-scatter.20.cloned.1.call-done = bf16[256,128]{0,1:T(8,128)(2,1)} async-done(((bf16[2048,128]{0,1:T(8,128)(2,1)}), bf16[256,128]{0,1:T(8,128)(2,1)}) %reduce-scatter.20.cloned.1.call-update) | async-done | bytes 65552 | tf_op jit(solution)/shard_map/reduce_scatter | solution.py:634
  856.6 6.9 convolution_convert_fusion.3
  864.8 7.1 convolution_convert_fusion.2
  871.9 5.7 convolution_convert_fusion
  885.6 5.8 reduce-scatter.28.cloned.1.call-done
  893.5 71.1 %reduce-scatter.26.cloned.1.call-done = bf16[2,512,704]{2,1,0:T(8,128)(2,1)} async-done(((bf16[2,2048,704]{2,1,0:T(8,128)(2,1)}), bf16[2,512,704]{2,1,0:T(8,128)(2,1)}) %reduce-scatter.26.cloned.1.call-update) | async-done | bytes 1441808 | tf_op jit(solution)/shard_map/reduce_scatter | solution.py:659
  967.4 136.8 %all-reduce.3.cloned.1.call-done = f32[2048,256]{1,0:T(8,128)} async-done(((f32[2048,256]{1,0:T(8,128)}), f32[2048,256]{1,0:T(8,128)}) %all-reduce.3.cloned.1.call-update) | async-done | bytes 2097168 | tf_op jit(solution)/shard_map/psum | solution.py:649
  1106.0 28.6 %reduce-scatter.22.cloned.1.call-done = bf16[512,256]{1,0:T(8,128)(2,1)} async-done(((bf16[2048,256]{1,0:T(8,128)(2,1)}), bf16[512,256]{1,0:T(8,128)(2,1)}) %reduce-scatter.22.cloned.1.call-update) | async-done | bytes 262160 | tf_op jit(solution)/shard_map/reduce_scatter | solution.py:657
  1136.3 29.4 %reduce-scatter.24.cloned.1.call-done = bf16[256,512]{1,0:T(8,128)(2,1)} async-done(((bf16[256,2048]{1,0:T(8,128)(2,1)}), bf16[256,512]{1,0:T(8,128)(2,1)}) %reduce-scatter.24.cloned.1.call-update) | async-done | bytes 262160 | tf_op jit(solution)/shard_map/reduce_scatter | solution.py:658
  1170.0 87.6 %reduce-scatter.16.cloned.1.call-done = bf16[256,2048]{1,0:T(8,128)(2,1)} async-done(((bf16[2048,2048]{1,0:T(8,128)(2,1)}), bf16[256,2048]{1,0:T(8,128)(2,1)}) %reduce-scatter.16.cloned.1.call-update) | async-done | bytes 1048592 | tf_op jit(solution)/shard_map/reduce_scatter | solution.py:628
  1261.1 39.6 %psum.22 = f32[2,2048]{1,0:T(2,128)S(1)} all-reduce(f32[2,2048]{1,0:T(2,128)S(1)} %pad_maximum_fusion.4), channel_id=1, replica_groups=mesh['dp'=4,'tensor'=8] {'dp','tensor'}, use_global_device_ids=true, to_apply=%region_31.32 | all-reduce | flops 4096 | bytes 32768 | tf_op jit(solution)/shard_map/psum | solution.py:649
  1306.2 43.0 %psum.23 = f32[]{:T(128)} all-reduce(f32[]{:T(128)S(6)} %add.234), channel_id=1, replica_groups=mesh['dp'=4,'tensor'=8] {'dp','tensor'}, use_global_device_ids=true, to_apply=%region_33.34 | all-reduce | flops 1 | bytes 8 | tf_op jit(solution)/shard_map/psum | solution.py:669
  1350.0 7.7 fusion.84
  1361.2 5.0 multiply_add_fusion
  1392.7 6.4 fusion.88
  (324 shorter events, 246.2 us)
Async XLA Ops:
  7.2 14.4 %copy-start = (bf16[256,2048]{1,0:T(8,128)(2,1)S(1)}, bf16[256,2048]{1,0:T(8,128)(2,1)}, u32[]{:S(2)}) copy-start(bf16[256,2048]{1,0:T(8,128)(2,1)} %param.26) | copy-start | bytes 3145732
  7.2 32.6 %all-gather.11.cloned.1.call-start = ((), (), s32[]{:S(2)}) async-start(), calls=%async_computation.11 | async-start | bytes 1310720 | tf_op jit(solution)/shard_map/all_gather | solution.py:509
  9.1 115.0 %all-gather.7.cloned.1.call-start = ((), (), s32[]{:S(2)}) async-start(), calls=%async_computation.9 | async-start | bytes 9437184 | tf_op jit(solution)/shard_map/all_gather | solution.py:527
  21.6 568.1 %copy-start.44 = (f32[1,2048]{1,0:T(1,128)}, f32[1,2048]{1,0:T(1,128)S(1)}, u32[]{:S(2)}) copy-start(f32[1,2048]{1,0:T(1,128)S(1)} %get-tuple-element.593) | copy-start | bytes 24580
  23.0 128.8 %all-gather.9.cloned.1.call-start = ((), (), s32[]{:S(2)}) async-start(), calls=%async_computation.10 | async-start | bytes 1310720 | tf_op jit(solution)/shard_map/all_gather | solution.py:508
  23.8 209.1 %all-gather.13.cloned.1.call-start = ((), (), s32[]{:S(2)}) async-start(), calls=%async_computation.12 | async-start | bytes 1310720 | tf_op jit(solution)/shard_map/all_gather | solution.py:510
  24.6 305.4 %reduce-scatter.12.cloned.1.call-start = ((), (), s32[]{:S(2)}) async-start(), calls=%async_computation.13 | async-start | bytes 9437184 | tf_op jit(solution)/shard_map/reduce_scatter | solution.py:562
  135.7 5.9 copy-start.21
  229.4 10.6 copy-start.6
  240.1 171.8 %all-gather.15.cloned.1.call-start = ((), (), s32[]{:S(2)}) async-start(), calls=%async_computation.14 | async-start | bytes 9437184 | tf_op jit(solution)/shard_map/all_gather | solution.py:569
  240.7 446.0 %all-gather.17.cloned.1.call-start = ((), (), s32[]{:S(2)}) async-start(), calls=%async_computation.16 | async-start | bytes 9437184 | tf_op jit(solution)/shard_map/all_gather | solution.py:580
  331.7 258.0 %copy-start.50 = (f32[256]{0:T(256)}, f32[256]{0:T(256)S(1)}, u32[]{:S(2)}) copy-start(f32[256]{0:T(256)S(1)} %fusion.76) | copy-start | bytes 3076
  589.8 96.9 %copy-start.37 = (bf16[256,2048]{1,0:T(8,128)(2,1)S(1)}, bf16[256,2048]{1,0:T(8,128)(2,1)}, u32[]{:S(2)}) copy-start(bf16[256,2048]{1,0:T(8,128)(2,1)} %all-gather.13.cloned.1.call-done) | copy-start | bytes 3145732
  593.1 223.4 %reduce-scatter.18.cloned.1.call-start = ((), (), s32[]{:S(2)}) async-start(), calls=%async_computation.18 | async-start | bytes 589824 | tf_op jit(solution)/shard_map/reduce_scatter | solution.py:631
  786.9 61.7 %reduce-scatter.20.cloned.1.call-start = ((), (), s32[]{:S(2)}) async-start(), calls=%async_computation.19 | async-start | bytes 589824 | tf_op jit(solution)/shard_map/reduce_scatter | solution.py:634
  789.2 102.2 %reduce-scatter.28.cloned.1.call-start = ((), (), s32[]{:S(2)}) async-start(), calls=%async_computation.24 | async-start | bytes 3604480
  789.8 174.9 %reduce-scatter.26.cloned.1.call-start = ((), (), s32[]{:S(2)}) async-start(), calls=%async_computation.22 | async-start | bytes 7864320 | tf_op jit(solution)/shard_map/reduce_scatter | solution.py:659
  790.5 59.9 %copy-start.11 = (bf16[256,2048]{1,0:T(8,128)(2,1)S(1)}, bf16[256,2048]{1,0:T(8,128)(2,1)}, u32[]{:S(2)}) copy-start(bf16[256,2048]{1,0:T(8,128)(2,1)} %fusion.52) | copy-start | bytes 3145732
  790.5 313.7 %all-reduce.3.cloned.1.call-start = ((), (), s32[]{:S(2)}) async-start(), calls=%async_computation.23 | async-start | bytes 4194304 | tf_op jit(solution)/shard_map/psum | solution.py:649
  852.2 282.4 %reduce-scatter.22.cloned.1.call-start = ((), (), s32[]{:S(2)}) async-start(), calls=%async_computation.20 | async-start | bytes 1310720 | tf_op jit(solution)/shard_map/reduce_scatter | solution.py:657
  863.5 8.4 copy-start.36
  863.5 302.1 %reduce-scatter.24.cloned.1.call-start = ((), (), s32[]{:S(2)}) async-start(), calls=%async_computation.21 | async-start | bytes 1310720 | tf_op jit(solution)/shard_map/reduce_scatter | solution.py:658
  871.9 385.7 %reduce-scatter.16.cloned.1.call-start = ((), (), s32[]{:S(2)}) async-start(), calls=%async_computation.17 | async-start | bytes 9437184 | tf_op jit(solution)/shard_map/reduce_scatter | solution.py:628
  877.6 514.5 %reduce-scatter.14.cloned.1.call-start = ((), (), s32[]{:S(2)}) async-start(), calls=%async_computation.15 | async-start | bytes 9437184 | tf_op jit(solution)/shard_map/reduce_scatter | solution.py:574
  885.6 372.0 %copy-start.2 = (bf16[256,2048]{1,0:T(8,128)(2,1)S(1)}, bf16[256,2048]{1,0:T(8,128)(2,1)}, u32[]{:S(2)}) copy-start(bf16[256,2048]{1,0:T(8,128)(2,1)} %param.26) | copy-start | bytes 3145732
  885.6 372.0 %copy-start.48 = (f32[1,2048]{1,0:T(1,128)S(1)}, f32[1,2048]{1,0:T(1,128)}, u32[]{:S(2)}) copy-start(f32[1,2048]{1,0:T(1,128)} %copy-done.47) | copy-start | bytes 24580
  885.6 372.0 %copy-start.57 = (f32[256]{0:T(256)S(1)}, f32[256]{0:T(256)}, u32[]{:S(2)}) copy-start(f32[256]{0:T(256)} %copy-done.56) | copy-start | bytes 3076
  885.6 372.0 %copy-start.62 = (bf16[2048,256]{1,0:T(8,128)(2,1)S(1)}, bf16[2048,256]{1,0:T(8,128)(2,1)}, u32[]{:S(2)}) copy-start(bf16[2048,256]{1,0:T(8,128)(2,1)} %all-gather.11.cloned.1.call-done) | copy-start | bytes 3145732
  1170.0 91.1 %copy-start.49 = (f32[2048]{0:T(1024)S(1)}, f32[2048]{0:T(1024)}, u32[]{:S(2)}) copy-start(f32[2048]{0:T(1024)} %get-tuple-element.503) | copy-start | bytes 24580
  1302.6 47.4 %copy-start.14 = (bf16[2,512,704]{2,1,0:T(8,128)(2,1)S(1)}, bf16[2,512,704]{2,1,0:T(8,128)(2,1)}, u32[]{:S(2)}) copy-start(bf16[2,512,704]{2,1,0:T(8,128)(2,1)} %reduce-scatter.26.cloned.1.call-done) | copy-start | bytes 4325380
  1374.7 4.9 copy-start.28
  1374.7 4.9 copy-start.30
  (51 other events, 134.1 us)
Sparse Core Ops, SparseCore 0:
  10.5 29.3 all-gather.10
  42.0 82.0 all-gather.6
  126.5 25.1 all-gather.8
  154.0 26.4 all-gather.12
  240.2 89.7 reduce-scatter.11
  331.4 80.3 all-gather.14
  593.2 93.3 all-gather.16
  787.0 29.4 reduce-scatter.17
  819.5 29.0 reduce-scatter.19
  851.5 39.8 reduce-scatter.27
  894.4 70.1 reduce-scatter.25
  970.4 133.7 all-reduce.2
  1107.9 26.6 reduce-scatter.21
  1137.9 27.7 reduce-scatter.23
  1167.9 89.5 reduce-scatter.15
  1259.8 90.0 reduce-scatter.13

commit v2 on v1

v2 whole, which is shorter than its diff:
```python
import functools
import math

import jax
import jax.numpy as jnp
from jax import lax
from jax.experimental import pallas as pl
from jax.experimental.pallas import tpu as pltpu
from jax.sharding import PartitionSpec as P

HD = 128
STEP = 10


EPSILON = 1e-05
MASKED = -1000000000.0
CLIP = 1.0
MOMENTUM = 0.9
LEARNING_RATES = (12.0, 12.0, 480.0, 48.0, 12.0, 960.0)
AVERAGE_TOP = 0.999
ROPE_BASE = 10000.0
MESH = pl.DeviceIdType.MESH
LOW = jnp.bfloat16
F32 = jnp.float32


def dot_nn(a, b):
    return jnp.dot(a, b, preferred_element_type=F32)


def dot_nt(a, b):
    return lax.dot_general(a, b, (((1,), (1,)), ((), ())), preferred_element_type=F32)


def dot_tn(a, b):
    return lax.dot_general(a, b, (((0,), (0,)), ((), ())), preferred_element_type=F32)


class Place:
    def __init__(self, nd, nt):
        self.nd, self.nt = nd, nt
        self.nx = 2 if nd % 2 == 0 else 1
        self.ny = nd // self.nx
        self.nz = nt // 2
        self.dp = lax.axis_index("dp")
        self.t = lax.axis_index("tensor")
        self.y = self.dp // self.nx
        self.x = lax.rem(self.dp, self.nx)
        self.z = self.t // 2
        self.c = lax.rem(self.t, 2)

    def x_peer(self):
        return self.y * self.nx + (1 - self.x)

    def y_peer(self, step):
        return lax.rem(self.y + step, self.ny) * self.nx + self.x

    def xy_peer(self, step):
        return lax.rem(self.y + step, self.ny) * self.nx + (1 - self.x)

    def sibling(self):
        return self.z * 2 + (1 - self.c)


def remote(src, dst, send, recv, dp, t):
    return pltpu.make_async_remote_copy(src, dst, send, recv, device_id=(dp, t), device_id_type=MESH)


def greet(at, dps=True, zs=True, core=True):
    bar = pltpu.get_barrier_semaphore()
    count = 0
    targets = []
    if dps:
        targets.append((at.x_peer(), at.t))
        targets += [(at.y_peer(s), at.t) for s in range(1, at.ny)]
    if core:
        targets.append((at.dp, at.sibling()))
    for target in targets:
        pl.semaphore_signal(bar, inc=1, device_id=target, device_id_type=MESH)
        count += 1
    if zs:
        @pl.when(at.z > 0)
        def _():
            pl.semaphore_signal(bar, inc=1, device_id=(at.dp, at.t - 2), device_id_type=MESH)

        @pl.when(at.z < at.nz - 1)
        def _():
            pl.semaphore_signal(bar, inc=1, device_id=(at.dp, at.t + 2), device_id_type=MESH)

        count = count + (at.z > 0).astype(jnp.int32) + (at.z < at.nz - 1).astype(jnp.int32)
    pl.semaphore_wait(bar, count)


def far_first(k, z, nz):
    j = nz - 1 - k
    m = jnp.minimum(z, nz - 1 - z)
    s = (j + 1) // 2
    two = jnp.where(lax.rem(j, 2) == 1, z - s, z + s)
    one = jnp.where(z < nz - 1 - z, j, nz - 1 - j)
    return jnp.where(j <= 2 * m, two, one)


class Gather:
    def __init__(self, at, src, dst, xs, ys, xf, yf, recv, kind):
        self.at, self.src, self.dst, self.kind = at, src, dst, kind
        self.xs, self.ys, self.xf, self.yf, self.recv = xs, ys, xf, yf, recv

    def own(self):
        at = self.at
        out = [remote(self.src, self.dst(at.dp), self.xs, self.recv.at[at.dp], at.x_peer(), at.t)]
        for s in range(1, at.ny):
            out.append(remote(self.src, self.dst(at.dp), self.ys.at[s - 1], self.recv.at[at.dp], at.y_peer(s), at.t))
        return out

    def passed(self):
        at = self.at
        out = []
        for s in range(1, at.ny):
            if self.kind == 0:
                o = at.x_peer()
                out.append(remote(self.dst(o), self.dst(o), self.yf.at[s - 1], self.recv.at[o], at.y_peer(s), at.t))
            else:
                o = at.y_peer(s)
                out.append(remote(self.dst(o), self.dst(o), self.xf.at[s - 1], self.recv.at[o], at.x_peer(), at.t))
        return out

    def arrived(self, o):
        remote(self.src, self.dst(o), self.xs, self.recv.at[o], self.at.x_peer(), self.at.t).wait_recv()

    def start(self):
        for cp in self.own():
            cp.start()

    def forward(self):
        at = self.at
        if self.kind == 0:
            self.arrived(at.x_peer())
        else:
            for s in range(1, at.ny):
                self.arrived(at.y_peer(s))
        for cp in self.passed():
            cp.start()

    def finish(self):
        at = self.at
        if self.kind == 0:
            for s in range(1, at.ny):
                self.arrived(at.y_peer(s))
        else:
            self.arrived(at.x_peer())
        for s in range(1, at.ny):
            self.arrived(at.xy_peer(s))

    def either(self, name):
        kind = self.kind
        for value in range(2):
            self.kind = value
            pl.when(kind == value)(getattr(self, name))
        self.kind = kind

    def finish_any(self):
        self.either("finish")

    def forward_any(self):
        self.either("forward")

    def drain_any(self):
        self.either("drain")

    def drain(self):
        for cp in self.own() + self.passed():
            cp.wait_send()


def mlp_kernel(nd, nt, xn_in, dy_in, wgu_in, wd_in,
               dxn_out, mine_g, land_g, mine_u, land_u, mine_d, land_d, mine_e, land_e, out_out,
               xall, dyv, wgu, wd, mid, dg, du, psend, pown, precv, zrecv,
               lsem, wx, wy, wxf, wyf, wr, ar, ac, asr, asl, ps, pr, zs, zr, osem, p1l, p1s, p1r):
    at = Place(nd, nt)
    nz = at.nz
    R, D = xn_in.shape
    Dd = wgu_in.shape[1]
    F = wgu_in.shape[2]
    Fh = F // 2
    rows = lambda t: pl.ds(pl.multiple_of(t * R, R), R)
    dcols = lambda o: pl.ds(pl.multiple_of(o * Dd, Dd), Dd)

    own_loads = [
        pltpu.make_async_copy(xn_in, xall.at[rows(at.t)], lsem.at[0]),
        pltpu.make_async_copy(dy_in, dyv, lsem.at[1]),
        pltpu.make_async_copy(wgu_in, wgu.at[:, dcols(at.dp)], lsem.at[2]),
        pltpu.make_async_copy(wd_in, wd.at[at.dp], lsem.at[3]),
    ]
    for cp in own_loads:
        cp.start()
    greet(at)

    gathers = []
    for p in range(2):
        gathers.append(Gather(at, wgu_in.at[p], lambda o, p=p: wgu.at[p, dcols(o)],
                              wx.at[p], wy.at[p], wxf.at[p], wyf.at[p], wr.at[p], p))
    for p in range(2):
        gathers.append(Gather(at, wd_in.at[pl.ds(p * Fh, Fh)], lambda o, p=p: wd.at[o, pl.ds(p * Fh, Fh)],
                              wx.at[2 + p], wy.at[2 + p], wxf.at[2 + p], wyf.at[2 + p], wr.at[2 + p], p))

    def right(o):
        return remote(xall.at[rows(o)], xall.at[rows(o)], asr.at[o], ar.at[o], at.dp, at.t + 2)

    def left(o):
        return remote(xall.at[rows(o)], xall.at[rows(o)], asl.at[o], ar.at[o], at.dp, at.t - 2)

    def across(o):
        return remote(xall.at[rows(o)], xall.at[rows(o)], ac.at[o], ar.at[o], at.dp, at.sibling())

    own_loads[0].wait()
    across(at.t).start()
    pl.when(at.z < nz - 1)(lambda: right(at.t).start())
    pl.when(at.z > 0)(lambda: left(at.t).start())
    for g in gathers[:2]:
        g.start()
    for g in gathers[2:]:
        g.start()

    def line_step(s):
        @pl.when(at.z - s >= 0)
        def _():
            o = at.t - 2 * s
            across(o).wait_recv()
            pl.when(at.z < nz - 1)(lambda: right(o).start())
            across(o).start()

        @pl.when(at.z + s < nz)
        def _():
            o = at.t + 2 * s
            across(o).wait_recv()
            pl.when(at.z > 0)(lambda: left(o).start())
            across(o).start()

    for g in gathers[:2]:
        g.forward()
    line_step(1)
    for g in gathers[2:]:
        g.forward()
    for s in range(2, nz):
        line_step(s)
    for cp in own_loads[1:]:
        cp.wait()
    for g in gathers:
        g.finish()
    for zz in range(nz):
        across(2 * zz + (1 - at.c)).wait_recv()

    def swap(d, slot):
        return remote(psend.at[slot], precv.at[d], ps.at[slot], pr.at[d], at.dp, at.sibling())

    def push_right(d):
        return remote(pown.at[d], zrecv.at[d], zs.at[d], zr.at[d], at.dp, at.t + 2)

    def push_left(d):
        slot = jnp.where(d == at.z - 1, nz, d)
        return remote(pown.at[d], zrecv.at[slot], zs.at[d], zr.at[slot], at.dp, at.t - 2)

    def came(slot):
        remote(pown.at[0], zrecv.at[slot], zs.at[0], zr.at[slot], at.dp, at.sibling()).wait_recv()

    is_end = (at.z == 0) | (at.z == nz - 1)

    def tile(tt, put):
        r = rows(tt)
        x = xall[r, :]
        gate = dot_nn(x, wgu[0])
        up = dot_nn(x, wgu[1])
        dmid = dot_nt(dyv[r, dcols(0)], wd[0])
        for o in range(1, nd):
            dmid = dmid + dot_nt(dyv[r, pl.ds(o * Dd, Dd)], wd[o])
        sig = 1.0 / (1.0 + jnp.exp(-gate))
        silu = gate * sig
        mid[r, :] = (silu * up).astype(LOW)
        du[r, :] = (dmid * silu).astype(LOW)
        dg[r, :] = (dmid * up * (sig * (1.0 + gate * (1.0 - sig)))).astype(LOW)
        put((dot_nt(dg[r, :], wgu[0]) + dot_nt(du[r, :], wgu[1])).astype(LOW))

    def chain(k):
        d = far_first(k, at.z, nz)
        swap(d, 0).wait_recv()

        @pl.when(is_end)
        def _():
            pown[d] = (pown[d].astype(F32) + precv[d].astype(F32)).astype(LOW)

        @pl.when(jnp.logical_not(is_end))
        def _():
            came(d)
            pown[d] = (pown[d].astype(F32) + precv[d].astype(F32) + zrecv[d].astype(F32)).astype(LOW)

        pl.when(d > at.z)(lambda: push_right(d).start())
        pl.when(d < at.z)(lambda: push_left(d).start())

    def half(i, _):
        k, own = i // 2, lax.rem(i, 2)
        d = far_first(k, at.z, nz)
        slot = lax.rem(k, 2)
        pl.when((own == 0) & (k >= 2))(lambda: swap(d, slot).wait_send())

        def put(v):
            @pl.when(own == 0)
            def _():
                psend[slot] = v
                swap(d, slot).start()

            @pl.when(own == 1)
            def _():
                pown[d] = v

        tile(2 * d + jnp.where(own == 0, 1 - at.c, at.c), put)
        late = jnp.where(is_end, k, k - 2)
        pl.when((own == 1) & (late >= 0) & (late < nz - 1))(lambda: chain(late))
        return 0

    lax.fori_loop(0, 2 * nz, half, 0)
    for k in range(max(0, nz - 2), nz):
        swap(0, k % 2).wait_send()

    for g in gathers:
        g.drain()
    for zz in range(nz):
        o = 2 * zz + at.c
        across(o).wait_send()
        pl.when((at.z < nz - 1) & (zz <= at.z))(lambda o=o: right(o).wait_send())
        pl.when((at.z > 0) & (zz >= at.z))(lambda o=o: left(o).wait_send())

    W = min(256, Dd)
    nx, ny = at.nx, at.ny

    def hop(n, src, o, mine, land):
        yy, xx = o // nx, lax.rem(o, nx)
        if n % 2 == 0:
            step = lax.rem(yy - at.y + ny, ny)
            slot = (step - 1) * nx + xx
            stays, place, peer = yy == at.y, xx, yy * nx + at.x
        else:
            slot, stays, place, peer = yy, xx == at.x, yy, at.y * nx + xx
        local = pltpu.make_async_copy(src, mine.at[place], p1l.at[n, place])
        slot = jnp.where(stays, 0, slot)
        away = remote(src, land.at[slot], p1s.at[n, slot], p1r.at[n, slot], jnp.where(stays, at.x_peer(), peer), at.t)
        return stays, local, away

    def order(n, i):
        if n % 2 == 0:
            return lax.rem(at.y + 1 + i // nx, ny) * nx + lax.rem(i, nx)
        return lax.rem(i, ny) * nx + jnp.where(i < ny, 1 - at.x, at.x)

    def send(n, src, o, mine, land):
        stays, local, away = hop(n, src, o, mine, land)
        pl.when(stays)(lambda: local.start())
        pl.when(jnp.logical_not(stays))(lambda: away.start())

    def settle(n, src, mine, land):
        for i in range(nd):
            stays, local, away = hop(n, src, order(n, i), mine, land)

            @pl.when(stays)
            def _():
                local.wait()

            @pl.when(jnp.logical_not(stays))
            def _():
                away.wait_send()
                away.wait_recv()

    def wgrad(n, mine, land):
        def block(i, _):
            o = order(n, i)

            def wtile(w, _):
                cols = pl.ds(pl.multiple_of(o * Dd + w * W, W), W)
                wgu[n, cols, :] = dot_tn(xall[:, cols], (du if n else dg)[...]).astype(LOW)
                return 0

            lax.fori_loop(0, Dd // W, wtile, 0)
            send(n, wgu.at[n, dcols(o)], o, mine, land)
            return 0

        lax.fori_loop(0, nd, block, 0)

    def dgrad(n, mine, land):
        half = pl.ds((n - 2) * Fh, Fh)

        def block(i, _):
            o = order(n, i)
            if n == 2:
                xall[pl.ds(0, F), dcols(o)] = dot_tn(mid[...], dyv[:, dcols(o)]).astype(LOW)
            send(n, xall.at[half, dcols(o)], o, mine, land)
            return 0

        lax.fori_loop(0, nd, block, 0)

    def otile(i, _):
        slot = lax.rem(i, 2)
        r = rows(i)
        pl.when(i >= 2)(lambda: pltpu.make_async_copy(psend.at[slot], out_out.at[r], osem.at[slot]).wait())

        def part(o, _):
            psend[slot, :, dcols(o)] = dot_nn(mid[r, :], wd[o]).astype(LOW)
            return 0

        lax.fori_loop(0, nd, part, 0)
        pltpu.make_async_copy(psend.at[slot], out_out.at[r], osem.at[slot]).start()
        return 0

    wgrad(0, mine_g, land_g)
    if nz >= 2:
        pl.when(jnp.logical_not(is_end))(lambda: chain(jnp.int32(nz - 2)))
    wgrad(1, mine_u, land_u)
    dgrad(2, mine_d, land_d)
    dgrad(3, mine_e, land_e)
    lax.fori_loop(0, nt, otile, 0)
    for s in range(2):
        pltpu.make_async_copy(psend.at[s], out_out.at[rows(0)], osem.at[s]).wait()

    swap(at.z, 0).wait_recv()
    dxn_out[...] = pown[at.z].astype(F32) + precv[at.z].astype(F32)

    @pl.when(at.z > 0)
    def _():
        came(at.z)
        dxn_out[...] = dxn_out[...] + zrecv[at.z].astype(F32)

    @pl.when(at.z < nz - 1)
    def _():
        came(nz)
        dxn_out[...] = dxn_out[...] + zrecv[nz].astype(F32)

    for zz in range(nz):
        @pl.when(zz != at.z)
        def _(zz=zz):
            remote(pown.at[zz], zrecv.at[zz], zs.at[zz], zr.at[zz], at.dp, at.sibling()).wait_send()
    settle(0, wgu.at[0, dcols(0)], mine_g, land_g)
    settle(1, wgu.at[1, dcols(0)], mine_u, land_u)
    settle(2, xall.at[pl.ds(0, Fh), dcols(0)], mine_d, land_d)
    settle(3, xall.at[pl.ds(0, Fh), dcols(0)], mine_e, land_e)


def mlp(nd, nt, xn, dy_all, wgu, wd):
    R, D = xn.shape
    S = dy_all.shape[0]
    Dd, F = wgu.shape[1:]
    nz = nt // 2
    ny = nd // 2
    dma = lambda *s: pltpu.SemaphoreType.DMA(s)
    shape = lambda *s: jax.ShapeDtypeStruct(s, LOW)
    Fh = F // 2
    slots = max(2 * (ny - 1), ny)
    hbm = pl.BlockSpec(memory_space=pltpu.HBM)
    vm = pl.BlockSpec(memory_space=pltpu.VMEM)
    return pl.pallas_call(
        functools.partial(mlp_kernel, nd, nt),
        out_shape=(
            jax.ShapeDtypeStruct((R, D), F32),
            shape(2, Dd, F), shape(2 * (ny - 1), Dd, F), shape(ny, Dd, F), shape(ny, Dd, F),
            shape(2, Fh, Dd), shape(2 * (ny - 1), Fh, Dd), shape(ny, Fh, Dd), shape(ny, Fh, Dd),
            shape(S, D),
        ),
        in_specs=[hbm] * 4,
        out_specs=(vm,) + (hbm,) * 9,
        scratch_shapes=[
            pltpu.VMEM((S, D), LOW), pltpu.VMEM((S, D), LOW), pltpu.VMEM((2, D, F), LOW), pltpu.VMEM((nd, F, Dd), LOW),
            pltpu.VMEM((S, F), LOW), pltpu.VMEM((S, F), LOW), pltpu.VMEM((S, F), LOW),
            pltpu.VMEM((2, R, D), LOW), pltpu.VMEM((nz, R, D), LOW), pltpu.VMEM((nz, R, D), LOW), pltpu.VMEM((nz + 1, R, D), LOW),
            dma(4), dma(4), dma(4, ny - 1), dma(4, ny - 1), dma(4, ny - 1), dma(4, nd),
            dma(nt), dma(nt), dma(nt), dma(nt), dma(2), dma(nz), dma(nz), dma(nz + 1), dma(2), dma(4, max(2, ny)), dma(4, slots), dma(4, slots),
        ],
        compiler_params=pltpu.CompilerParams(collective_id=1, has_side_effects=True, vmem_limit_bytes=63 << 20),
        cost_estimate=pl.CostEstimate(flops=12 * S * D * F, bytes_accessed=40 << 20, transcendentals=S * F),
        name="mlp",
    )(xn, dy_all, wgu, wd)


def swap_halves(u):
    h = u.shape[-1] // 2
    return jnp.concatenate([u[:, h:], u[:, :h]], axis=1)


def near_first(k, z, nz):
    return far_first(nz - 1 - k, z, nz)


def greet_all(at):
    bar = pltpu.get_barrier_semaphore()
    for s in range(1, at.nd):
        pl.semaphore_signal(bar, inc=1, device_id=(lax.rem(at.dp + s, at.nd), at.t), device_id_type=MESH)
    for s in range(1, at.nt):
        pl.semaphore_signal(bar, inc=1, device_id=(at.dp, lax.rem(at.t + s, at.nt)), device_id_type=MESH)
    pl.semaphore_wait(bar, at.nd - 1 + at.nt - 1)


class Line:
    def __init__(self, at, view, right, left, recv, across=None):
        self.at, self.view, self.rs, self.ls, self.recv, self.across = at, view, right, left, recv, across

    def right(self, o):
        return remote(self.view(o), self.view(o), self.rs.at[o], self.recv.at[o], self.at.dp, self.at.t + 2)

    def left(self, o):
        return remote(self.view(o), self.view(o), self.ls.at[o], self.recv.at[o], self.at.dp, self.at.t - 2)

    def pass_on(self, o, to_right, to_left):
        at = self.at
        if to_right:
            pl.when(at.z < at.nz - 1)(lambda: self.right(o).start())
        if to_left:
            pl.when(at.z > 0)(lambda: self.left(o).start())
        if self.across is not None:
            self.across(o).start()

    def start(self):
        self.pass_on(self.at.z, True, True)

    def arrived(self, o):
        remote(self.view(o), self.view(o), self.rs.at[o], self.recv.at[o], self.at.dp, self.at.sibling()).wait_recv()

    def step(self, s):
        at = self.at

        @pl.when(at.z - s >= 0)
        def _():
            self.arrived(at.z - s)
            self.pass_on(at.z - s, True, False)

        @pl.when(at.z + s < at.nz)
        def _():
            self.arrived(at.z + s)
            self.pass_on(at.z + s, False, True)

    def drain(self):
        at = self.at
        for o in range(at.nz):
            pl.when((at.z < at.nz - 1) & (o <= at.z))(lambda o=o: self.right(o).wait_send())
            pl.when((at.z > 0) & (o >= at.z))(lambda o=o: self.left(o).wait_send())
            if self.across is not None:
                self.across(o).wait_send()


def attend_kernel(nd, nt, tok, gain, wq_in, wkv_in, wo_in, cosf, sins, lo_in,
                  h1_out, xn2_out, gfull, lse_out,
                  xn1_out, wq_out, wo_out, wkv_out, kv_out, q_out, o_out,
                  xn1, wq, wo, wkv, kvs, qs, os_, pback, precv,
                  lsem, gs, gr, vx, vy, vxf, vyf, vr, qx, qy, qxf, qyf, qr, ox, oy, oxf, oyf, orr,
                  qlr, qll, qlv, olr, oll, olv, klr, kll, klv, klc, klcr, cs, cr, outs):
    at = Place(nd, nt)
    nz = at.nz
    R, D = tok.shape
    Dd, HC = wq_in.shape
    TQ = min(256, 2 * R)
    rows = lambda t: pl.ds(pl.multiple_of(t * R, R), R)
    drows = lambda o: pl.ds(pl.multiple_of(o * Dd, Dd), Dd)
    hcols = lambda j: pl.ds(pl.multiple_of(j * HC, HC), HC)

    loads = [
        pltpu.make_async_copy(wkv_in, wkv.at[drows(at.dp)], lsem.at[0]),
        pltpu.make_async_copy(wq_in, wq.at[at.z, drows(at.dp)], lsem.at[1]),
        pltpu.make_async_copy(wo_in, wo.at[at.dp, hcols(at.z)], lsem.at[2]),
    ]
    for cp in loads:
        cp.start()
    gfull[at.dp] = gain[...]
    greet_all(at)

    def gain_copy(s):
        return remote(gain, gfull.at[at.dp], gs.at[s - 1], gr.at[s - 1], lax.rem(at.dp + s, nd), at.t)

    for s in range(1, nd):
        gain_copy(s).start()
    Dh = Dd // 2
    gkv = [Gather(at, wkv_in.at[pl.ds(p * Dh, Dh)], lambda o, p=p: wkv.at[pl.ds(pl.multiple_of(o * Dd + p * Dh, Dh), Dh)],
                  vx.at[p], vy.at[p], vxf.at[p], vyf.at[p], vr.at[p], p) for p in range(2)]

    def gq(k):
        j = near_first(k, at.z, nz)
        return Gather(at, wq.at[j, drows(at.dp)], lambda o: wq.at[j, drows(o)], qx.at[k], qy.at[k], qxf.at[k], qyf.at[k], qr.at[k], lax.rem(k, 2) if not isinstance(k, int) else k % 2)

    def go(k):
        j = near_first(k, at.z, nz)
        return Gather(at, wo.at[at.dp, hcols(j)], lambda o: wo.at[o, hcols(j)], ox.at[k], oy.at[k], oxf.at[k], oyf.at[k], orr.at[k], lax.rem(k, 2) if not isinstance(k, int) else k % 2)

    lq = Line(at, lambda o: wq.at[o, drows(at.dp)], qlr, qll, qlv)
    lo = Line(at, lambda o: wo.at[at.dp, hcols(o)], olr, oll, olv)

    def kv_view(o):
        return kvs.at[rows(2 * o + at.c)]

    def kv_across(o):
        return remote(kv_view(o), kv_view(o), klc.at[o], klcr.at[o], at.dp, at.sibling())

    lkv = Line(at, kv_view, klr, kll, klv, kv_across)

    for g in gkv:
        g.start()
    loads[1].wait()
    lq.start()
    gq(0).start()

    for s in range(1, nd):
        gain_copy(s).wait_recv()

    def scaled(v, row, write):
        r = lax.rsqrt(jnp.mean(v * v, axis=-1, keepdims=True) + EPSILON)
        for o in range(nd):
            cols = pl.ds(o * Dd, Dd)
            write(cols, (v[:, o * Dd:(o + 1) * Dd] * r * gfull[o, row:row + 1, :]).astype(LOW))

    mine = rows(at.c)

    def put_xn1(cols, v):
        xn1[mine, cols] = v

    scaled(tok[...].astype(F32), 0, put_xn1)
    xn1_across = remote(xn1.at[mine], xn1.at[mine], cs.at[0], cr.at[0], at.dp, at.sibling())
    xn1_across.start()

    for g in gkv:
        g.forward()
    loads[0].wait()
    for g in gkv:
        g.finish()
    kvpre = dot_nn(xn1[mine, :], wkv[...])
    kk = kvpre[:, :HD]
    kvs[rows(at.t), pl.ds(0, HD)] = (kk * cosf[mine, :] + swap_halves(kk) * sins[mine, :]).astype(LOW)
    kvs[rows(at.t), pl.ds(HD, HD)] = kvpre[:, HD:].astype(LOW)
    lkv.start()
    loads[2].wait()
    lo.start()
    for s in range(1, nz):
        lq.step(s)
        gq(s).start()
        gq(s - 1).forward()
        lkv.step(s)
    gq(nz - 1).forward()
    xn1_across.wait_recv()
    go(0).start()
    for s in range(1, nz):
        lo.step(s)
        go(s).start()
    for o in range(nz):
        kv_across(o).wait_recv()

    scale = 1.0 / math.sqrt(HD)
    S = kvs.shape[0]
    lane = lax.broadcasted_iota(jnp.int32, (TQ, 128), 1)

    def pair(k, _):
        j = near_first(k, at.z, nz)
        g = gq(k)
        g.finish_any()
        qpre = dot_nn(xn1[...], wq[j])
        for hh in range(HC // HD):
            u = qpre[:, hh * HD:(hh + 1) * HD]
            qs[:, pl.ds(pl.multiple_of(j * HC + hh * HD, HD), HD)] = (u * cosf[...] + swap_halves(u) * sins[...]).astype(LOW)

        def head(i, _):
            hh, tq = lax.rem(i, HC // HD), i // (HC // HD)
            rr = pl.ds(pl.multiple_of(tq * TQ, TQ), TQ)
            cols = pl.ds(pl.multiple_of(j * HC + hh * HD, HD), HD)
            s = dot_nt(qs[rr, cols], kvs[:, pl.ds(0, HD)])
            place = lax.broadcasted_iota(jnp.int32, (TQ, S), 1)
            here = at.z * 2 * R + tq * TQ + lax.broadcasted_iota(jnp.int32, (TQ, 1), 0)
            s = jnp.where((place >= lo_in[rr, :]) & (place <= here), s * scale, MASKED)
            m = jnp.max(s, axis=-1, keepdims=True)
            p = jnp.exp(s - m)
            total = jnp.sum(p, axis=-1, keepdims=True)
            att = dot_nn(p.astype(LOW), kvs[:, pl.ds(HD, HD)])
            os_[rr, cols] = (att / total).astype(LOW)
            hid = j * (HC // HD) + hh
            lse_out[rr, :] = jnp.where(lane == hid, m + jnp.log(total), lse_out[rr, :])
            return 0

        lax.fori_loop(0, (HC // HD) * (2 * R // TQ), head, 0)
        go(k).forward_any()
        return 0

    lse_out[...] = jnp.zeros_like(lse_out)
    lax.fori_loop(0, nz, pair, 0)
    keep = [
        pltpu.make_async_copy(xn1, xn1_out, outs.at[0]),
        pltpu.make_async_copy(wq, wq_out, outs.at[1]),
        pltpu.make_async_copy(wkv, wkv_out, outs.at[2]),
        pltpu.make_async_copy(kvs, kv_out, outs.at[3]),
        pltpu.make_async_copy(qs, q_out, outs.at[4]),
        pltpu.make_async_copy(os_, o_out, outs.at[5]),
    ]
    for cp in keep:
        cp.start()

    lax.fori_loop(0, nz, lambda k, _: (go(k).finish_any(), 0)[1], 0)
    keep.append(pltpu.make_async_copy(wo, wo_out, outs.at[6]))
    keep[-1].start()
    theirs = rows(1 - at.c)
    for o in range(nd):
        pback[:, pl.ds(o * Dd, Dd)] = dot_nn(os_[theirs, :], wo[o]).astype(LOW)
    back = remote(pback, precv, cs.at[1], cr.at[1], at.dp, at.sibling())
    back.start()
    for o in range(nd):
        cols = pl.ds(o * Dd, Dd)
        h1_out[:, cols] = tok[:, cols].astype(F32) + dot_nn(os_[mine, :], wo[o])
    back.wait_recv()
    h1_out[...] = h1_out[...] + precv[...].astype(F32)

    def put_xn2(cols, v):
        xn2_out[:, cols] = v

    scaled(h1_out[...], 1, put_xn2)

    for s in range(1, nd):
        gain_copy(s).wait_send()
    for g in gkv:
        g.drain()
    xn1_across.wait_send()
    back.wait_send()
    lq.drain()
    lo.drain()
    lkv.drain()

    def drain(k, _):
        gq(k).drain_any()
        go(k).drain_any()
        return 0

    lax.fori_loop(0, nz, drain, 0)
    for cp in keep:
        cp.wait()


def attend(nd, nt, tok, gain, wq, wkv, wo, cosf, sins, lo):
    R, D = tok.shape
    Dd, HC = wq.shape
    S = R * nt
    nz, ny = nt // 2, nd // 2
    dma = lambda *s: pltpu.SemaphoreType.DMA(s)
    hbm = pl.BlockSpec(memory_space=pltpu.HBM)
    vm = pl.BlockSpec(memory_space=pltpu.VMEM)
    shapes = [((R, D), F32), ((R, D), LOW), ((nd, 8, Dd), F32), ((2 * R, 128), F32),
              ((2 * R, D), LOW), ((nz, D, HC), LOW), ((nd, nz * HC, Dd), LOW), ((D, 2 * HD), LOW), ((S, 2 * HD), LOW),
              ((2 * R, nz * HC), LOW), ((2 * R, nz * HC), LOW)]
    yg = lambda n: [dma(n), dma(n, ny - 1), dma(n, ny - 1), dma(n, ny - 1), dma(n, nd)]
    return pl.pallas_call(
        functools.partial(attend_kernel, nd, nt),
        out_shape=tuple(jax.ShapeDtypeStruct(*s) for s in shapes),
        in_specs=[vm, vm, hbm, hbm, hbm, vm, vm, vm],
        out_specs=(vm, vm, vm, vm) + (hbm,) * 7,
        scratch_shapes=[pltpu.VMEM(*s) for s in shapes[4:]] + [pltpu.VMEM((R, D), LOW), pltpu.VMEM((R, D), LOW)]
        + [dma(3), dma(nd - 1), dma(nd - 1)] + yg(2) + yg(nz) + yg(nz)
        + [dma(nz)] * 3 + [dma(nz)] * 3 + [dma(nz)] * 5 + [dma(2), dma(2), dma(7)],
        compiler_params=pltpu.CompilerParams(collective_id=2, has_side_effects=True, vmem_limit_bytes=63 << 20),
        cost_estimate=pl.CostEstimate(flops=20 << 30, bytes_accessed=40 << 20, transcendentals=8 * 512 * 2048),
        name="attend",
    )(tok, gain, wq, wkv, wo, cosf, sins, lo)


class Scatter:
    def __init__(self, at, kind, view, land, land2, ss, rs, ss2, rs2):
        self.at, self.kind, self.view = at, kind, view
        self.land, self.land2 = land, land2
        self.ss, self.rs, self.ss2, self.rs2 = ss, rs, ss2, rs2

    def first(self):
        at = self.at
        out = []
        if self.kind == 0:
            for s in range(1, at.ny):
                for xx in range(at.nx):
                    slot = (s - 1) * at.nx + xx
                    o = lax.rem(at.y + s, at.ny) * at.nx + xx
                    out.append(remote(self.view(o), self.land(slot), self.ss.at[slot], self.rs.at[slot], at.y_peer(s), at.t))
        else:
            for yy in range(at.ny):
                o = yy * at.nx + 1 - at.x
                out.append(remote(self.view(o), self.land(yy), self.ss.at[yy], self.rs.at[yy], at.x_peer(), at.t))
        return out

    def second(self):
        at = self.at
        if self.kind == 0:
            return [remote(self.view(at.x_peer()), self.land2(0), self.ss2.at[0], self.rs2.at[0], at.x_peer(), at.t)]
        return [remote(self.view(at.y_peer(s)), self.land2(s - 1), self.ss2.at[s - 1], self.rs2.at[s - 1], at.y_peer(s), at.t)
                for s in range(1, at.ny)]

    def start(self):
        for cp in self.first():
            cp.start()

    def add(self, o, slots):
        total = self.view(o)[...].astype(F32)
        for slot in slots:
            total = total + self.land(slot)[...].astype(F32)
        self.view(o)[...] = total.astype(LOW)

    def middle(self):
        at = self.at
        for cp in self.first():
            cp.wait_recv()
        if self.kind == 0:
            self.add(at.x_peer(), [(s - 1) * at.nx + 1 - at.x for s in range(1, at.ny)])
        else:
            for s in range(1, at.ny):
                self.add(at.y_peer(s), [lax.rem(at.y + s, at.ny)])
        for cp in self.second():
            cp.start()
        if self.kind == 0:
            self.add(at.dp, [(s - 1) * at.nx + at.x for s in range(1, at.ny)])
        else:
            self.add(at.dp, [at.y])

    def total(self):
        total = self.view(self.at.dp)[...].astype(F32)
        for i, cp in enumerate(self.second()):
            cp.wait_recv()
            total = total + self.land2(i)[...].astype(F32)
        return total

    def drain(self):
        for cp in self.first() + self.second():
            cp.wait_send()

    def either(self, name, put=None):
        kind = self.kind
        for value in range(2):
            self.kind = value
            call = getattr(self, name)
            if put is None:
                pl.when(kind == value)(call)
            else:
                pl.when(kind == value)(lambda call=call: put(call()))
        self.kind = kind


def grads_kernel(nd, nt, dy, tok, gfull, cosf, sins, lo_row, lse, later,
                 h1_in, dxn2_in, xn1_in, wq_in, wo_in, wkv_in, kv_in, q_in, o_in,
                 mine_g, land_g, mine_u, land_u, mine_d, land_d, mine_e, land_e,
                 tgrad, gq_out, go_out, gkv_out, gg_out, norm_out, keep_g, keep_u, keep_d, keep_e, got_g, got_u, got_d, got_e,
                 xn1, wq, wo, wkv, kvs, qs, os_, dos, dh1b, dxn1, lset, dkv, dq,
                 bg, bu, bd, be, lg, lu, ld, le, tg, tu, td, te,
                 ql, ql2, ol, ol2, qz, oz, qlz, olz, kvb, kland, kz, xrecv, wl, wd2, w2, w2l, wfin, gl, gpart, u2, u2l, gfin, share, norms, normd,
                 lsem, xsem, fs, fr, qss, qsr, qss2, qsr2, oss, osr, oss2, osr2, qzs, qzr, ozs, ozr,
                 ks, kr, kzs, kzr, ws, wr, w2s, w2r, w3s, w3r, us, ur, u2s, u2r, u3s, u3r, ns, nr, n2s, n2r, outs):
    at = Place(nd, nt)
    nz, nx, ny = at.nz, at.nx, at.ny
    R, D = tok.shape
    Dd = wo.shape[2]
    HC = wq.shape[2]
    Ds = wl.shape[1]
    NH = HC // HD
    KT = 2 * R
    S = kvs.shape[0]
    rows = lambda t: pl.ds(pl.multiple_of(t * R, R), R)
    drows = lambda o: pl.ds(pl.multiple_of(o * Dd, Dd), Dd)
    hcols = lambda j: pl.ds(pl.multiple_of(j * HC, HC), HC)
    mine, theirs = rows(at.c), rows(1 - at.c)
    scale = 1.0 / math.sqrt(HD)

    pieces = [(bg, mine_g), (bu, mine_u), (bd, mine_d), (be, mine_e), (tg, land_g), (tu, land_u), (td, land_d), (te, land_e),
              (wo, wo_in), (os_, o_in), (qs, q_in), (kvs, kv_in), (xn1, xn1_in), (wq, wq_in), (wkv, wkv_in),
              (dxn1.at[pl.ds(0, R)], h1_in), (dxn1.at[pl.ds(R, R)], dxn2_in)]
    loads = [pltpu.make_async_copy(src, dst, lsem.at[i]) for i, (dst, src) in enumerate(pieces)]
    for cp in loads:
        cp.start()
    greet_all(at)

    def rms_back(v_of, e_of, row, put):
        chunks = [pl.ds(o * Dd, Dd) for o in range(nd)]
        squares = jnp.zeros((R, 1), F32)
        inner = jnp.zeros((R, 1), F32)
        for o, cols in enumerate(chunks):
            v = v_of(cols)
            squares = squares + jnp.sum(v * v, axis=-1, keepdims=True)
            inner = inner + jnp.sum(e_of(cols) * gfull[o, row:row + 1, :] * v, axis=-1, keepdims=True)
        r = lax.rsqrt(squares / D + EPSILON)
        inner = inner * (r * r * r) / D
        for o, cols in enumerate(chunks):
            v, e = v_of(cols), e_of(cols)
            gpart[row:row + 1, cols] = jnp.sum(e * v * r, axis=0, keepdims=True)
            put(cols, r * (e * gfull[o, row:row + 1, :]) - v * inner)

    gpart[...] = jnp.zeros_like(gpart)

    def put_dh1(cols, v):
        total = dy[:, cols].astype(F32) + v
        tgrad[:, cols] = total
        dh1b[mine, cols] = total.astype(LOW)

    loads[15].wait()
    loads[16].wait()
    rms_back(lambda cols: dxn1[pl.ds(0, R), cols], lambda cols: dxn1[pl.ds(R, R), cols], 1, put_dh1)
    swap_dh1 = remote(dh1b.at[mine], dh1b.at[mine], xsem.at[0], xsem.at[1], at.dp, at.sibling())
    swap_dh1.start()

    big = []
    for n, (buf, got, second) in enumerate([(bg, tg, lg), (bu, tu, lu), (bd, td, ld), (be, te, le)]):
        loads[n].wait()
        loads[4 + n].wait()
        if n % 2 == 0:
            keep, keep_slots = at.x, [(s - 1) * nx + at.x for s in range(1, ny)]
            away = [(1 - at.x, [(s - 1) * nx + 1 - at.x for s in range(1, ny)], at.x_peer())]
        else:
            keep, keep_slots = at.y, [at.y]
            away = [(lax.rem(at.y + s, ny), [lax.rem(at.y + s, ny)], at.y_peer(s)) for s in range(1, ny)]
        copies = []
        for i, (place, slots, peer) in enumerate(away):
            total = buf[place].astype(F32)
            for slot in slots:
                total = total + got[slot].astype(F32)
            buf[place] = total.astype(LOW)
            copies.append(remote(buf.at[place], second.at[i], fs.at[n, i], fr.at[n, i], peer, at.t))
            copies[-1].start()
        total = buf[keep].astype(F32)
        for slot in keep_slots:
            total = total + got[slot].astype(F32)
        buf[keep] = total.astype(LOW)
        big.append((buf, keep, second, copies))

    for i in range(8, 15):
        loads[i].wait()
    swap_dh1.wait_recv()
    def do_pair(j, _):
        acc = dot_nt(dh1b[:, pl.ds(0, Dd)], wo[0, hcols(j), :])
        for o in range(1, nd):
            acc = acc + dot_nt(dh1b[:, pl.ds(o * Dd, Dd)], wo[o, hcols(j), :])
        dos[:, hcols(j)] = acc.astype(LOW)
        return 0

    lax.fori_loop(0, nz, do_pair, 0)

    def kind_of(k):
        return k % 2 if isinstance(k, int) else lax.rem(k, 2)

    def so(k):
        j = far_first(k, at.z, nz)
        return Scatter(at, kind_of(k), lambda o: wo.at[o, hcols(j)], lambda i: ol.at[k, i], lambda i: ol2.at[k, i],
                       oss.at[k], osr.at[k], oss2.at[k], osr2.at[k])

    def sq(k):
        j = far_first(k, at.z, nz)
        return Scatter(at, kind_of(k), lambda o: wq.at[j, drows(o)], lambda i: ql.at[k, i], lambda i: ql2.at[k, i],
                       qss.at[k], qsr.at[k], qss2.at[k], qsr2.at[k])

    def wo_unit(k, _):
        j = far_first(k, at.z, nz)

        def part(o, _):
            wo[o, hcols(j), :] = dot_tn(os_[:, hcols(j)], dh1b[:, drows(o)]).astype(LOW)
            return 0

        lax.fori_loop(0, nd, part, 0)
        so(k).either("start")
        return 0

    lax.fori_loop(0, nz, wo_unit, 0)

    lset[...] = lse[...].T
    dkv[...] = jnp.zeros_like(dkv)
    dxn1[...] = jnp.zeros_like(dxn1)
    here = at.z * KT + lax.broadcasted_iota(jnp.int32, (1, KT), 1)
    low_row = lo_row[0:1, :]

    def unit(k, _):
        j = far_first(k, at.z, nz)
        for hh in range(NH):
            cols = pl.ds(pl.multiple_of(j * HC + hh * HD, HD), HD)
            hid = j * NH + hh
            lrow = lset[pl.ds(hid, 1), :]
            qh = qs[:, cols]
            doh = dos[:, cols]
            delta = jnp.sum((doh.astype(F32) * os_[:, cols].astype(F32)).T, axis=0, keepdims=True)
            dq[...] = jnp.zeros_like(dq)

            def tile(b, _):
                kr_ = pl.ds(pl.multiple_of(b * KT, KT), KT)
                kt = kvs[kr_, pl.ds(0, HD)]
                vt = kvs[kr_, pl.ds(HD, HD)]
                s = dot_nt(kt, qh)
                place = b * KT + lax.broadcasted_iota(jnp.int32, (KT, KT), 0)
                s = jnp.where((place >= low_row) & (place <= here), s * scale, MASKED)
                p = jnp.exp(s - lrow)
                dkv[kr_, pl.ds(HD, HD)] += dot_nn(p.astype(LOW), doh)
                ds = (p * (dot_nt(vt, doh) - delta)).astype(LOW)
                dkv[kr_, pl.ds(0, HD)] += dot_nn(ds, qh)
                dq[...] += dot_tn(ds, kt)
                return 0

            lax.fori_loop(0, at.z + 1, tile, 0)
            u = dq[...] * scale
            qs[:, cols] = (u * cosf[...] - swap_halves(u) * sins[...]).astype(LOW)
        dqp = qs[:, hcols(j)]

        def back(o, _):
            dxn1[:, drows(o)] += dot_nt(dqp, wq[j, drows(o), :])
            wq[j, drows(o), :] = dot_tn(xn1[:, drows(o)], dqp).astype(LOW)
            return 0

        lax.fori_loop(0, nd, back, 0)
        sq(k).either("start")
        so(k).either("middle")
        return 0

    lax.fori_loop(0, nz, unit, 0)

    dkv[:, pl.ds(0, HD)] = dkv[:, pl.ds(0, HD)] * scale
    kvb[...] = dkv[...].astype(LOW)
    kswap = [remote(kvb.at[rows(2 * zz + 1 - at.c)], kland.at[zz], ks.at[zz], kr.at[zz], at.dp, at.sibling()) for zz in range(nz)]
    for cp in kswap:
        cp.start()
    swap_dh1.wait_send()
    dh1b[mine, :] = dxn1[theirs, :].astype(LOW)
    xswap = remote(dh1b.at[mine], xrecv, xsem.at[2], xsem.at[3], at.dp, at.sibling())
    xswap.start()

    def kpush(s):
        zz = lax.rem(at.z + s, nz)
        return remote(kvb.at[rows(2 * zz + at.c)], kz.at[s - 1], kzs.at[s - 1], kzr.at[s - 1], at.dp, 2 * zz + at.c)

    for s in range(1, nz + 1):
        zz = lax.rem(at.z + s, nz)
        r = rows(2 * zz + at.c)
        remote(kvb.at[rows(0)], kland.at[zz], ks.at[zz], kr.at[zz], at.dp, at.sibling()).wait_recv()
        dkv[r, :] = dkv[r, :] + kland[zz].astype(F32)
        if s < nz:
            kvb[r, :] = dkv[r, :].astype(LOW)
            kpush(s).start()

    lax.fori_loop(0, nz, lambda k, _: (sq(k).either("middle"), 0)[1], 0)
    total = dkv[rows(at.t), :] + later[...].astype(F32)
    for s in range(1, nz):
        kpush(s).wait_recv()
        total = total + kz[s - 1].astype(F32)
    dk = total[:, :HD]
    dk = dk * cosf[mine, :] - swap_halves(dk) * sins[mine, :]
    dkvp = jnp.concatenate([dk, total[:, HD:]], axis=1).astype(LOW)


    def wpush(s):
        tt = lax.rem(at.t + s, nt)
        return remote(wd2.at[pl.ds(pl.multiple_of(tt * Ds, Ds), Ds)], wl.at[at.t], ws.at[s - 1], wr.at[at.t], at.dp, tt)

    def upush(s):
        tt = lax.rem(at.t + s, nt)
        return remote(gpart.at[:, pl.ds(pl.multiple_of(tt * Ds, Ds), Ds)], gl.at[at.t], us.at[s - 1], ur.at[at.t], at.dp, tt)

    for o in range(nd):
        wd2[pl.ds(o * Dd, Dd), :] = dot_tn(xn1[mine, pl.ds(o * Dd, Dd)], dkvp).astype(LOW)
    for s in range(1, nt):
        wpush(s).start()

    xswap.wait_recv()
    for o in range(nd):
        cols = pl.ds(o * Dd, Dd)
        dxn1[mine, cols] = dxn1[mine, cols] + xrecv[:, cols].astype(F32) + dot_nt(dkvp, wkv[cols, :])

    def put_tokens(cols, v):
        tgrad[:, cols] = tgrad[:, cols] + v

    rms_back(lambda cols: tok[:, cols].astype(F32), lambda cols: dxn1[mine, cols], 0, put_tokens)
    for s in range(1, nt):
        upush(s).start()

    def zpush(k, buf, land, ss, rs):
        j = far_first(k, at.z, nz)
        return remote(buf.at[k], land.at[at.z], ss.at[k], rs.at[at.z], at.dp, 2 * j + at.c)

    def o_total(k, _):
        def put(v):
            oz[k] = v.astype(LOW)

        so(k).either("total", put)
        pl.when(k < nz - 1)(lambda: zpush(k, oz, olz, ozs, ozr).start())
        return 0

    def q_total(k, _):
        def put(v):
            qz[k] = v.astype(LOW)

        sq(k).either("total", put)
        pl.when(k < nz - 1)(lambda: zpush(k, qz, qlz, qzs, qzr).start())
        return 0

    lax.fori_loop(0, nz, o_total, 0)

    per = nt // nd
    wl[at.t] = wd2[pl.ds(pl.multiple_of(at.t * Ds, Ds), Ds), :]
    gl[at.t] = gpart[:, pl.ds(pl.multiple_of(at.t * Ds, Ds), Ds)]
    for s in range(1, nt):
        o = lax.rem(at.t + s, nt)
        remote(wd2.at[pl.ds(0, Ds)], wl.at[o], ws.at[s - 1], wr.at[o], at.dp, o).wait_recv()
        remote(gpart.at[:, pl.ds(0, Ds)], gl.at[o], us.at[s - 1], ur.at[o], at.dp, o).wait_recv()
    wsum = wl[0].astype(F32)
    usum = gl[0]
    for o in range(1, nt):
        wsum = wsum + wl[o].astype(F32)
        usum = usum + gl[o]
    owner = at.t // per
    is_owner = at.dp == owner
    slot = jnp.where(is_owner, at.t - at.dp * per, 0)
    w2[...] = wsum.astype(LOW)
    u2[...] = usum
    to = jnp.where(is_owner, lax.rem(at.dp + 1, nd), owner)
    give_w = remote(w2, w2l.at[at.dp], w2s.at[0], w2r.at[at.dp], to, at.t)
    give_u = remote(u2, u2l.at[at.dp], u2s.at[0], u2r.at[at.dp], to, at.t)

    def spread(s):
        tt = lax.rem(at.t + s, nt)
        return [remote(wfin.at[slot], wfin.at[slot], w3s.at[s - 1], w3r.at[slot], at.dp, tt),
                remote(gfin.at[slot], gfin.at[slot], u3s.at[s - 1], u3r.at[slot], at.dp, tt)]

    @pl.when(jnp.logical_not(is_owner))
    def _():
        give_w.start()
        give_u.start()

    lax.fori_loop(0, nz, q_total, 0)

    def square(v):
        return jnp.sum(v * v, axis=(0, 1), keepdims=True)

    share[...] = jnp.zeros_like(share)

    @pl.when(is_owner)
    def _():
        w2l[at.dp] = w2[...]
        u2l[at.dp] = u2[...]
        for s in range(1, nd):
            o = lax.rem(at.dp + s, nd)
            remote(w2, w2l.at[o], w2s.at[0], w2r.at[o], o, at.t).wait_recv()
            remote(u2, u2l.at[o], u2s.at[0], u2r.at[o], o, at.t).wait_recv()
        wtot = w2l[0].astype(F32)
        utot = u2l[0]
        for o in range(1, nd):
            wtot = wtot + w2l[o].astype(F32)
            utot = utot + u2l[o]
        wfin[slot] = wtot.astype(LOW)
        gfin[slot] = utot
        shared = square(wtot.astype(LOW).astype(F32)) + square(utot)
        share[...] = jnp.broadcast_to(shared, share.shape)
        for s in range(1, nt):
            for cp in spread(s):
                cp.start()

    squares = jnp.zeros((1, 1), F32)
    out_copies = []
    for n, (buf, keep, second, copies) in enumerate(big):
        total = buf[keep].astype(F32)
        for i, cp in enumerate(copies):
            cp.wait_recv()
            total = total + second[i].astype(F32)
        squares = squares + square(total)
        out_copies.append(pltpu.make_async_copy(second, (got_g, got_u, got_d, got_e)[n], outs.at[n]))
        out_copies.append(pltpu.make_async_copy(buf.at[keep], (keep_g, keep_u, keep_d, keep_e)[n], outs.at[4 + n]))
        for cp in out_copies[-2:]:
            cp.start()
    own_k = nz - 1
    for buf, land, ss, rs, out in ((oz, olz, ozs, ozr, go_out), (qz, qlz, qzs, qzr, gq_out)):
        total = buf[own_k].astype(F32)
        for s in range(1, nz):
            zz = lax.rem(at.z + s, nz)
            remote(buf.at[0], land.at[zz], ss.at[0], rs.at[zz], at.dp, at.sibling()).wait_recv()
            total = total + land[zz].astype(F32)
        squares = squares + square(total)
        out[...] = total
    squares = squares + share[0:1, 0:1]

    norms[at.t] = jnp.broadcast_to(squares, norms.shape[1:])

    def npush(s):
        return remote(norms.at[at.t], norms.at[at.t], ns.at[s - 1], nr.at[at.t], at.dp, lax.rem(at.t + s, nt))

    def n2push(s):
        return remote(normd.at[at.dp], normd.at[at.dp], n2s.at[s - 1], n2r.at[at.dp], lax.rem(at.dp + s, nd), at.t)

    for s in range(1, nt):
        npush(s).start()
    for q in range(per):
        t_from = at.dp * per + q

        @pl.when(at.t != t_from)
        def _(q=q, t_from=t_from):
            remote(wfin.at[q], wfin.at[q], w3s.at[0], w3r.at[q], at.dp, at.sibling()).wait_recv()
            remote(gfin.at[q], gfin.at[q], u3s.at[0], u3r.at[q], at.dp, at.sibling()).wait_recv()

        gkv_out[pl.ds(q * Ds, Ds), :] = wfin[q].astype(F32)
        gg_out[:, pl.ds(q * Ds, Ds)] = gfin[q]
    for s in range(1, nt):
        o = lax.rem(at.t + s, nt)
        remote(norms.at[o], norms.at[o], ns.at[s - 1], nr.at[o], at.dp, o).wait_recv()
    group = norms[0]
    for o in range(1, nt):
        group = group + norms[o]
    normd[at.dp] = group
    for s in range(1, nd):
        n2push(s).start()
    for s in range(1, nd):
        o = lax.rem(at.dp + s, nd)
        remote(normd.at[o], normd.at[o], n2s.at[s - 1], n2r.at[o], o, at.t).wait_recv()
    group = normd[0]
    for o in range(1, nd):
        group = group + normd[o]
    norm_out[...] = jnp.sqrt(group)

    for cp in out_copies:
        cp.wait()
    xswap.wait_send()
    for _, _, _, copies in big:
        for cp in copies:
            cp.wait_send()
    for cp in kswap:
        cp.wait_send()
    for s in range(1, nz):
        kpush(s).wait_send()
    for s in range(1, nt):
        wpush(s).wait_send()
        upush(s).wait_send()
        npush(s).wait_send()
    for s in range(1, nd):
        n2push(s).wait_send()

    def drain(k, _):
        so(k).either("drain")
        sq(k).either("drain")

        @pl.when(k < nz - 1)
        def _():
            zpush(k, oz, olz, ozs, ozr).wait_send()
            zpush(k, qz, qlz, qzs, qzr).wait_send()

        return 0

    lax.fori_loop(0, nz, drain, 0)

    @pl.when(jnp.logical_not(is_owner))
    def _():
        give_w.wait_send()
        give_u.wait_send()

    @pl.when(is_owner)
    def _():
        for s in range(1, nt):
            for cp in spread(s):
                cp.wait_send()


def grads(nd, nt, small, big_in, pieces):
    R, D = small[1].shape
    nz, ny = nt // 2, nd // 2
    h1, dxn2, xn1, wq, wo, wkv, kv, q, o = big_in
    Dd, HC = wo.shape[2], wq.shape[2]
    F = pieces[0].shape[2]
    Fh = F // 2
    S = R * nt
    Ds = D // nt
    W2 = 2 * HD
    slots = max(2 * (ny - 1), ny)
    hops = max(1, ny - 1)
    dma = lambda *s: pltpu.SemaphoreType.DMA(s)
    hbm = pl.BlockSpec(memory_space=pltpu.HBM)
    vm = pl.BlockSpec(memory_space=pltpu.VMEM)
    b = lambda *s: pltpu.VMEM(s, LOW)
    f = lambda *s: pltpu.VMEM(s, F32)
    shapes = [(R, D), (Dd, HC), (HC, Dd), (Dd, W2), (8, Dd), (8, 128)]
    lows = [(Dd, F), (Dd, F), (Fh, Dd), (Fh, Dd), (1, Dd, F), (hops, Dd, F), (1, Fh, Dd), (hops, Fh, Dd)]
    return pl.pallas_call(
        functools.partial(grads_kernel, nd, nt),
        out_shape=tuple([jax.ShapeDtypeStruct(s, F32) for s in shapes] + [jax.ShapeDtypeStruct(s, LOW) for s in lows]),
        in_specs=[vm] * 8 + [hbm] * 17,
        out_specs=(vm,) * 6 + (hbm,) * 8,
        scratch_shapes=[
            b(2 * R, D), b(nz, D, HC), b(nd, nz * HC, Dd), b(D, W2), b(S, W2), b(2 * R, nz * HC), b(2 * R, nz * HC), b(2 * R, nz * HC),
            b(2 * R, D), f(2 * R, D), f(128, 2 * R), f(S, W2), f(2 * R, HD),
            b(2, Dd, F), b(ny, Dd, F), b(2, Fh, Dd), b(ny, Fh, Dd),
            b(1, Dd, F), b(hops, Dd, F), b(1, Fh, Dd), b(hops, Fh, Dd),
            b(2 * (ny - 1), Dd, F), b(ny, Dd, F), b(2 * (ny - 1), Fh, Dd), b(ny, Fh, Dd),
            b(nz, slots, Dd, HC), b(nz, hops, Dd, HC), b(nz, slots, HC, Dd), b(nz, hops, HC, Dd),
            b(nz, Dd, HC), b(nz, HC, Dd), b(nz, Dd, HC), b(nz, HC, Dd),
            b(S, W2), b(nz, R, W2), b(nz, R, W2), b(R, D),
            b(nt, Ds, W2), b(D, W2), b(Ds, W2), b(nd, Ds, W2), b(nt // nd, Ds, W2),
            f(nt, 8, Ds), f(8, D), f(8, Ds), f(nd, 8, Ds), f(nt // nd, 8, Ds), f(8, 128), f(nt, 8, 128), f(nd, 8, 128),
            dma(17), dma(4), dma(4, hops), dma(4, hops),
            dma(nz, slots), dma(nz, slots), dma(nz, hops), dma(nz, hops), dma(nz, slots), dma(nz, slots), dma(nz, hops), dma(nz, hops),
            dma(nz), dma(nz), dma(nz), dma(nz),
            dma(nz), dma(nz), dma(nz), dma(nz),
            dma(nt), dma(nt), dma(1), dma(nd), dma(nt), dma(nt // nd),
            dma(nt), dma(nt), dma(1), dma(nd), dma(nt), dma(nt // nd),
            dma(nt), dma(nt), dma(nd), dma(nd), dma(8),
        ],
        compiler_params=pltpu.CompilerParams(collective_id=3, has_side_effects=True, vmem_limit_bytes=63 << 20),
        cost_estimate=pl.CostEstimate(flops=30 << 30, bytes_accessed=40 << 20, transcendentals=8 * 512 * 2048),
        name="grads",
    )(*small, *big_in, *pieces)


def advance(grad_raw, weight, moment, average, factor, rate):
    average_decay = min(AVERAGE_TOP, (1.0 + STEP) / (10.0 + STEP))
    clipped = grad_raw * factor
    moment_new = MOMENTUM * moment + clipped
    weight_new = weight - rate * (clipped + MOMENTUM * moment_new)
    average_new = average_decay * average + (1.0 - average_decay) * weight_new
    return (clipped, moment_new, average_new, weight_new, weight_new.astype(jnp.bfloat16))


def local(
    tokens,
    cotangent,
    kv_later,
    lengths,
    query_weight,
    query_moment,
    query_average,
    keyvalue_weight,
    keyvalue_moment,
    keyvalue_average,
    output_weight,
    output_moment,
    output_average,
    gateup_weight,
    gateup_moment,
    gateup_average,
    down_weight,
    down_moment,
    down_average,
    norm_gains,
    gains_moment,
    gains_average,
):
    masters = (query_weight, keyvalue_weight, output_weight, gateup_weight, down_weight, norm_gains)
    low_query, low_kv, low_output, low_gateup, low_down, low_gains = (w.astype(LOW) for w in masters)
    nd, nt = lax.axis_size("dp"), lax.axis_size("tensor")
    row_count = tokens.shape[0]
    pair_rows = 2 * row_count

    doc_lengths = lengths[0]
    endings = jnp.cumsum(doc_lengths)
    beginnings = endings - doc_lengths
    places = (lax.axis_index("tensor") // 2) * pair_rows + jnp.arange(pair_rows, dtype=jnp.int32)
    segment = jnp.sum((places[:, None] >= endings[None, :]).astype(jnp.int32), axis=1)
    picked = segment[:, None] == jnp.arange(doc_lengths.shape[0], dtype=jnp.int32)[None, :]
    first = jnp.sum(jnp.where(picked, beginnings[None, :], 0), axis=1).astype(jnp.int32)
    half_size = HD // 2
    frequency = jnp.exp(jnp.arange(half_size, dtype=F32) * (-2.0 * math.log(ROPE_BASE) / HD))
    angles = (places - first).astype(F32)[:, None] * frequency[None, :]
    cosine, sine = jnp.cos(angles), jnp.sin(angles)
    cosine_full = jnp.concatenate([cosine, cosine], axis=1)
    sine_full = jnp.concatenate([-sine, sine], axis=1)
    gain_rows = jnp.pad(low_gains.astype(F32), ((0, 6), (0, 0)))

    grad_rows = lax.all_gather(cotangent, "tensor", axis=0, tiled=True)
    hidden_one, normed_two, gains_all, lse, normed_one, all_query, all_output, all_kv, kv_rows, queries, attended = attend(
        nd, nt, tokens, gain_rows, low_query, low_kv, low_output, cosine_full, sine_full, first[:, None]
    )
    grad_normed_two, *pieces, mlp_rows = mlp(nd, nt, normed_two, grad_rows, low_gateup, low_down)
    mixed = hidden_one + lax.psum_scatter(mlp_rows, "tensor", scatter_dimension=0, tiled=True).astype(F32)
    tokens_grad, own_query, own_output, grad_keyvalue, gains_sum, norm_tile, *halves = grads(
        nd,
        nt,
        (cotangent, tokens, gains_all, cosine_full, sine_full, jnp.broadcast_to(first[None, :], (8, pair_rows)), lse, kv_later),
        (hidden_one, grad_normed_two, normed_one, all_query, all_output, all_kv, kv_rows, queries, attended),
        pieces,
    )
    whole = [kept.astype(F32) + jnp.sum(got.astype(F32), axis=0) for kept, got in zip(halves[:4], halves[4:])]
    own_gateup = jnp.stack(whole[:2])
    own_down = jnp.concatenate(whole[2:], axis=0)
    grad_gains = gains_sum[:2]
    grad_norm = norm_tile[0, 0]
    factor = jnp.minimum(1.0, CLIP / (grad_norm + 1e-06))
    query_set = advance(
        own_query, query_weight, query_moment, query_average, factor, LEARNING_RATES[0]
    )
    keyvalue_set = advance(
        grad_keyvalue, keyvalue_weight, keyvalue_moment, keyvalue_average, factor, LEARNING_RATES[1]
    )
    output_set = advance(
        own_output, output_weight, output_moment, output_average, factor, LEARNING_RATES[2]
    )
    gateup_set = advance(
        own_gateup, gateup_weight, gateup_moment, gateup_average, factor, LEARNING_RATES[3]
    )
    down_set = advance(own_down, down_weight, down_moment, down_average, factor, LEARNING_RATES[4])
    gains_set = advance(
        grad_gains, norm_gains, gains_moment, gains_average, factor, LEARNING_RATES[5]
    )
    return (
        mixed,
        mixed.astype(jnp.bfloat16),
        tokens_grad,
        grad_norm,
        query_set[0],
        query_set[1],
        query_set[2],
        query_set[3],
        query_set[4],
        keyvalue_set[0],
        keyvalue_set[1],
        keyvalue_set[2],
        keyvalue_set[3],
        keyvalue_set[4],
        output_set[0],
        output_set[1],
        output_set[2],
        output_set[3],
        output_set[4],
        gateup_set[0],
        gateup_set[1],
        gateup_set[2],
        gateup_set[3],
        gateup_set[4],
        down_set[0],
        down_set[1],
        down_set[2],
        down_set[3],
        down_set[4],
        gains_set[0],
        gains_set[1],
        gains_set[2],
        gains_set[3],
        gains_set[4],
    )


def solution(mesh):
    return jax.shard_map(
        local,
        mesh=mesh,
        in_specs=(
            P(("dp", "tensor"), None),
            P(("dp", "tensor"), None),
            P(("dp", "tensor"), None),
            P("dp", None),
            P("dp", "tensor"),
            P("dp", "tensor"),
            P("dp", "tensor"),
            P("dp", None),
            P("dp", None),
            P("dp", None),
            P("tensor", "dp"),
            P("tensor", "dp"),
            P("tensor", "dp"),
            P(None, "dp", "tensor"),
            P(None, "dp", "tensor"),
            P(None, "dp", "tensor"),
            P("tensor", "dp"),
            P("tensor", "dp"),
            P("tensor", "dp"),
            P(None, "dp"),
            P(None, "dp"),
            P(None, "dp"),
        ),
        out_specs=(
            P(("dp", "tensor"), None),
            P(("dp", "tensor"), None),
            P(("dp", "tensor"), None),
            P(),
            P("dp", "tensor"),
            P("dp", "tensor"),
            P("dp", "tensor"),
            P("dp", "tensor"),
            P("dp", "tensor"),
            P("dp", None),
            P("dp", None),
            P("dp", None),
            P("dp", None),
            P("dp", None),
            P("tensor", "dp"),
            P("tensor", "dp"),
            P("tensor", "dp"),
            P("tensor", "dp"),
            P("tensor", "dp"),
            P(None, "dp", "tensor"),
            P(None, "dp", "tensor"),
            P(None, "dp", "tensor"),
            P(None, "dp", "tensor"),
            P(None, "dp", "tensor"),
            P("tensor", "dp"),
            P("tensor", "dp"),
            P("tensor", "dp"),
            P("tensor", "dp"),
            P("tensor", "dp"),
            P(None, "dp"),
            P(None, "dp"),
            P(None, "dp"),
            P(None, "dp"),
            P(None, "dp"),
        ),
        check_vma=False,
    )
```

time: 1420 us -> 657 us (0.46)
  waiting for transfers between devices: 784 us -> 0.72 us
  Pallas kernels: 174 us -> 556 us
  matrix products: 137 us -> 0 us
  blocking collectives: 92.2 us -> 0 us
  other arithmetic: 115 us -> 42.9 us
  local copies, waits for them, and re-layouts: 67.2 us -> 35.2 us
  loops' own time: 16.1 us -> 0 us
    pallas_call x0 -> x2, Pallas kernels: none -> 362 us  [the longest x1 211 us: grads(): pl.pallas_call(functools.partial(grads_kernel, nd, nt), out_shape=tuple([...]
    reduce_scatter x7 -> x0, waiting for transfers between devices: 358 us -> none  [the longest x1 87.6 us: local(): lax.psum_scatter(normed_part.astype(jnp.bfloat16), 'tensor', scatter_dime...]
    all_gather x5 -> x0, waiting for transfers between devices: 203 us -> none  [the longest x1 93.5 us: local(): lax.all_gather(grad_hidden.astype(jnp.bfloat16), 'tensor', axis=0, tiled=...]
    psum x1 -> x0, waiting for transfers between devices: 137 us -> none  [local(): lax.psum((grad_keyvalue_part, jnp.stack([gain_grad_one, gain_grad_two])),...]
    dot_general x37 -> x0, matrix products: 137 us -> none  [the longest x8 21.1 us: block_scores(): jnp.einsum('hqd,kd->hqk', query_block, keys_low, preferred_element_type=j...]
    psum x2 -> x0, blocking collectives: 82.7 us -> none  [the longest x1 43 us: local(): grad_norm = jnp.sqrt(lax.psum(local_squares, ('dp', 'tensor')))]
    all_gather x1, waiting for transfers between devices: 78.7 us -> 0.02 us  [local(): grad_rows = lax.all_gather(cotangent, 'tensor', axis=0, tiled=True)]
    reduce_sum x15 -> x2, other arithmetic: 28 us -> 0.17 us  [the longest x1 0.09 us: local(): jnp.sum((places[:, None] >= endings[None, :]).astype(jnp.int32), axis=1)]
  transfers between devices with their start and end apart: 16 -> 2, of which waited for: 14 -> 0; matrix products, arithmetic and copies ran while one was open for 14% -> 11% of each run, Pallas kernels for 0% -> 56%
where the time goes in v2:
time: 657 us; the launch traced here: 651 us
  Pallas kernels  556 us (85%)
  other arithmetic  42.9 us (7%)
  local copies, waits for them, and re-layouts  35.2 us (5%)
  between operations  15.5 us (2%)
    pallas_call x1, Pallas kernels, grads(): pl.pallas_call(functools.partial(grads_kernel, nd, nt), out_shape=tuple([...  211 us
    pallas_call x1, Pallas kernels, mlp(): pl.pallas_call(functools.partial(mlp_kernel, nd, nt), out_shape=(jax.Shap...  194 us
    pallas_call x1, Pallas kernels, attend(): pl.pallas_call(functools.partial(attend_kernel, nd, nt), out_shape=tuple(...  152 us
    unnamed x83, local copies, waits for them, and re-layouts  29.9 us
  transfers between devices with their start and end apart: 2, of which 0 were waited for; matrix products, arithmetic and copies ran while one was open for 11% of the time, Pallas kernels for 56%

profile of v2, /device:TPU:0, one launch (start us, length us, event | category | flops | bytes accessed | tf_op | source)
XLA Modules:
  0.0 650.8 jit_solution(13003909577832277374)
XLA Ops:
  8.0 1.0 reduce-window.4
  10.8 1.8 convert_element_type.72.wq_in
  12.6 1.8 convert_element_type.73.wkv_in
  15.1 1.3 convert_element_type.77
  16.4 2.7 copy.86.wgu_in
  22.6 151.7 %attend.1 = (f32[256,2048]{1,0:T(8,128)}, bf16[256,2048]{1,0:T(8,128)(2,1)}, f32[4,8,512]{2,1,0:T(8,128)}, f32[512,128]{1,0:T(8,128)}, bf16[512,2048]{1,0:T(8,12...) custom-call(bf16[256,2048]{1,0:T(8,128)(2,1)} %tok.3, ...), custom_call_target="tpu_custom_call" | custom-call | flops 21474836480 | bytes 41943040 | tf_op jit(solution)/shard_map/attend/pallas_call | solution.py:745
  174.3 193.9 %mlp.1 = (f32[256,2048]{1,0:T(8,128)}, bf16[2,512,704]{2,1,0:T(8,128)(2,1)}, bf16[2,512,704]{2,1,0:T(8,128)(2,1)}, bf16[2,512,704]{2,1,0:T(8,128)(2,1)}, bf16[2,...) custom-call(bf16[256,2048]{1,0:T(8,128)(2,1)} %get-tuple-element.70., ...), custom_call_target="tpu_custom_call" | custom-call | flops 35433480192 | bytes 41943040 | tf_op jit(solution)/shard_map/mlp/pallas_call | solution.py:456
  368.2 1.8 copy-done.3
  370.0 2.5 copy.89
  372.6 3.6 copy.87
  376.2 2.3 copy.88
  379.1 210.8 %grads.1 = (f32[256,2048]{1,0:T(8,128)}, f32[512,256]{1,0:T(8,128)}, f32[256,512]{1,0:T(8,128)}, f32[512,256]{1,0:T(8,128)}, f32[8,512]{1,0:T(8,128)}, /*index=5...) custom-call(bf16[256,2048]{1,0:T(8,128)(2,1)} %dy.1, ...), custom_call_target="tpu_custom_call" | custom-call | flops 32212254720 | bytes 41943040 | tf_op jit(solution)/shard_map/grads/pallas_call | solution.py:1266
  589.8 1.2 slice.6
  591.7 1.7 fusion.1
  593.4 1.7 fusion
  596.0 4.0 fusion.6
  600.0 3.4 copy.93
  603.4 5.0 multiply_add_fusion
  608.4 3.4 copy.92
  611.8 3.4 copy.90
  615.2 3.9 multiply_add_fusion.1
  619.1 3.6 copy.91
  622.7 1.5 copy.94
  624.3 1.4 fusion.4
  626.6 1.2 fusion.7
  628.8 1.2 fusion.8
  631.0 1.2 fusion.9
  633.8 2.3 fusion.5
  636.1 1.5 multiply_add_fusion.2
  637.7 1.1 copy-done.9
  638.8 3.4 fusion.10
  642.2 1.3 copy.96
  (98 shorter events, 12.9 us)
Async XLA Ops:
  7.2 7.1 %copy-start.14 = (f32[256,512]{1,0:T(8,128)S(1)}, f32[256,512]{1,0:T(8,128)}, u32[]{:S(2)}) copy-start(f32[256,512]{1,0:T(8,128)} %param.32) | copy-start | bytes 1572868
  7.2 7.8 %copy-start.34 = (f32[2,512]{1,0:T(2,128)S(1)}, f32[2,512]{1,0:T(2,128)}, u32[]{:S(2)}) copy-start(f32[2,512]{1,0:T(2,128)} %param.41) | copy-start | bytes 12292
  7.2 7.8 %copy-start.2 = (f32[2,512,704]{1,2,0:T(8,128)S(1)}, f32[2,512,704]{1,2,0:T(8,128)}, u32[]{:S(2)}) copy-start(f32[2,512,704]{1,2,0:T(8,128)} %param.35) | copy-start | bytes 8650756
  7.2 167.1 %all-gather.2.cloned.1.call-start = ((), (), s32[]{:S(2)}) async-start(), calls=%async_computation.1 | async-start | bytes 9437184 | tf_op jit(solution)/shard_map/all_gather | solution.py:1350
  8.0 629.7 %reduce-scatter.2.cloned.1.call-start = ((), (), s32[]{:S(2)}) async-start(), calls=%async_computation.2 | async-start | bytes 9437184 | tf_op jit(solution)/shard_map/reduce_scatter | solution.py:1355
  16.4 2.7 copy-start.5
  372.6 3.6 copy-start.8
  591.7 3.4 copy-start.1
  593.4 2.5 copy-start
  619.1 3.6 copy-start.4
  622.7 3.0 copy-start.35
  622.7 3.6 copy-start.31
  622.7 3.6 copy-start.32
  622.7 3.7 copy-start.29
  622.7 3.7 copy-start.30
  624.2 2.3 copy-start.15
  624.2 2.3 copy-start.23
  624.2 2.3 copy-start.28
  625.7 2.1 copy-start.33
  626.6 2.2 copy-start.16
  626.6 2.2 copy-start.24
  626.6 2.2 copy-start.27
  627.8 2.2 copy-start.11
  628.8 2.2 copy-start.17
  628.8 2.2 copy-start.25
  628.8 2.1 copy-start.26
  630.0 2.2 copy-start.12
  631.0 2.9 copy-start.6
  631.0 2.9 copy-start.18
  633.8 2.3 copy-start.19
  636.1 2.6 copy-start.9
  638.7 3.4 copy-start.10
  (7 other events, 10.4 us)
Sparse Core Ops, SparseCore 0:
  9.7 110.3 all-gather.1
  368.4 111.3 reduce-scatter.1

commit v3 on v2

--- a/solution.py
+++ b/solution.py
@@ -100,6 +100,10 @@
     return jnp.where(j <= 2 * m, two, one)
 
 
+def near_first(k, z, nz):
+    return far_first(nz - 1 - k, z, nz)
+
+
 class Gather:
     def __init__(self, at, src, dst, xs, ys, xf, yf, recv, kind):
         self.at, self.src, self.dst, self.kind = at, src, dst, kind
@@ -172,24 +176,26 @@
             cp.wait_send()
 
 
-def mlp_kernel(nd, nt, xn_in, dy_in, wgu_in, wd_in,
-               dxn_out, mine_g, land_g, mine_u, land_u, mine_d, land_d, mine_e, land_e, out_out,
-               xall, dyv, wgu, wd, mid, dg, du, psend, pown, precv, zrecv,
-               lsem, wx, wy, wxf, wyf, wr, ar, ac, asr, asl, ps, pr, zs, zr, osem, p1l, p1s, p1r):
+def mlp_kernel(nd, nt, xn_in, dy_in, w_all, w_in,
+               dxn_out, mine_g, land_g, mine_u, land_u, down_out, out_out,
+               both, wts, act, psend, pown, precv, zrecv, bsend, bown, bland,
+               lsem, wx, wy, wxf, wyf, wr, ar, ac, asr, asl, ps, pr, zs, zr, bs, br, osem, dsem, p1l, p1s, p1r):
     at = Place(nd, nt)
-    nz = at.nz
+    nz, nx, ny = at.nz, at.nx, at.ny
     R, D = xn_in.shape
-    Dd = wgu_in.shape[1]
-    F = wgu_in.shape[2]
+    F, Dd = w_in.shape
     Fh = F // 2
+    CH = zs.shape[1]
+    CR = R // CH
     rows = lambda t: pl.ds(pl.multiple_of(t * R, R), R)
     dcols = lambda o: pl.ds(pl.multiple_of(o * Dd, Dd), Dd)
+    xall, dyv = both.at[0], both.at[1]
 
     own_loads = [
         pltpu.make_async_copy(xn_in, xall.at[rows(at.t)], lsem.at[0]),
         pltpu.make_async_copy(dy_in, dyv, lsem.at[1]),
-        pltpu.make_async_copy(wgu_in, wgu.at[:, dcols(at.dp)], lsem.at[2]),
-        pltpu.make_async_copy(wd_in, wd.at[at.dp], lsem.at[3]),
+        pltpu.make_async_copy(w_all, wts.at[pl.ds(0, 2)], lsem.at[2]),
+        pltpu.make_async_copy(w_in, wts.at[2, :, dcols(at.dp)], lsem.at[3]),
     ]
     for cp in own_loads:
         cp.start()
@@ -197,11 +203,9 @@
 
     gathers = []
     for p in range(2):
-        gathers.append(Gather(at, wgu_in.at[p], lambda o, p=p: wgu.at[p, dcols(o)],
+        half = pl.ds(p * Fh, Fh)
+        gathers.append(Gather(at, w_in.at[half], lambda o, half=half: wts.at[2, half, dcols(o)],
                               wx.at[p], wy.at[p], wxf.at[p], wyf.at[p], wr.at[p], p))
-    for p in range(2):
-        gathers.append(Gather(at, wd_in.at[pl.ds(p * Fh, Fh)], lambda o, p=p: wd.at[o, pl.ds(p * Fh, Fh)],
-                              wx.at[2 + p], wy.at[2 + p], wxf.at[2 + p], wyf.at[2 + p], wr.at[2 + p], p))
 
     def right(o):
         return remote(xall.at[rows(o)], xall.at[rows(o)], asr.at[o], ar.at[o], at.dp, at.t + 2)
@@ -213,12 +217,10 @@
         return remote(xall.at[rows(o)], xall.at[rows(o)], ac.at[o], ar.at[o], at.dp, at.sibling())
 
     own_loads[0].wait()
-    across(at.t).start()
     pl.when(at.z < nz - 1)(lambda: right(at.t).start())
     pl.when(at.z > 0)(lambda: left(at.t).start())
-    for g in gathers[:2]:
-        g.start()
-    for g in gathers[2:]:
+    across(at.t).start()
+    for g in gathers:
         g.start()
 
     def line_step(s):
@@ -236,103 +238,139 @@
             pl.when(at.z > 0)(lambda: left(o).start())
             across(o).start()
 
-    for g in gathers[:2]:
+    for g in gathers:
         g.forward()
-    line_step(1)
-    for g in gathers[2:]:
-        g.forward()
-    for s in range(2, nz):
-        line_step(s)
     for cp in own_loads[1:]:
         cp.wait()
+
+    is_end = (at.z == 0) | (at.z == nz - 1)
+    piece = lambda c: pl.ds(pl.multiple_of(c * CR, CR), CR)
+
+    def swap(d):
+        return remote(psend, precv.at[d], ps.at[0], pr.at[d], at.dp, at.sibling())
+
+    def push_right(d, c):
+        return remote(pown.at[d, piece(c)], zrecv.at[d, piece(c)], zs.at[d, c], zr.at[d, c], at.dp, at.t + 2)
+
+    def push_left(d, c):
+        slot = jnp.where(d == at.z - 1, nz, d)
+        return remote(pown.at[d, piece(c)], zrecv.at[slot, piece(c)], zs.at[d, c], zr.at[slot, c], at.dp, at.t - 2)
+
+    def came(slot, c):
+        remote(pown.at[0, piece(c)], zrecv.at[slot, piece(c)], zs.at[0, c], zr.at[slot, c], at.dp, at.sibling()).wait_recv()
+
+    def relay(d, c, push):
+        pl.when(c == 0)(lambda: swap(d).wait_recv())
+
+        @pl.when(is_end)
+        def _():
+            pown[d, piece(c)] = (pown[d, piece(c)].astype(F32) + precv[d, piece(c)].astype(F32)).astype(LOW)
+
+        @pl.when(jnp.logical_not(is_end))
+        def _():
+            came(d, c)
+            pown[d, piece(c)] = (pown[d, piece(c)].astype(F32) + precv[d, piece(c)].astype(F32)
+                                 + zrecv[d, piece(c)].astype(F32)).astype(LOW)
+
+        push(d, c).start()
+
+    def relays(s, c):
+        pl.when(s > at.z)(lambda: relay(s, c, push_right))
+        pl.when(nz - 1 - s < at.z)(lambda: relay(nz - 1 - s, c, push_left))
+
+    def branch_swap(j):
+        return remote(bsend, bland.at[j], bs.at[0], br.at[j], at.dp, at.sibling())
+
+    def branch_copy(slot, j):
+        return pltpu.make_async_copy(bown.at[slot], out_out.at[j], osem.at[slot])
+
+    def branch_sum(k):
+        j = near_first(k, at.z, nz)
+        slot = lax.rem(k, 2)
+        branch_swap(j).wait_recv()
+
+        def part(c, _):
+            bown[slot, piece(c)] = (bown[slot, piece(c)].astype(F32) + bland[j, piece(c)].astype(F32)).astype(LOW)
+            return 0
+
+        lax.fori_loop(0, CH, part, 0)
+        branch_copy(slot, j).start()
+
+    def forward(j):
+        r = pl.ds(pl.multiple_of(j * 2 * R, 2 * R), 2 * R)
+        for lo in range(0, F, 256):
+            part = pl.ds(lo, min(256, F - lo))
+            gate, up = dot_nt(xall[r, :], wts[0, part, :]), dot_nt(xall[r, :], wts[1, part, :])
+            dmid = dot_nt(dyv[r, :], wts[2, part, :])
+            sig = 1.0 / (1.0 + jnp.exp(-gate))
+            silu = gate * sig
+            act[2, r, part] = (silu * up).astype(LOW)
+            act[1, r, part] = (dmid * silu).astype(LOW)
+            act[0, r, part] = (dmid * up * (sig * (1.0 + gate * (1.0 - sig)))).astype(LOW)
+
+    def block(k, _):
+        pl.when((k == nz - 1) & (k >= 2))(lambda: line_step(k))
+        j = near_first(k, at.z, nz)
+        across(2 * j + 1 - at.c).wait_recv()
+        slot = lax.rem(k, 2)
+        forward(j)
+        pl.when((k >= 1) & (k < nz - 2))(lambda: line_step(k + 1))
+        pl.when(k >= 1)(lambda: swap(j).wait_send())
+        r = pl.ds(pl.multiple_of(j * 2 * R, 2 * R), 2 * R)
+
+        def back(o, _):
+            cols = dcols(o)
+            v = dot_nn(act[0, r, :], wts[0, :, cols]) + dot_nn(act[1, r, :], wts[1, :, cols])
+            first = at.c == 0
+            psend[:, cols] = jnp.where(first, v[R:], v[:R]).astype(LOW)
+            pown[j, :, cols] = jnp.where(first, v[:R], v[R:]).astype(LOW)
+            return 0
+
+        lax.fori_loop(0, nd, back, 0)
+        swap(j).start()
+        s = jnp.where(is_end, k, k - 1)
+
+        @pl.when((s >= 1) & (is_end | (s < nz - 2)))
+        def _():
+            lax.fori_loop(0, CH, lambda c, _: (relays(s, c), 0)[1], 0)
+
+        pl.when(k >= 1)(lambda: branch_sum(k - 1))
+        pl.when(k >= 1)(lambda: branch_swap(j).wait_send())
+        pl.when(k >= 2)(lambda: branch_copy(slot, j).wait())
+
+        def branch(o, _):
+            cols = dcols(o)
+            v = dot_nn(act[2, r, :], wts[2, :, cols])
+            first = at.c == 0
+            bsend[:, cols] = jnp.where(first, v[R:], v[:R]).astype(LOW)
+            bown[slot, :, cols] = jnp.where(first, v[:R], v[R:]).astype(LOW)
+            return 0
+
+        lax.fori_loop(0, nd, branch, 0)
+        branch_swap(j).start()
+        return 0
+
+    if nz > 1:
+        line_step(1)
     for g in gathers:
         g.finish()
-    for zz in range(nz):
-        across(2 * zz + (1 - at.c)).wait_recv()
-
-    def swap(d, slot):
-        return remote(psend.at[slot], precv.at[d], ps.at[slot], pr.at[d], at.dp, at.sibling())
-
-    def push_right(d):
-        return remote(pown.at[d], zrecv.at[d], zs.at[d], zr.at[d], at.dp, at.t + 2)
-
-    def push_left(d):
-        slot = jnp.where(d == at.z - 1, nz, d)
-        return remote(pown.at[d], zrecv.at[slot], zs.at[d], zr.at[slot], at.dp, at.t - 2)
-
-    def came(slot):
-        remote(pown.at[0], zrecv.at[slot], zs.at[0], zr.at[slot], at.dp, at.sibling()).wait_recv()
-
-    is_end = (at.z == 0) | (at.z == nz - 1)
-
-    def tile(tt, put):
-        r = rows(tt)
-        x = xall[r, :]
-        gate = dot_nn(x, wgu[0])
-        up = dot_nn(x, wgu[1])
-        dmid = dot_nt(dyv[r, dcols(0)], wd[0])
-        for o in range(1, nd):
-            dmid = dmid + dot_nt(dyv[r, pl.ds(o * Dd, Dd)], wd[o])
-        sig = 1.0 / (1.0 + jnp.exp(-gate))
-        silu = gate * sig
-        mid[r, :] = (silu * up).astype(LOW)
-        du[r, :] = (dmid * silu).astype(LOW)
-        dg[r, :] = (dmid * up * (sig * (1.0 + gate * (1.0 - sig)))).astype(LOW)
-        put((dot_nt(dg[r, :], wgu[0]) + dot_nt(du[r, :], wgu[1])).astype(LOW))
-
-    def chain(k):
-        d = far_first(k, at.z, nz)
-        swap(d, 0).wait_recv()
-
-        @pl.when(is_end)
-        def _():
-            pown[d] = (pown[d].astype(F32) + precv[d].astype(F32)).astype(LOW)
-
-        @pl.when(jnp.logical_not(is_end))
-        def _():
-            came(d)
-            pown[d] = (pown[d].astype(F32) + precv[d].astype(F32) + zrecv[d].astype(F32)).astype(LOW)
-
-        pl.when(d > at.z)(lambda: push_right(d).start())
-        pl.when(d < at.z)(lambda: push_left(d).start())
-
-    def half(i, _):
-        k, own = i // 2, lax.rem(i, 2)
-        d = far_first(k, at.z, nz)
-        slot = lax.rem(k, 2)
-        pl.when((own == 0) & (k >= 2))(lambda: swap(d, slot).wait_send())
-
-        def put(v):
-            @pl.when(own == 0)
-            def _():
-                psend[slot] = v
-                swap(d, slot).start()
-
-            @pl.when(own == 1)
-            def _():
-                pown[d] = v
-
-        tile(2 * d + jnp.where(own == 0, 1 - at.c, at.c), put)
-        late = jnp.where(is_end, k, k - 2)
-        pl.when((own == 1) & (late >= 0) & (late < nz - 1))(lambda: chain(late))
-        return 0
-
-    lax.fori_loop(0, 2 * nz, half, 0)
-    for k in range(max(0, nz - 2), nz):
-        swap(0, k % 2).wait_send()
-
+    lax.fori_loop(0, nz, block, 0)
+    swap(0).wait_send()
+    branch_swap(0).wait_send()
+    branch_sum(jnp.int32(nz - 1))
     for g in gathers:
         g.drain()
-    for zz in range(nz):
-        o = 2 * zz + at.c
-        across(o).wait_send()
-        pl.when((at.z < nz - 1) & (zz <= at.z))(lambda o=o: right(o).wait_send())
-        pl.when((at.z > 0) & (zz >= at.z))(lambda o=o: left(o).wait_send())
-
-    W = min(256, Dd)
-    nx, ny = at.nx, at.ny
-
-    def hop(n, src, o, mine, land):
+
+    outs = ((mine_g, land_g), (mine_u, land_u))
+
+    def source(n, o):
+        return wts.at[n, :, dcols(o)]
+
+    def down_copy(o):
+        return pltpu.make_async_copy(wts.at[2, :, dcols(o)], down_out.at[:, dcols(o)], dsem.at[o])
+
+    def hop(n, o):
+        mine, land = outs[n]
         yy, xx = o // nx, lax.rem(o, nx)
         if n % 2 == 0:
             step = lax.rem(yy - at.y + ny, ny)
@@ -340,9 +378,9 @@
             stays, place, peer = yy == at.y, xx, yy * nx + at.x
         else:
             slot, stays, place, peer = yy, xx == at.x, yy, at.y * nx + xx
-        local = pltpu.make_async_copy(src, mine.at[place], p1l.at[n, place])
+        local = pltpu.make_async_copy(source(n, o), mine.at[place], p1l.at[n, place])
         slot = jnp.where(stays, 0, slot)
-        away = remote(src, land.at[slot], p1s.at[n, slot], p1r.at[n, slot], jnp.where(stays, at.x_peer(), peer), at.t)
+        away = remote(source(n, o), land.at[slot], p1s.at[n, slot], p1r.at[n, slot], jnp.where(stays, at.x_peer(), peer), at.t)
         return stays, local, away
 
     def order(n, i):
@@ -350,14 +388,14 @@
             return lax.rem(at.y + 1 + i // nx, ny) * nx + lax.rem(i, nx)
         return lax.rem(i, ny) * nx + jnp.where(i < ny, 1 - at.x, at.x)
 
-    def send(n, src, o, mine, land):
-        stays, local, away = hop(n, src, o, mine, land)
+    def send(n, o):
+        stays, local, away = hop(n, o)
         pl.when(stays)(lambda: local.start())
         pl.when(jnp.logical_not(stays))(lambda: away.start())
 
-    def settle(n, src, mine, land):
-        for i in range(nd):
-            stays, local, away = hop(n, src, order(n, i), mine, land)
+    def settle(n):
+        def one(i, _):
+            stays, local, away = hop(n, order(n, i))
 
             @pl.when(stays)
             def _():
@@ -368,121 +406,96 @@
                 away.wait_send()
                 away.wait_recv()
 
-    def wgrad(n, mine, land):
-        def block(i, _):
-            o = order(n, i)
-
-            def wtile(w, _):
-                cols = pl.ds(pl.multiple_of(o * Dd + w * W, W), W)
-                wgu[n, cols, :] = dot_tn(xall[:, cols], (du if n else dg)[...]).astype(LOW)
-                return 0
-
-            lax.fori_loop(0, Dd // W, wtile, 0)
-            send(n, wgu.at[n, dcols(o)], o, mine, land)
             return 0
 
-        lax.fori_loop(0, nd, block, 0)
-
-    def dgrad(n, mine, land):
-        half = pl.ds((n - 2) * Fh, Fh)
-
-        def block(i, _):
-            o = order(n, i)
-            if n == 2:
-                xall[pl.ds(0, F), dcols(o)] = dot_tn(mid[...], dyv[:, dcols(o)]).astype(LOW)
-            send(n, xall.at[half, dcols(o)], o, mine, land)
-            return 0
-
-        lax.fori_loop(0, nd, block, 0)
-
-    def otile(i, _):
-        slot = lax.rem(i, 2)
-        r = rows(i)
-        pl.when(i >= 2)(lambda: pltpu.make_async_copy(psend.at[slot], out_out.at[r], osem.at[slot]).wait())
-
-        def part(o, _):
-            psend[slot, :, dcols(o)] = dot_nn(mid[r, :], wd[o]).astype(LOW)
-            return 0
-
-        lax.fori_loop(0, nd, part, 0)
-        pltpu.make_async_copy(psend.at[slot], out_out.at[r], osem.at[slot]).start()
+        lax.fori_loop(0, nd, one, 0)
+
+    def wgrad(p, _):
+        n, i = p // nd, lax.rem(p, nd)
+        middle = jnp.logical_not(is_end)
+        early, late = p - 1, p // 2 - 3
+        pl.when(middle & (early >= 0) & (early < CH))(lambda: relays(jnp.int32(nz - 2), early))
+        pl.when(middle & (lax.rem(p, 2) == 0) & (late >= 0) & (late < CH - 1))(lambda: relays(jnp.int32(nz - 1), late))
+        o = jnp.where(n == 1, order(1, i), order(0, i))
+        for lo in range(0, F, 384):
+            part = pl.ds(lo, min(384, F - lo))
+            wts[n, part, dcols(o)] = dot_tn(act[n, :, part], both[n // 2, :, dcols(o)]).astype(LOW)
+        pl.when(n == 0)(lambda: send(0, o))
+        pl.when(n == 1)(lambda: send(1, o))
+        pl.when(n == 2)(lambda: down_copy(o).start())
         return 0
 
-    wgrad(0, mine_g, land_g)
-    if nz >= 2:
-        pl.when(jnp.logical_not(is_end))(lambda: chain(jnp.int32(nz - 2)))
-    wgrad(1, mine_u, land_u)
-    dgrad(2, mine_d, land_d)
-    dgrad(3, mine_e, land_e)
-    lax.fori_loop(0, nt, otile, 0)
-    for s in range(2):
-        pltpu.make_async_copy(psend.at[s], out_out.at[rows(0)], osem.at[s]).wait()
-
-    swap(at.z, 0).wait_recv()
-    dxn_out[...] = pown[at.z].astype(F32) + precv[at.z].astype(F32)
-
-    @pl.when(at.z > 0)
-    def _():
-        came(at.z)
-        dxn_out[...] = dxn_out[...] + zrecv[at.z].astype(F32)
-
-    @pl.when(at.z < nz - 1)
-    def _():
-        came(nz)
-        dxn_out[...] = dxn_out[...] + zrecv[nz].astype(F32)
+    lax.fori_loop(0, 3 * nd, wgrad, 0)
+    pl.when(jnp.logical_not(is_end))(lambda: relays(jnp.int32(nz - 1), jnp.int32(CH - 1)))
+    for slot in range(2):
+        branch_copy(slot, 0).wait()
+
+    swap(at.z).wait_recv()
+    for c in range(CH):
+        part = pl.ds(c * CR, CR)
+        pl.when(at.z > 0)(lambda c=c: came(at.z, c))
+        pl.when(at.z < nz - 1)(lambda c=c: came(nz, c))
+        total = pown[at.z, part].astype(F32) + precv[at.z, part].astype(F32)
+        total = total + jnp.where(at.z > 0, zrecv[at.z, part].astype(F32), 0.0)
+        total = total + jnp.where(at.z < nz - 1, zrecv[nz, part].astype(F32), 0.0)
+        dxn_out[part, :] = total.astype(LOW)
 
     for zz in range(nz):
+        o = 2 * zz + at.c
+
         @pl.when(zz != at.z)
         def _(zz=zz):
-            remote(pown.at[zz], zrecv.at[zz], zs.at[zz], zr.at[zz], at.dp, at.sibling()).wait_send()
-    settle(0, wgu.at[0, dcols(0)], mine_g, land_g)
-    settle(1, wgu.at[1, dcols(0)], mine_u, land_u)
-    settle(2, xall.at[pl.ds(0, Fh), dcols(0)], mine_d, land_d)
-    settle(3, xall.at[pl.ds(0, Fh), dcols(0)], mine_e, land_e)
-
-
-def mlp(nd, nt, xn, dy_all, wgu, wd):
+            for c in range(CH):
+                push_right(jnp.int32(zz), c).wait_send()
+
+        across(o).wait_send()
+        pl.when((at.z < nz - 1) & (zz <= at.z))(lambda o=o: right(o).wait_send())
+        pl.when((at.z > 0) & (zz >= at.z))(lambda o=o: left(o).wait_send())
+    for n in range(2):
+        settle(n)
+    for o in range(nd):
+        down_copy(o).wait()
+
+
+def mlp(nd, nt, xn, dy_all, w_all, w):
     R, D = xn.shape
     S = dy_all.shape[0]
-    Dd, F = wgu.shape[1:]
+    F, Dd = w.shape
     nz = nt // 2
     ny = nd // 2
+    ch = 4
     dma = lambda *s: pltpu.SemaphoreType.DMA(s)
     shape = lambda *s: jax.ShapeDtypeStruct(s, LOW)
-    Fh = F // 2
+    b = lambda *s: pltpu.VMEM(s, LOW)
     slots = max(2 * (ny - 1), ny)
     hbm = pl.BlockSpec(memory_space=pltpu.HBM)
     vm = pl.BlockSpec(memory_space=pltpu.VMEM)
     return pl.pallas_call(
         functools.partial(mlp_kernel, nd, nt),
         out_shape=(
-            jax.ShapeDtypeStruct((R, D), F32),
-            shape(2, Dd, F), shape(2 * (ny - 1), Dd, F), shape(ny, Dd, F), shape(ny, Dd, F),
-            shape(2, Fh, Dd), shape(2 * (ny - 1), Fh, Dd), shape(ny, Fh, Dd), shape(ny, Fh, Dd),
-            shape(S, D),
+            shape(R, D),
+            shape(2, F, Dd), shape(2 * (ny - 1), F, Dd), shape(ny, F, Dd), shape(ny, F, Dd),
+            shape(F, D),
+            shape(nz, R, D),
         ),
         in_specs=[hbm] * 4,
-        out_specs=(vm,) + (hbm,) * 9,
+        out_specs=(vm,) + (hbm,) * 6,
         scratch_shapes=[
-            pltpu.VMEM((S, D), LOW), pltpu.VMEM((S, D), LOW), pltpu.VMEM((2, D, F), LOW), pltpu.VMEM((nd, F, Dd), LOW),
-            pltpu.VMEM((S, F), LOW), pltpu.VMEM((S, F), LOW), pltpu.VMEM((S, F), LOW),
-            pltpu.VMEM((2, R, D), LOW), pltpu.VMEM((nz, R, D), LOW), pltpu.VMEM((nz, R, D), LOW), pltpu.VMEM((nz + 1, R, D), LOW),
-            dma(4), dma(4), dma(4, ny - 1), dma(4, ny - 1), dma(4, ny - 1), dma(4, nd),
-            dma(nt), dma(nt), dma(nt), dma(nt), dma(2), dma(nz), dma(nz), dma(nz + 1), dma(2), dma(4, max(2, ny)), dma(4, slots), dma(4, slots),
+            b(2, S, D), b(3, F, D), b(3, S, F),
+            b(R, D), b(nz, R, D), b(nz, R, D), b(nz + 1, R, D), b(R, D), b(2, R, D), b(nz, R, D),
+            dma(4), dma(2), dma(2, ny - 1), dma(2, ny - 1), dma(2, ny - 1), dma(2, nd),
+            dma(nt), dma(nt), dma(nt), dma(nt), dma(1), dma(nz), dma(nz, ch), dma(nz + 1, ch), dma(1), dma(nz), dma(2), dma(nd),
+            dma(2, max(2, ny)), dma(2, slots), dma(2, slots),
         ],
         compiler_params=pltpu.CompilerParams(collective_id=1, has_side_effects=True, vmem_limit_bytes=63 << 20),
         cost_estimate=pl.CostEstimate(flops=12 * S * D * F, bytes_accessed=40 << 20, transcendentals=S * F),
         name="mlp",
-    )(xn, dy_all, wgu, wd)
+    )(xn, dy_all, w_all, w)
 
 
 def swap_halves(u):
     h = u.shape[-1] // 2
     return jnp.concatenate([u[:, h:], u[:, :h]], axis=1)
-
-
-def near_first(k, z, nz):
-    return far_first(nz - 1 - k, z, nz)
 
 
 def greet_all(at):
@@ -541,12 +554,13 @@
                 self.across(o).wait_send()
 
 
-def attend_kernel(nd, nt, tok, gain, wq_in, wkv_in, wo_in, cosf, sins, lo_in,
+def attend_kernel(nd, nt, tok, gain, wq_in, wkv_in, wo_in, cosf, sins, lo_in, dy_in, w_in,
                   h1_out, xn2_out, gfull, lse_out,
-                  xn1_out, wq_out, wo_out, wkv_out, kv_out, q_out, o_out,
+                  xn1_out, wq_out, wo_out, wkv_out, kv_out, q_out, o_out, dy_all, w_all,
                   xn1, wq, wo, wkv, kvs, qs, os_, pback, precv,
                   lsem, gs, gr, vx, vy, vxf, vyf, vr, qx, qy, qxf, qyf, qr, ox, oy, oxf, oyf, orr,
-                  qlr, qll, qlv, olr, oll, olv, klr, kll, klv, klc, klcr, cs, cr, outs):
+                  qlr, qll, qlv, olr, oll, olv, klr, kll, klv, klc, klcr, cs, cr, outs,
+                  ylr, yll, ylv, ylc, mx, my, mxf, myf, mr, fsem):
     at = Place(nd, nt)
     nz = at.nz
     R, D = tok.shape
@@ -594,6 +608,21 @@
 
     lkv = Line(at, kv_view, klr, kll, klv, kv_across)
 
+    for_mlp = [pltpu.make_async_copy(dy_in, dy_all.at[rows(at.t)], fsem.at[0]),
+               pltpu.make_async_copy(w_in.at[0], w_all.at[0, :, drows(at.dp)], fsem.at[1]),
+               pltpu.make_async_copy(w_in.at[1], w_all.at[1, :, drows(at.dp)], fsem.at[2])]
+    for cp in for_mlp:
+        cp.start()
+    gw = [Gather(at, w_in.at[p], lambda o, p=p: w_all.at[p, :, drows(o)], mx.at[p], my.at[p], mxf.at[p], myf.at[p], mr.at[p], p)
+          for p in range(2)]
+
+    def dy_view(o):
+        return dy_all.at[rows(2 * o + at.c)]
+
+    def dy_across(o):
+        return remote(dy_view(o), dy_view(o), ylc.at[o], ylv.at[1, o], at.dp, at.sibling())
+
+    ldy = Line(at, dy_view, ylr, yll, ylv.at[0], dy_across)
     for g in gkv:
         g.start()
     loads[1].wait()
@@ -641,6 +670,8 @@
     for s in range(1, nz):
         lo.step(s)
         go(s).start()
+    for_mlp[0].wait()
+    ldy.start()
     for o in range(nz):
         kv_across(o).wait_recv()
 
@@ -680,6 +711,9 @@
 
     lse_out[...] = jnp.zeros_like(lse_out)
     lax.fori_loop(0, nz, pair, 0)
+    for g in gw:
+        g.start()
+    ldy.step(1)
     keep = [
         pltpu.make_async_copy(xn1, xn1_out, outs.at[0]),
         pltpu.make_async_copy(wq, wq_out, outs.at[1]),
@@ -709,6 +743,19 @@
         xn2_out[:, cols] = v
 
     scaled(h1_out[...], 1, put_xn2)
+    for g in gw:
+        g.forward()
+    for s in range(2, nz):
+        ldy.step(s)
+    for g in gw:
+        g.finish()
+    for o in range(nz):
+        dy_across(o).wait_recv()
+    for cp in for_mlp[1:]:
+        cp.wait()
+    for g in gw:
+        g.drain()
+    ldy.drain()
 
     for s in range(1, nd):
         gain_copy(s).wait_send()
@@ -730,7 +777,7 @@
         cp.wait()
 
 
-def attend(nd, nt, tok, gain, wq, wkv, wo, cosf, sins, lo):
+def attend(nd, nt, tok, gain, wq, wkv, wo, cosf, sins, lo, dy, w):
     R, D = tok.shape
     Dd, HC = wq.shape
     S = R * nt
@@ -741,19 +788,21 @@
     shapes = [((R, D), F32), ((R, D), LOW), ((nd, 8, Dd), F32), ((2 * R, 128), F32),
               ((2 * R, D), LOW), ((nz, D, HC), LOW), ((nd, nz * HC, Dd), LOW), ((D, 2 * HD), LOW), ((S, 2 * HD), LOW),
               ((2 * R, nz * HC), LOW), ((2 * R, nz * HC), LOW)]
+    gathered = [((S, D), LOW), ((2, w.shape[1], D), LOW)]
     yg = lambda n: [dma(n), dma(n, ny - 1), dma(n, ny - 1), dma(n, ny - 1), dma(n, nd)]
     return pl.pallas_call(
         functools.partial(attend_kernel, nd, nt),
-        out_shape=tuple(jax.ShapeDtypeStruct(*s) for s in shapes),
-        in_specs=[vm, vm, hbm, hbm, hbm, vm, vm, vm],
-        out_specs=(vm, vm, vm, vm) + (hbm,) * 7,
+        out_shape=tuple(jax.ShapeDtypeStruct(*s) for s in shapes + gathered),
+        in_specs=[vm, vm, hbm, hbm, hbm, vm, vm, vm, hbm, hbm],
+        out_specs=(vm, vm, vm, vm) + (hbm,) * 9,
         scratch_shapes=[pltpu.VMEM(*s) for s in shapes[4:]] + [pltpu.VMEM((R, D), LOW), pltpu.VMEM((R, D), LOW)]
         + [dma(3), dma(nd - 1), dma(nd - 1)] + yg(2) + yg(nz) + yg(nz)
-        + [dma(nz)] * 3 + [dma(nz)] * 3 + [dma(nz)] * 5 + [dma(2), dma(2), dma(7)],
+        + [dma(nz)] * 3 + [dma(nz)] * 3 + [dma(nz)] * 5 + [dma(2), dma(2), dma(7)]
+        + [dma(nz), dma(nz), dma(2, nz), dma(nz)] + yg(2) + [dma(3)],
         compiler_params=pltpu.CompilerParams(collective_id=2, has_side_effects=True, vmem_limit_bytes=63 << 20),
         cost_estimate=pl.CostEstimate(flops=20 << 30, bytes_accessed=40 << 20, transcendentals=8 * 512 * 2048),
         name="attend",
-    )(tok, gain, wq, wkv, wo, cosf, sins, lo)
+    )(tok, gain, wq, wkv, wo, cosf, sins, lo, dy, w)
 
 
 class Scatter:
@@ -835,13 +884,13 @@
 
 def grads_kernel(nd, nt, dy, tok, gfull, cosf, sins, lo_row, lse, later,
                  h1_in, dxn2_in, xn1_in, wq_in, wo_in, wkv_in, kv_in, q_in, o_in,
-                 mine_g, land_g, mine_u, land_u, mine_d, land_d, mine_e, land_e,
+                 mine_g, land_g, mine_u, land_u, down_in,
                  tgrad, gq_out, go_out, gkv_out, gg_out, norm_out, keep_g, keep_u, keep_d, keep_e, got_g, got_u, got_d, got_e,
                  xn1, wq, wo, wkv, kvs, qs, os_, dos, dh1b, dxn1, lset, dkv, dq,
                  bg, bu, bd, be, lg, lu, ld, le, tg, tu, td, te,
-                 ql, ql2, ol, ol2, qz, oz, qlz, olz, kvb, kland, kz, xrecv, wl, wd2, w2, w2l, wfin, gl, gpart, u2, u2l, gfin, share, norms, normd,
+                 ql, ql2, ol, ol2, qz, oz, qlz, olz, kvb, kland, kz, xrecv, wl, wcl, wd2, w2, w2l, wfin, gl, gpart, u2, u2l, gfin, share, norms, normd,
                  lsem, xsem, fs, fr, qss, qsr, qss2, qsr2, oss, osr, oss2, osr2, qzs, qzr, ozs, ozr,
-                 ks, kr, kzs, kzr, ws, wr, w2s, w2r, w3s, w3r, us, ur, u2s, u2r, u3s, u3r, ns, nr, n2s, n2r, outs):
+                 ks, kr, kzs, kzr, ws, wr, wcs, wcr, w2s, w2r, w3s, w3r, us, ur, u2s, u2r, u3s, u3r, ns, nr, n2s, n2r, outs, hs, hr):
     at = Place(nd, nt)
     nz, nx, ny = at.nz, at.nx, at.ny
     R, D = tok.shape
@@ -857,13 +906,28 @@
     mine, theirs = rows(at.c), rows(1 - at.c)
     scale = 1.0 / math.sqrt(HD)
 
-    pieces = [(bg, mine_g), (bu, mine_u), (bd, mine_d), (be, mine_e), (tg, land_g), (tu, land_u), (td, land_d), (te, land_e),
+    Fh = bd.shape[1]
+    pieces = [(bg, mine_g), (bu, mine_u), (tg, land_g), (tu, land_u),
               (wo, wo_in), (os_, o_in), (qs, q_in), (kvs, kv_in), (xn1, xn1_in), (wq, wq_in), (wkv, wkv_in),
-              (dxn1.at[pl.ds(0, R)], h1_in), (dxn1.at[pl.ds(R, R)], dxn2_in)]
+              (dxn1.at[pl.ds(0, R)], h1_in), (xrecv, dxn2_in)]
+    down = lambda n, o: down_in.at[pl.ds(n * Fh, Fh), drows(o)]
+    pieces += [(bd.at[xx], down(0, at.y * nx + xx)) for xx in range(nx)]
+    pieces += [(be.at[yy], down(1, yy * nx + at.x)) for yy in range(ny)]
     loads = [pltpu.make_async_copy(src, dst, lsem.at[i]) for i, (dst, src) in enumerate(pieces)]
-    for cp in loads:
+    for cp in loads[11:13] + loads[:11] + loads[13:]:
         cp.start()
     greet_all(at)
+
+    down_hops = []
+    for s in range(1, ny):
+        for xx in range(nx):
+            slot = (s - 1) * nx + xx
+            o = lax.rem(at.y + s, ny) * nx + xx
+            down_hops.append(remote(down(0, o), td.at[slot], hs.at[0, slot], hr.at[0, slot], at.y_peer(s), at.t))
+    for yy in range(ny):
+        down_hops.append(remote(down(1, yy * nx + 1 - at.x), te.at[yy], hs.at[1, yy], hr.at[1, yy], at.x_peer(), at.t))
+    for cp in down_hops:
+        cp.start()
 
     def rms_back(v_of, e_of, row, put):
         chunks = [pl.ds(o * Dd, Dd) for o in range(nd)]
@@ -887,16 +951,182 @@
         tgrad[:, cols] = total
         dh1b[mine, cols] = total.astype(LOW)
 
-    loads[15].wait()
-    loads[16].wait()
-    rms_back(lambda cols: dxn1[pl.ds(0, R), cols], lambda cols: dxn1[pl.ds(R, R), cols], 1, put_dh1)
+    loads[11].wait()
+    loads[12].wait()
+    rms_back(lambda cols: dxn1[pl.ds(0, R), cols], lambda cols: xrecv[:, cols].astype(F32), 1, put_dh1)
     swap_dh1 = remote(dh1b.at[mine], dh1b.at[mine], xsem.at[0], xsem.at[1], at.dp, at.sibling())
     swap_dh1.start()
 
+    for i in range(4, 11):
+        loads[i].wait()
+    swap_dh1.wait_recv()
+    def do_pair(j, _):
+        acc = dot_nt(dh1b[:, pl.ds(0, Dd)], wo[0, hcols(j), :])
+        for o in range(1, nd):
+            acc = acc + dot_nt(dh1b[:, pl.ds(o * Dd, Dd)], wo[o, hcols(j), :])
+        dos[:, hcols(j)] = acc.astype(LOW)
+        return 0
+
+    lax.fori_loop(0, nz, do_pair, 0)
+
+    def kind_of(k):
+        return k % 2 if isinstance(k, int) else lax.rem(k, 2)
+
+    def so(k):
+        j = far_first(k, at.z, nz)
+        return Scatter(at, kind_of(k), lambda o: wo.at[o, hcols(j)], lambda i: ol.at[k, i], lambda i: ol2.at[k, i],
+                       oss.at[k], osr.at[k], oss2.at[k], osr2.at[k])
+
+    def sq(k):
+        j = far_first(k, at.z, nz)
+        return Scatter(at, kind_of(k), lambda o: wq.at[j, drows(o)], lambda i: ql.at[k, i], lambda i: ql2.at[k, i],
+                       qss.at[k], qsr.at[k], qss2.at[k], qsr2.at[k])
+
+    def wo_unit(k, _):
+        j = far_first(k, at.z, nz)
+
+        def part(o, _):
+            wo[o, hcols(j), :] = dot_tn(os_[:, hcols(j)], dh1b[:, drows(o)]).astype(LOW)
+            return 0
+
+        lax.fori_loop(0, nd, part, 0)
+        so(k).either("start")
+        return 0
+
+    lax.fori_loop(0, nz, wo_unit, 0)
+
+    def zpush(k, buf, land, ss, rs):
+        j = far_first(k, at.z, nz)
+        return remote(buf.at[k], land.at[at.z], ss.at[k], rs.at[at.z], at.dp, 2 * j + at.c)
+
+    def o_total(k):
+        def put(v):
+            oz[k] = v.astype(LOW)
+
+        so(k).either("total", put)
+        pl.when(k < nz - 1)(lambda: zpush(k, oz, olz, ozs, ozr).start())
+
+    def q_total(k):
+        def put(v):
+            qz[k] = v.astype(LOW)
+
+        sq(k).either("total", put)
+        pl.when(k < nz - 1)(lambda: zpush(k, qz, qlz, qzs, qzr).start())
+
+    lset[...] = lse[...].T
+    dkv[...] = jnp.zeros_like(dkv)
+    dxn1[...] = jnp.zeros_like(dxn1)
+    here = at.z * KT + lax.broadcasted_iota(jnp.int32, (1, KT), 1)
+    low_row = lo_row[0:1, :]
+
+    def unit(k, _):
+        j = far_first(k, at.z, nz)
+        for hh in range(NH):
+            cols = pl.ds(pl.multiple_of(j * HC + hh * HD, HD), HD)
+            hid = j * NH + hh
+            lrow = lset[pl.ds(hid, 1), :]
+            qh = qs[:, cols]
+            doh = dos[:, cols]
+            delta = jnp.sum((doh.astype(F32) * os_[:, cols].astype(F32)).T, axis=0, keepdims=True)
+            dq[...] = jnp.zeros_like(dq)
+
+            def tile(b, _):
+                kr_ = pl.ds(pl.multiple_of(b * KT, KT), KT)
+                kt = kvs[kr_, pl.ds(0, HD)]
+                vt = kvs[kr_, pl.ds(HD, HD)]
+                s = dot_nt(kt, qh)
+                place = b * KT + lax.broadcasted_iota(jnp.int32, (KT, KT), 0)
+                s = jnp.where((place >= low_row) & (place <= here), s * scale, MASKED)
+                p = jnp.exp(s - lrow)
+                dkv[kr_, pl.ds(HD, HD)] += dot_nn(p.astype(LOW), doh)
+                ds = (p * (dot_nt(vt, doh) - delta)).astype(LOW)
+                dkv[kr_, pl.ds(0, HD)] += dot_nn(ds, qh)
+                dq[...] += dot_tn(ds, kt)
+                return 0
+
+            lax.fori_loop(0, at.z + 1, tile, 0)
+            u = dq[...] * scale
+            qs[:, cols] = (u * cosf[...] - swap_halves(u) * sins[...]).astype(LOW)
+        dqp = qs[:, hcols(j)]
+
+        def back(o, _):
+            dxn1[:, drows(o)] += dot_nt(dqp, wq[j, drows(o), :])
+            wq[j, drows(o), :] = dot_tn(xn1[:, drows(o)], dqp).astype(LOW)
+            return 0
+
+        lax.fori_loop(0, nd, back, 0)
+        sq(k).either("start")
+        pl.when(k >= 1)(lambda: so(k - 1).either("middle"))
+        pl.when(k >= 2)(lambda: o_total(k - 2))
+        return 0
+
+    lax.fori_loop(0, nz, unit, 0)
+
+    dkv[:, pl.ds(0, HD)] = dkv[:, pl.ds(0, HD)] * scale
+    kvb[...] = dkv[...].astype(LOW)
+    kswap = [remote(kvb.at[rows(2 * zz + 1 - at.c)], kland.at[zz], ks.at[zz], kr.at[zz], at.dp, at.sibling()) for zz in range(nz)]
+    for cp in kswap:
+        cp.start()
+    swap_dh1.wait_send()
+    dh1b[mine, :] = dxn1[theirs, :].astype(LOW)
+    xswap = remote(dh1b.at[mine], xrecv, xsem.at[2], xsem.at[3], at.dp, at.sibling())
+    xswap.start()
+
+    def kpush(s):
+        zz = lax.rem(at.z + s, nz)
+        return remote(kvb.at[rows(2 * zz + at.c)], kz.at[s - 1], kzs.at[s - 1], kzr.at[s - 1], at.dp, 2 * zz + at.c)
+
+    k_last = jnp.int32(nz - 1)
+    so(k_last).either("middle")
+    for s in range(1, nz + 1):
+        zz = lax.rem(at.z + s, nz)
+        r = rows(2 * zz + at.c)
+        remote(kvb.at[rows(0)], kland.at[zz], ks.at[zz], kr.at[zz], at.dp, at.sibling()).wait_recv()
+        dkv[r, :] = dkv[r, :] + kland[zz].astype(F32)
+        if s < nz:
+            kvb[r, :] = dkv[r, :].astype(LOW)
+            kpush(s).start()
+
+    lax.fori_loop(0, max(nz - 2, 1), lambda k, _: (sq(k).either("middle"), 0)[1], 0)
+    if nz >= 2:
+        o_total(jnp.int32(nz - 2))
+    total = dkv[rows(at.t), :] + later[...].astype(F32)
+    for s in range(1, nz):
+        kpush(s).wait_recv()
+        total = total + kz[s - 1].astype(F32)
+    dk = total[:, :HD]
+    dk = dk * cosf[mine, :] - swap_halves(dk) * sins[mine, :]
+    dkvp = jnp.concatenate([dk, total[:, HD:]], axis=1).astype(LOW)
+
+
+    slices = lambda t: pl.ds(pl.multiple_of(t * Ds, Ds), Ds)
+
+    def wswap(zz):
+        return remote(wd2.at[slices(2 * zz + 1 - at.c)], wcl.at[zz], wcs.at[zz], wcr.at[zz], at.dp, at.sibling())
+
+    def wpush(s):
+        zz = lax.rem(at.z + s, nz)
+        return remote(wd2.at[slices(2 * zz + at.c)], wl.at[s - 1], ws.at[s - 1], wr.at[s - 1], at.dp, 2 * zz + at.c)
+
+    def upush(s):
+        tt = lax.rem(at.t + s, nt)
+        return remote(gpart.at[:, slices(tt)], gl.at[at.t], us.at[s - 1], ur.at[at.t], at.dp, tt)
+
+    for o in range(nd):
+        wd2[pl.ds(o * Dd, Dd), :] = dot_tn(xn1[mine, pl.ds(o * Dd, Dd)], dkvp).astype(LOW)
+    for zz in range(nz):
+        wswap(zz).start()
+    lax.fori_loop(max(nz - 2, 1), nz, lambda k, _: (sq(k).either("middle"), 0)[1], 0)
     big = []
     for n, (buf, got, second) in enumerate([(bg, tg, lg), (bu, tu, lu), (bd, td, ld), (be, te, le)]):
-        loads[n].wait()
-        loads[4 + n].wait()
+        if n < 2:
+            loads[n].wait()
+            loads[2 + n].wait()
+        elif n == 2:
+            for cp in loads[13:]:
+                cp.wait()
+            for cp in down_hops:
+                cp.wait_recv()
         if n % 2 == 0:
             keep, keep_slots = at.x, [(s - 1) * nx + at.x for s in range(1, ny)]
             away = [(1 - at.x, [(s - 1) * nx + 1 - at.x for s in range(1, ny)], at.x_peer())]
@@ -917,137 +1147,14 @@
         buf[keep] = total.astype(LOW)
         big.append((buf, keep, second, copies))
 
-    for i in range(8, 15):
-        loads[i].wait()
-    swap_dh1.wait_recv()
-    def do_pair(j, _):
-        acc = dot_nt(dh1b[:, pl.ds(0, Dd)], wo[0, hcols(j), :])
-        for o in range(1, nd):
-            acc = acc + dot_nt(dh1b[:, pl.ds(o * Dd, Dd)], wo[o, hcols(j), :])
-        dos[:, hcols(j)] = acc.astype(LOW)
-        return 0
-
-    lax.fori_loop(0, nz, do_pair, 0)
-
-    def kind_of(k):
-        return k % 2 if isinstance(k, int) else lax.rem(k, 2)
-
-    def so(k):
-        j = far_first(k, at.z, nz)
-        return Scatter(at, kind_of(k), lambda o: wo.at[o, hcols(j)], lambda i: ol.at[k, i], lambda i: ol2.at[k, i],
-                       oss.at[k], osr.at[k], oss2.at[k], osr2.at[k])
-
-    def sq(k):
-        j = far_first(k, at.z, nz)
-        return Scatter(at, kind_of(k), lambda o: wq.at[j, drows(o)], lambda i: ql.at[k, i], lambda i: ql2.at[k, i],
-                       qss.at[k], qsr.at[k], qss2.at[k], qsr2.at[k])
-
-    def wo_unit(k, _):
-        j = far_first(k, at.z, nz)
-
-        def part(o, _):
-            wo[o, hcols(j), :] = dot_tn(os_[:, hcols(j)], dh1b[:, drows(o)]).astype(LOW)
-            return 0
-
-        lax.fori_loop(0, nd, part, 0)
-        so(k).either("start")
-        return 0
-
-    lax.fori_loop(0, nz, wo_unit, 0)
-
-    lset[...] = lse[...].T
-    dkv[...] = jnp.zeros_like(dkv)
-    dxn1[...] = jnp.zeros_like(dxn1)
-    here = at.z * KT + lax.broadcasted_iota(jnp.int32, (1, KT), 1)
-    low_row = lo_row[0:1, :]
-
-    def unit(k, _):
-        j = far_first(k, at.z, nz)
-        for hh in range(NH):
-            cols = pl.ds(pl.multiple_of(j * HC + hh * HD, HD), HD)
-            hid = j * NH + hh
-            lrow = lset[pl.ds(hid, 1), :]
-            qh = qs[:, cols]
-            doh = dos[:, cols]
-            delta = jnp.sum((doh.astype(F32) * os_[:, cols].astype(F32)).T, axis=0, keepdims=True)
-            dq[...] = jnp.zeros_like(dq)
-
-            def tile(b, _):
-                kr_ = pl.ds(pl.multiple_of(b * KT, KT), KT)
-                kt = kvs[kr_, pl.ds(0, HD)]
-                vt = kvs[kr_, pl.ds(HD, HD)]
-                s = dot_nt(kt, qh)
-                place = b * KT + lax.broadcasted_iota(jnp.int32, (KT, KT), 0)
-                s = jnp.where((place >= low_row) & (place <= here), s * scale, MASKED)
-                p = jnp.exp(s - lrow)
-                dkv[kr_, pl.ds(HD, HD)] += dot_nn(p.astype(LOW), doh)
-                ds = (p * (dot_nt(vt, doh) - delta)).astype(LOW)
-                dkv[kr_, pl.ds(0, HD)] += dot_nn(ds, qh)
-                dq[...] += dot_tn(ds, kt)
-                return 0
-
-            lax.fori_loop(0, at.z + 1, tile, 0)
-            u = dq[...] * scale
-            qs[:, cols] = (u * cosf[...] - swap_halves(u) * sins[...]).astype(LOW)
-        dqp = qs[:, hcols(j)]
-
-        def back(o, _):
-            dxn1[:, drows(o)] += dot_nt(dqp, wq[j, drows(o), :])
-            wq[j, drows(o), :] = dot_tn(xn1[:, drows(o)], dqp).astype(LOW)
-            return 0
-
-        lax.fori_loop(0, nd, back, 0)
-        sq(k).either("start")
-        so(k).either("middle")
-        return 0
-
-    lax.fori_loop(0, nz, unit, 0)
-
-    dkv[:, pl.ds(0, HD)] = dkv[:, pl.ds(0, HD)] * scale
-    kvb[...] = dkv[...].astype(LOW)
-    kswap = [remote(kvb.at[rows(2 * zz + 1 - at.c)], kland.at[zz], ks.at[zz], kr.at[zz], at.dp, at.sibling()) for zz in range(nz)]
-    for cp in kswap:
-        cp.start()
-    swap_dh1.wait_send()
-    dh1b[mine, :] = dxn1[theirs, :].astype(LOW)
-    xswap = remote(dh1b.at[mine], xrecv, xsem.at[2], xsem.at[3], at.dp, at.sibling())
-    xswap.start()
-
-    def kpush(s):
-        zz = lax.rem(at.z + s, nz)
-        return remote(kvb.at[rows(2 * zz + at.c)], kz.at[s - 1], kzs.at[s - 1], kzr.at[s - 1], at.dp, 2 * zz + at.c)
-
     for s in range(1, nz + 1):
         zz = lax.rem(at.z + s, nz)
-        r = rows(2 * zz + at.c)
-        remote(kvb.at[rows(0)], kland.at[zz], ks.at[zz], kr.at[zz], at.dp, at.sibling()).wait_recv()
-        dkv[r, :] = dkv[r, :] + kland[zz].astype(F32)
+        r = slices(2 * zz + at.c)
+        remote(wd2.at[slices(0)], wcl.at[zz], wcs.at[zz], wcr.at[zz], at.dp, at.sibling()).wait_recv()
+        wd2[r, :] = (wd2[r, :].astype(F32) + wcl[zz].astype(F32)).astype(LOW)
         if s < nz:
-            kvb[r, :] = dkv[r, :].astype(LOW)
-            kpush(s).start()
-
-    lax.fori_loop(0, nz, lambda k, _: (sq(k).either("middle"), 0)[1], 0)
-    total = dkv[rows(at.t), :] + later[...].astype(F32)
-    for s in range(1, nz):
-        kpush(s).wait_recv()
-        total = total + kz[s - 1].astype(F32)
-    dk = total[:, :HD]
-    dk = dk * cosf[mine, :] - swap_halves(dk) * sins[mine, :]
-    dkvp = jnp.concatenate([dk, total[:, HD:]], axis=1).astype(LOW)
-
-
-    def wpush(s):
-        tt = lax.rem(at.t + s, nt)
-        return remote(wd2.at[pl.ds(pl.multiple_of(tt * Ds, Ds), Ds)], wl.at[at.t], ws.at[s - 1], wr.at[at.t], at.dp, tt)
-
-    def upush(s):
-        tt = lax.rem(at.t + s, nt)
-        return remote(gpart.at[:, pl.ds(pl.multiple_of(tt * Ds, Ds), Ds)], gl.at[at.t], us.at[s - 1], ur.at[at.t], at.dp, tt)
-
-    for o in range(nd):
-        wd2[pl.ds(o * Dd, Dd), :] = dot_tn(xn1[mine, pl.ds(o * Dd, Dd)], dkvp).astype(LOW)
-    for s in range(1, nt):
-        wpush(s).start()
+            wpush(s).start()
+    o_total(k_last)
 
     xswap.wait_recv()
     for o in range(nd):
@@ -1061,39 +1168,19 @@
     for s in range(1, nt):
         upush(s).start()
 
-    def zpush(k, buf, land, ss, rs):
-        j = far_first(k, at.z, nz)
-        return remote(buf.at[k], land.at[at.z], ss.at[k], rs.at[at.z], at.dp, 2 * j + at.c)
-
-    def o_total(k, _):
-        def put(v):
-            oz[k] = v.astype(LOW)
-
-        so(k).either("total", put)
-        pl.when(k < nz - 1)(lambda: zpush(k, oz, olz, ozs, ozr).start())
-        return 0
-
-    def q_total(k, _):
-        def put(v):
-            qz[k] = v.astype(LOW)
-
-        sq(k).either("total", put)
-        pl.when(k < nz - 1)(lambda: zpush(k, qz, qlz, qzs, qzr).start())
-        return 0
-
-    lax.fori_loop(0, nz, o_total, 0)
+    lax.fori_loop(0, max(nz - 2, 1), lambda k, _: (q_total(k), 0)[1], 0)
 
     per = nt // nd
-    wl[at.t] = wd2[pl.ds(pl.multiple_of(at.t * Ds, Ds), Ds), :]
-    gl[at.t] = gpart[:, pl.ds(pl.multiple_of(at.t * Ds, Ds), Ds)]
+    gl[at.t] = gpart[:, slices(at.t)]
+    wsum = wd2[slices(at.t), :].astype(F32)
+    for s in range(1, nz):
+        wpush(s).wait_recv()
+        wsum = wsum + wl[s - 1].astype(F32)
     for s in range(1, nt):
         o = lax.rem(at.t + s, nt)
-        remote(wd2.at[pl.ds(0, Ds)], wl.at[o], ws.at[s - 1], wr.at[o], at.dp, o).wait_recv()
         remote(gpart.at[:, pl.ds(0, Ds)], gl.at[o], us.at[s - 1], ur.at[o], at.dp, o).wait_recv()
-    wsum = wl[0].astype(F32)
     usum = gl[0]
     for o in range(1, nt):
-        wsum = wsum + wl[o].astype(F32)
         usum = usum + gl[o]
     owner = at.t // per
     is_owner = at.dp == owner
@@ -1104,17 +1191,19 @@
     give_w = remote(w2, w2l.at[at.dp], w2s.at[0], w2r.at[at.dp], to, at.t)
     give_u = remote(u2, u2l.at[at.dp], u2s.at[0], u2r.at[at.dp], to, at.t)
 
-    def spread(s):
-        tt = lax.rem(at.t + s, nt)
-        return [remote(wfin.at[slot], wfin.at[slot], w3s.at[s - 1], w3r.at[slot], at.dp, tt),
-                remote(gfin.at[slot], gfin.at[slot], u3s.at[s - 1], u3r.at[slot], at.dp, tt)]
+    def spread(q, i, t):
+        return [remote(wfin.at[q], wfin.at[q], w3s.at[q, i], w3r.at[q], at.dp, t),
+                remote(gfin.at[q], gfin.at[q], u3s.at[q, i], u3r.at[q], at.dp, t)]
+
+    def spread_along(s):
+        return spread(slot, s, 2 * lax.rem(at.z + s, nz) + at.c)
 
     @pl.when(jnp.logical_not(is_owner))
     def _():
         give_w.start()
         give_u.start()
 
-    lax.fori_loop(0, nz, q_total, 0)
+    lax.fori_loop(max(nz - 2, 1), nz, lambda k, _: (q_total(k), 0)[1], 0)
 
     def square(v):
         return jnp.sum(v * v, axis=(0, 1), keepdims=True)
@@ -1138,8 +1227,8 @@
         gfin[slot] = utot
         shared = square(wtot.astype(LOW).astype(F32)) + square(utot)
         share[...] = jnp.broadcast_to(shared, share.shape)
-        for s in range(1, nt):
-            for cp in spread(s):
+        for s in range(1, nz):
+            for cp in spread_along(s):
                 cp.start()
 
     squares = jnp.zeros((1, 1), F32)
@@ -1175,16 +1264,6 @@
 
     for s in range(1, nt):
         npush(s).start()
-    for q in range(per):
-        t_from = at.dp * per + q
-
-        @pl.when(at.t != t_from)
-        def _(q=q, t_from=t_from):
-            remote(wfin.at[q], wfin.at[q], w3s.at[0], w3r.at[q], at.dp, at.sibling()).wait_recv()
-            remote(gfin.at[q], gfin.at[q], u3s.at[0], u3r.at[q], at.dp, at.sibling()).wait_recv()
-
-        gkv_out[pl.ds(q * Ds, Ds), :] = wfin[q].astype(F32)
-        gg_out[:, pl.ds(q * Ds, Ds)] = gfin[q]
     for s in range(1, nt):
         o = lax.rem(at.t + s, nt)
         remote(norms.at[o], norms.at[o], ns.at[s - 1], nr.at[o], at.dp, o).wait_recv()
@@ -1202,8 +1281,33 @@
         group = group + normd[o]
     norm_out[...] = jnp.sqrt(group)
 
+    for q in range(per):
+        t_from = at.dp * per + q
+        same = at.c == lax.rem(t_from, 2)
+
+        def slice_came(q=q):
+            for cp in spread(q, 0, at.sibling()):
+                cp.wait_recv()
+
+        pl.when(at.t != t_from)(slice_came)
+
+        @pl.when(same)
+        def _(q=q):
+            for cp in spread(q, 0, at.sibling()):
+                cp.start()
+
+        gkv_out[pl.ds(q * Ds, Ds), :] = wfin[q].astype(F32)
+        gg_out[:, pl.ds(q * Ds, Ds)] = gfin[q]
+
+        @pl.when(same)
+        def _(q=q):
+            for cp in spread(q, 0, at.sibling()):
+                cp.wait_send()
+
     for cp in out_copies:
         cp.wait()
+    for cp in down_hops:
+        cp.wait_send()
     xswap.wait_send()
     for _, _, _, copies in big:
         for cp in copies:
@@ -1212,8 +1316,11 @@
         cp.wait_send()
     for s in range(1, nz):
         kpush(s).wait_send()
+    for zz in range(nz):
+        wswap(zz).wait_send()
+    for s in range(1, nz):
+        wpush(s).wait_send()
     for s in range(1, nt):
-        wpush(s).wait_send()
         upush(s).wait_send()
         npush(s).wait_send()
     for s in range(1, nd):
@@ -1239,8 +1346,8 @@
 
     @pl.when(is_owner)
     def _():
-        for s in range(1, nt):
-            for cp in spread(s):
+        for s in range(1, nz):
+            for cp in spread_along(s):
                 cp.wait_send()
 
 
@@ -1249,7 +1356,7 @@
     nz, ny = nt // 2, nd // 2
     h1, dxn2, xn1, wq, wo, wkv, kv, q, o = big_in
     Dd, HC = wo.shape[2], wq.shape[2]
-    F = pieces[0].shape[2]
+    F = pieces[0].shape[1]
     Fh = F // 2
     S = R * nt
     Ds = D // nt
@@ -1262,30 +1369,30 @@
     b = lambda *s: pltpu.VMEM(s, LOW)
     f = lambda *s: pltpu.VMEM(s, F32)
     shapes = [(R, D), (Dd, HC), (HC, Dd), (Dd, W2), (8, Dd), (8, 128)]
-    lows = [(Dd, F), (Dd, F), (Fh, Dd), (Fh, Dd), (1, Dd, F), (hops, Dd, F), (1, Fh, Dd), (hops, Fh, Dd)]
+    lows = [(F, Dd), (F, Dd), (Fh, Dd), (Fh, Dd), (1, F, Dd), (hops, F, Dd), (1, Fh, Dd), (hops, Fh, Dd)]
     return pl.pallas_call(
         functools.partial(grads_kernel, nd, nt),
         out_shape=tuple([jax.ShapeDtypeStruct(s, F32) for s in shapes] + [jax.ShapeDtypeStruct(s, LOW) for s in lows]),
-        in_specs=[vm] * 8 + [hbm] * 17,
+        in_specs=[vm] * 8 + [hbm] * 14,
         out_specs=(vm,) * 6 + (hbm,) * 8,
         scratch_shapes=[
             b(2 * R, D), b(nz, D, HC), b(nd, nz * HC, Dd), b(D, W2), b(S, W2), b(2 * R, nz * HC), b(2 * R, nz * HC), b(2 * R, nz * HC),
             b(2 * R, D), f(2 * R, D), f(128, 2 * R), f(S, W2), f(2 * R, HD),
-            b(2, Dd, F), b(ny, Dd, F), b(2, Fh, Dd), b(ny, Fh, Dd),
-            b(1, Dd, F), b(hops, Dd, F), b(1, Fh, Dd), b(hops, Fh, Dd),
-            b(2 * (ny - 1), Dd, F), b(ny, Dd, F), b(2 * (ny - 1), Fh, Dd), b(ny, Fh, Dd),
+            b(2, F, Dd), b(ny, F, Dd), b(2, Fh, Dd), b(ny, Fh, Dd),
+            b(1, F, Dd), b(hops, F, Dd), b(1, Fh, Dd), b(hops, Fh, Dd),
+            b(2 * (ny - 1), F, Dd), b(ny, F, Dd), b(2 * (ny - 1), Fh, Dd), b(ny, Fh, Dd),
             b(nz, slots, Dd, HC), b(nz, hops, Dd, HC), b(nz, slots, HC, Dd), b(nz, hops, HC, Dd),
             b(nz, Dd, HC), b(nz, HC, Dd), b(nz, Dd, HC), b(nz, HC, Dd),
             b(S, W2), b(nz, R, W2), b(nz, R, W2), b(R, D),
-            b(nt, Ds, W2), b(D, W2), b(Ds, W2), b(nd, Ds, W2), b(nt // nd, Ds, W2),
+            b(nz, Ds, W2), b(nz, Ds, W2), b(D, W2), b(Ds, W2), b(nd, Ds, W2), b(nt // nd, Ds, W2),
             f(nt, 8, Ds), f(8, D), f(8, Ds), f(nd, 8, Ds), f(nt // nd, 8, Ds), f(8, 128), f(nt, 8, 128), f(nd, 8, 128),
-            dma(17), dma(4), dma(4, hops), dma(4, hops),
+            dma(13 + 2 + ny), dma(4), dma(4, hops), dma(4, hops),
             dma(nz, slots), dma(nz, slots), dma(nz, hops), dma(nz, hops), dma(nz, slots), dma(nz, slots), dma(nz, hops), dma(nz, hops),
             dma(nz), dma(nz), dma(nz), dma(nz),
             dma(nz), dma(nz), dma(nz), dma(nz),
-            dma(nt), dma(nt), dma(1), dma(nd), dma(nt), dma(nt // nd),
-            dma(nt), dma(nt), dma(1), dma(nd), dma(nt), dma(nt // nd),
-            dma(nt), dma(nt), dma(nd), dma(nd), dma(8),
+            dma(nz), dma(nz), dma(nz), dma(nz), dma(1), dma(nd), dma(nt // nd, nz), dma(nt // nd),
+            dma(nt), dma(nt), dma(1), dma(nd), dma(nt // nd, nz), dma(nt // nd),
+            dma(nt), dma(nt), dma(nd), dma(nd), dma(8), dma(2, slots), dma(2, slots),
         ],
         compiler_params=pltpu.CompilerParams(collective_id=3, has_side_effects=True, vmem_limit_bytes=63 << 20),
         cost_estimate=pl.CostEstimate(flops=30 << 30, bytes_accessed=40 << 20, transcendentals=8 * 512 * 2048),
@@ -1327,7 +1434,9 @@
     gains_average,
 ):
     masters = (query_weight, keyvalue_weight, output_weight, gateup_weight, down_weight, norm_gains)
-    low_query, low_kv, low_output, low_gateup, low_down, low_gains = (w.astype(LOW) for w in masters)
+    low_query, low_kv, low_output, _, _, low_gains = (w.astype(LOW) for w in masters)
+    low_gateup = jnp.swapaxes(gateup_weight, 1, 2).astype(LOW)
+    low_down = down_weight.astype(LOW)
     nd, nt = lax.axis_size("dp"), lax.axis_size("tensor")
     row_count = tokens.shape[0]
     pair_rows = 2 * row_count
@@ -1347,12 +1456,14 @@
     sine_full = jnp.concatenate([-sine, sine], axis=1)
     gain_rows = jnp.pad(low_gains.astype(F32), ((0, 6), (0, 0)))
 
-    grad_rows = lax.all_gather(cotangent, "tensor", axis=0, tiled=True)
-    hidden_one, normed_two, gains_all, lse, normed_one, all_query, all_output, all_kv, kv_rows, queries, attended = attend(
-        nd, nt, tokens, gain_rows, low_query, low_kv, low_output, cosine_full, sine_full, first[:, None]
+    hidden_one, normed_two, gains_all, lse, normed_one, all_query, all_output, all_kv, kv_rows, queries, attended, grad_rows, gate_up = attend(
+        nd, nt, tokens, gain_rows, low_query, low_kv, low_output, cosine_full, sine_full, first[:, None],
+        cotangent, low_gateup
     )
-    grad_normed_two, *pieces, mlp_rows = mlp(nd, nt, normed_two, grad_rows, low_gateup, low_down)
-    mixed = hidden_one + lax.psum_scatter(mlp_rows, "tensor", scatter_dimension=0, tiled=True).astype(F32)
+    grad_normed_two, *pieces, mlp_rows = mlp(nd, nt, normed_two, grad_rows, gate_up, low_down)
+    cores = [list(range(core, nt, 2)) for core in range(2)]
+    mlp_own = lax.psum_scatter(mlp_rows, "tensor", scatter_dimension=0, axis_index_groups=cores, tiled=False)
+    mixed = hidden_one + mlp_own.astype(F32)
     tokens_grad, own_query, own_output, grad_keyvalue, gains_sum, norm_tile, *halves = grads(
         nd,
         nt,
@@ -1361,7 +1472,7 @@
         pieces,
     )
     whole = [kept.astype(F32) + jnp.sum(got.astype(F32), axis=0) for kept, got in zip(halves[:4], halves[4:])]
-    own_gateup = jnp.stack(whole[:2])
+    own_gateup = jnp.swapaxes(jnp.stack(whole[:2]), 1, 2)
     own_down = jnp.concatenate(whole[2:], axis=0)
     grad_gains = gains_sum[:2]
     grad_norm = norm_tile[0, 0]

time: 657 us -> 568 us (0.86)
  Pallas kernels: 556 us -> 499 us
  local copies, waits for them, and re-layouts: 35.2 us -> 11.5 us
  other arithmetic: 42.9 us -> 34.9 us
    pallas_call x1, Pallas kernels: 211 us -> 167 us  [grads(): pl.pallas_call(functools.partial(grads_kernel, nd, nt), out_shape=tuple([...]
    unnamed x83 -> x77, local copies, waits for them, and re-layouts: 29.9 us -> 8.79 us
    pallas_call x1, Pallas kernels: 194 us -> 182 us  [mlp(): pl.pallas_call(functools.partial(mlp_kernel, nd, nt), out_shape=(shape(R,...]
  transfers between devices with their start and end apart: 2 -> 1, of which waited for: 0 -> 0; matrix products, arithmetic and copies ran while one was open for 11% -> 4% of each run, Pallas kernels for 56% -> 30%
where the time goes in v3:
time: 568 us; the launch traced here: 561 us
  Pallas kernels  499 us (88%)
  other arithmetic  34.9 us (6%)
  between operations  15.5 us (3%)
  local copies, waits for them, and re-layouts  11.5 us (2%)
    pallas_call x1, Pallas kernels, mlp(): pl.pallas_call(functools.partial(mlp_kernel, nd, nt), out_shape=(shape(R,...  182 us
    pallas_call x1, Pallas kernels, grads(): pl.pallas_call(functools.partial(grads_kernel, nd, nt), out_shape=tuple([...  167 us
    pallas_call x1, Pallas kernels, attend(): pl.pallas_call(functools.partial(attend_kernel, nd, nt), out_shape=tuple(...  150 us
  transfers between devices with their start and end apart: 1, of which 0 were waited for; matrix products, arithmetic and copies ran while one was open for 4% of the time, Pallas kernels for 30%

profile of v3, /device:TPU:0, one launch (start us, length us, event | category | flops | bytes accessed | tf_op | source)
XLA Modules:
  0.0 560.9 jit_solution(7432691617767816459)
XLA Ops:
  7.3 0.8 reduce-window.4
  8.1 0.7 fusion.4
  9.0 0.9 copy.57.lo_in
  9.8 3.2 convert_bitcast_fusion.w_in
  13.1 0.7 convert_element_type.77.wq_in
  13.8 0.7 convert_element_type.78.wkv_in
  14.5 0.7 convert_element_type.79.wo_in
  15.9 0.9 convert_element_type.84.w_in
  16.8 1.0 fusion.3
  17.8 1.0 pad_maximum_fusion
  18.8 150.0 %attend.1 = (f32[256,2048]{1,0:T(8,128)}, bf16[256,2048]{1,0:T(8,128)(2,1)}, f32[4,8,512]{2,1,0:T(8,128)}, f32[512,128]{1,0:T(8,128)}, bf16[512,2048]{1,0:T(8,12...) custom-call(bf16[256,2048]{1,0:T(8,128)(2,1)} %tok.3, ...), custom_call_target="tpu_custom_call" | custom-call | flops 21474836480 | bytes 41943040 | tf_op jit(solution)/shard_map/attend/pallas_call | solution.py:793
  168.9 182.2 %mlp.1 = (bf16[256,2048]{1,0:T(8,128)(2,1)}, bf16[2,704,512]{2,1,0:T(8,128)(2,1)}, bf16[2,704,512]{2,1,0:T(8,128)(2,1)}, bf16[2,704,512]{2,1,0:T(8,128)(2,1)}, b...) custom-call(bf16[256,2048]{1,0:T(8,128)(2,1)} %get-tuple-element.69.xn_in, ...), custom_call_target="tpu_custom_call" | custom-call | flops 35433480192 | bytes 41943040 | tf_op jit(solution)/shard_map/mlp/pallas_call | solution.py:473
  351.7 166.9 %grads.1 = (f32[256,2048]{1,0:T(8,128)}, f32[512,256]{1,0:T(8,128)}, f32[256,512]{1,0:T(8,128)}, f32[512,256]{1,0:T(8,128)}, f32[8,512]{1,0:T(8,128)}, /*index=5...) custom-call(bf16[256,2048]{1,0:T(8,128)(2,1)} %dy.1, ...), custom_call_target="tpu_custom_call" | custom-call | flops 32212254720 | bytes 41943040 | tf_op jit(solution)/shard_map/grads/pallas_call | solution.py:1373
  518.6 1.2 slice.6
  520.5 1.3 fusion.5
  522.4 1.3 convert_add_fusion.4
  524.0 1.2 fusion.9
  525.2 0.9 multiply_add_fusion.4
  527.0 1.2 fusion.10
  528.1 0.9 multiply_add_fusion.6
  529.9 1.2 fusion.11
  531.0 0.9 multiply_add_fusion.8
  532.9 0.9 copy-done.19
  534.3 1.1 copy-done.3
  535.9 2.3 fusion.6
  538.1 1.1 copy-done.4
  539.2 1.4 multiply_add_fusion.2
  540.7 1.1 copy-done
  541.8 3.9 fusion.7
  545.7 2.5 multiply_add_fusion
  548.2 4.1 fusion.12
  552.3 1.3 copy.59
  (87 shorter events, 5.9 us)
Async XLA Ops:
  7.2 541.0 %reduce-scatter.2.cloned.1.call-start = ((), (), s32[]{:S(2)}) async-start(), calls=%async_computation.1 | async-start | bytes 5242880 | tf_op jit(solution)/shard_map/reduce_scatter | solution.py:1465
  9.8 3.2 copy-start.15
  9.8 4.0 copy-start.13
  9.8 4.7 copy-start.11
  13.1 2.2 copy-start.35
  13.1 2.8 copy-start.2
  351.7 168.8 %copy-start.37 = (f32[2,512]{1,0:T(2,128)S(1)}, f32[2,512]{1,0:T(2,128)}, u32[]{:S(2)}) copy-start(f32[2,512]{1,0:T(2,128)} %param.42) | copy-start | bytes 12292
  351.7 170.2 %copy-start.36 = (f32[2,512]{1,0:T(2,128)S(1)}, f32[2,512]{1,0:T(2,128)}, u32[]{:S(2)}) copy-start(f32[2,512]{1,0:T(2,128)} %param.43) | copy-start | bytes 12292
  518.5 5.2 copy-start.32
  518.6 5.2 copy-start.33
  521.8 2.1 copy-start.34
  522.4 1.5 copy-start.12
  522.4 1.5 copy-start.26
  522.4 1.6 copy-start.31
  525.2 2.9 copy-start.8
  525.2 1.4 copy-start.14
  525.2 1.6 copy-start.27
  525.2 1.7 copy-start.30
  528.1 2.9 copy-start.9
  528.1 1.4 copy-start.16
  528.1 1.6 copy-start.28
  528.1 1.7 copy-start.29
  531.0 1.9 copy-start.10
  531.0 1.5 copy-start.21
  531.0 1.7 copy-start.22
  534.1 1.8 copy-start.17
  535.8 3.4 copy-start.18
  535.8 4.8 copy-start.6
  539.2 2.5 copy-start
  541.8 3.9 copy-start.5
  545.7 2.5 copy-start.1
  548.2 4.1 copy-start.7
  (7 other events, 8.5 us)
Sparse Core Ops, SparseCore 0:
  351.2 84.7 reduce-scatter.1

commit v4 on v3

--- a/solution.py
+++ b/solution.py
@@ -274,6 +274,16 @@
 
         push(d, c).start()
 
+    lower = at.z < nz - 1 - at.z
+
+    def near_relay(s, c):
+        pl.when(lower & (s > at.z))(lambda: relay(s, c, push_right))
+        pl.when(jnp.logical_not(lower) & (nz - 1 - s < at.z))(lambda: relay(nz - 1 - s, c, push_left))
+
+    def far_relay(s, c):
+        pl.when(jnp.logical_not(lower) & (s > at.z))(lambda: relay(s, c, push_right))
+        pl.when(lower & (nz - 1 - s < at.z))(lambda: relay(nz - 1 - s, c, push_left))
+
     def relays(s, c):
         pl.when(s > at.z)(lambda: relay(s, c, push_right))
         pl.when(nz - 1 - s < at.z)(lambda: relay(nz - 1 - s, c, push_left))
@@ -284,8 +294,11 @@
     def branch_copy(slot, j):
         return pltpu.make_async_copy(bown.at[slot], out_out.at[j], osem.at[slot])
 
+    def turn(k):
+        return near_first(jnp.where(k < 2, 1 - k, k), at.z, nz)
+
     def branch_sum(k):
-        j = near_first(k, at.z, nz)
+        j = turn(k)
         slot = lax.rem(k, 2)
         branch_swap(j).wait_recv()
 
@@ -309,12 +322,11 @@
             act[0, r, part] = (dmid * up * (sig * (1.0 + gate * (1.0 - sig)))).astype(LOW)
 
     def block(k, _):
-        pl.when((k == nz - 1) & (k >= 2))(lambda: line_step(k))
-        j = near_first(k, at.z, nz)
+        pl.when(k >= 2)(lambda: line_step(k))
+        j = turn(k)
         across(2 * j + 1 - at.c).wait_recv()
         slot = lax.rem(k, 2)
         forward(j)
-        pl.when((k >= 1) & (k < nz - 2))(lambda: line_step(k + 1))
         pl.when(k >= 1)(lambda: swap(j).wait_send())
         r = pl.ds(pl.multiple_of(j * 2 * R, 2 * R), 2 * R)
 
@@ -328,7 +340,7 @@
 
         lax.fori_loop(0, nd, back, 0)
         swap(j).start()
-        s = jnp.where(is_end, k, k - 1)
+        s = jnp.where(is_end, jnp.where(k < 2, 1 - k, k), k - 1)
 
         @pl.when((s >= 1) & (is_end | (s < nz - 2)))
         def _():
@@ -415,7 +427,9 @@
         middle = jnp.logical_not(is_end)
         early, late = p - 1, p // 2 - 3
         pl.when(middle & (early >= 0) & (early < CH))(lambda: relays(jnp.int32(nz - 2), early))
-        pl.when(middle & (lax.rem(p, 2) == 0) & (late >= 0) & (late < CH - 1))(lambda: relays(jnp.int32(nz - 1), late))
+        turn_now = middle & (lax.rem(p, 2) == 0) & (late >= 0) & (late < CH - 1)
+        pl.when(turn_now)(lambda: near_relay(jnp.int32(nz - 1), late))
+        pl.when(turn_now & (late >= 1))(lambda: far_relay(jnp.int32(nz - 1), late - 1))
         o = jnp.where(n == 1, order(1, i), order(0, i))
         for lo in range(0, F, 384):
             part = pl.ds(lo, min(384, F - lo))
@@ -426,7 +440,13 @@
         return 0
 
     lax.fori_loop(0, 3 * nd, wgrad, 0)
-    pl.when(jnp.logical_not(is_end))(lambda: relays(jnp.int32(nz - 1), jnp.int32(CH - 1)))
+
+    @pl.when(jnp.logical_not(is_end))
+    def _():
+        near_relay(jnp.int32(nz - 1), jnp.int32(CH - 1))
+        far_relay(jnp.int32(nz - 1), jnp.int32(CH - 2))
+        far_relay(jnp.int32(nz - 1), jnp.int32(CH - 1))
+
     for slot in range(2):
         branch_copy(slot, 0).wait()
 
@@ -554,10 +574,10 @@
                 self.across(o).wait_send()
 
 
-def attend_kernel(nd, nt, tok, gain, wq_in, wkv_in, wo_in, cosf, sins, lo_in, dy_in, w_in,
+def attend_kernel(nd, nt, tok, gain, wq_in, wkv_in, wo_in, cosf, sins, lo_row, dy_in, w_in,
                   h1_out, xn2_out, gfull, lse_out,
                   xn1_out, wq_out, wo_out, wkv_out, kv_out, q_out, o_out, dy_all, w_all,
-                  xn1, wq, wo, wkv, kvs, qs, os_, pback, precv,
+                  xn1, wq, wo, wkv, kvs, qs, os_, acc, pback, precv,
                   lsem, gs, gr, vx, vy, vxf, vyf, vr, qx, qy, qxf, qyf, qr, ox, oy, oxf, oyf, orr,
                   qlr, qll, qlv, olr, oll, olv, klr, kll, klv, klc, klcr, cs, cr, outs,
                   ylr, yll, ylv, ylc, mx, my, mxf, myf, mr, fsem):
@@ -565,7 +585,6 @@
     nz = at.nz
     R, D = tok.shape
     Dd, HC = wq_in.shape
-    TQ = min(256, 2 * R)
     rows = lambda t: pl.ds(pl.multiple_of(t * R, R), R)
     drows = lambda o: pl.ds(pl.multiple_of(o * Dd, Dd), Dd)
     hcols = lambda j: pl.ds(pl.multiple_of(j * HC, HC), HC)
@@ -676,8 +695,9 @@
         kv_across(o).wait_recv()
 
     scale = 1.0 / math.sqrt(HD)
-    S = kvs.shape[0]
-    lane = lax.broadcasted_iota(jnp.int32, (TQ, 128), 1)
+    KT = 2 * R
+    here = at.z * KT + lax.broadcasted_iota(jnp.int32, (1, KT), 1)
+    low_row = lo_row[0:1, :]
 
     def pair(k, _):
         j = near_first(k, at.z, nz)
@@ -688,28 +708,29 @@
             u = qpre[:, hh * HD:(hh + 1) * HD]
             qs[:, pl.ds(pl.multiple_of(j * HC + hh * HD, HD), HD)] = (u * cosf[...] + swap_halves(u) * sins[...]).astype(LOW)
 
-        def head(i, _):
-            hh, tq = lax.rem(i, HC // HD), i // (HC // HD)
-            rr = pl.ds(pl.multiple_of(tq * TQ, TQ), TQ)
+        for hh in range(HC // HD):
             cols = pl.ds(pl.multiple_of(j * HC + hh * HD, HD), HD)
-            s = dot_nt(qs[rr, cols], kvs[:, pl.ds(0, HD)])
-            place = lax.broadcasted_iota(jnp.int32, (TQ, S), 1)
-            here = at.z * 2 * R + tq * TQ + lax.broadcasted_iota(jnp.int32, (TQ, 1), 0)
-            s = jnp.where((place >= lo_in[rr, :]) & (place <= here), s * scale, MASKED)
-            m = jnp.max(s, axis=-1, keepdims=True)
-            p = jnp.exp(s - m)
-            total = jnp.sum(p, axis=-1, keepdims=True)
-            att = dot_nn(p.astype(LOW), kvs[:, pl.ds(HD, HD)])
-            os_[rr, cols] = (att / total).astype(LOW)
-            hid = j * (HC // HD) + hh
-            lse_out[rr, :] = jnp.where(lane == hid, m + jnp.log(total), lse_out[rr, :])
-            return 0
-
-        lax.fori_loop(0, (HC // HD) * (2 * R // TQ), head, 0)
+            qh = qs[:, cols]
+            acc[...] = jnp.zeros_like(acc)
+
+            def tile(b, carry):
+                top, total = carry
+                kr = pl.ds(pl.multiple_of(b * KT, KT), KT)
+                s = dot_nt(kvs[kr, pl.ds(0, HD)], qh)
+                place = b * KT + lax.broadcasted_iota(jnp.int32, (KT, KT), 0)
+                s = jnp.where((place >= low_row) & (place <= here), s * scale, MASKED)
+                new_top = jnp.maximum(top, jnp.max(s, axis=0, keepdims=True))
+                p = jnp.exp(s - new_top)
+                fade = jnp.exp(top - new_top)
+                acc[...] = acc[...] * fade + dot_tn(kvs[kr, pl.ds(HD, HD)], p.astype(LOW))
+                return new_top, total * fade + jnp.sum(p, axis=0, keepdims=True)
+
+            top, total = lax.fori_loop(0, at.z + 1, tile, (jnp.full((1, KT), MASKED, F32), jnp.zeros((1, KT), F32)))
+            os_[:, cols] = (acc[...] / total).T.astype(LOW)
+            lse_out[pl.ds(j * (HC // HD) + hh, 1), :] = top + jnp.log(total)
         go(k).forward_any()
         return 0
 
-    lse_out[...] = jnp.zeros_like(lse_out)
     lax.fori_loop(0, nz, pair, 0)
     for g in gw:
         g.start()
@@ -785,7 +806,7 @@
     dma = lambda *s: pltpu.SemaphoreType.DMA(s)
     hbm = pl.BlockSpec(memory_space=pltpu.HBM)
     vm = pl.BlockSpec(memory_space=pltpu.VMEM)
-    shapes = [((R, D), F32), ((R, D), LOW), ((nd, 8, Dd), F32), ((2 * R, 128), F32),
+    shapes = [((R, D), F32), ((R, D), LOW), ((nd, 8, Dd), F32), ((nz * (HC // HD), 2 * R), F32),
               ((2 * R, D), LOW), ((nz, D, HC), LOW), ((nd, nz * HC, Dd), LOW), ((D, 2 * HD), LOW), ((S, 2 * HD), LOW),
               ((2 * R, nz * HC), LOW), ((2 * R, nz * HC), LOW)]
     gathered = [((S, D), LOW), ((2, w.shape[1], D), LOW)]
@@ -795,7 +816,7 @@
         out_shape=tuple(jax.ShapeDtypeStruct(*s) for s in shapes + gathered),
         in_specs=[vm, vm, hbm, hbm, hbm, vm, vm, vm, hbm, hbm],
         out_specs=(vm, vm, vm, vm) + (hbm,) * 9,
-        scratch_shapes=[pltpu.VMEM(*s) for s in shapes[4:]] + [pltpu.VMEM((R, D), LOW), pltpu.VMEM((R, D), LOW)]
+        scratch_shapes=[pltpu.VMEM(*s) for s in shapes[4:]] + [pltpu.VMEM((HD, 2 * R), F32), pltpu.VMEM((R, D), LOW), pltpu.VMEM((R, D), LOW)]
         + [dma(3), dma(nd - 1), dma(nd - 1)] + yg(2) + yg(nz) + yg(nz)
         + [dma(nz)] * 3 + [dma(nz)] * 3 + [dma(nz)] * 5 + [dma(2), dma(2), dma(7)]
         + [dma(nz), dma(nz), dma(2, nz), dma(nz)] + yg(2) + [dma(3)],
@@ -886,7 +907,7 @@
                  h1_in, dxn2_in, xn1_in, wq_in, wo_in, wkv_in, kv_in, q_in, o_in,
                  mine_g, land_g, mine_u, land_u, down_in,
                  tgrad, gq_out, go_out, gkv_out, gg_out, norm_out, keep_g, keep_u, keep_d, keep_e, got_g, got_u, got_d, got_e,
-                 xn1, wq, wo, wkv, kvs, qs, os_, dos, dh1b, dxn1, lset, dkv, dq,
+                 xn1, wq, wo, wkv, kvs, qs, os_, dos, dh1b, dxn1, dkv, dq,
                  bg, bu, bd, be, lg, lu, ld, le, tg, tu, td, te,
                  ql, ql2, ol, ol2, qz, oz, qlz, olz, kvb, kland, kz, xrecv, wl, wcl, wd2, w2, w2l, wfin, gl, gpart, u2, u2l, gfin, share, norms, normd,
                  lsem, xsem, fs, fr, qss, qsr, qss2, qsr2, oss, osr, oss2, osr2, qzs, qzr, ozs, ozr,
@@ -1013,7 +1034,6 @@
         sq(k).either("total", put)
         pl.when(k < nz - 1)(lambda: zpush(k, qz, qlz, qzs, qzr).start())
 
-    lset[...] = lse[...].T
     dkv[...] = jnp.zeros_like(dkv)
     dxn1[...] = jnp.zeros_like(dxn1)
     here = at.z * KT + lax.broadcasted_iota(jnp.int32, (1, KT), 1)
@@ -1024,7 +1044,7 @@
         for hh in range(NH):
             cols = pl.ds(pl.multiple_of(j * HC + hh * HD, HD), HD)
             hid = j * NH + hh
-            lrow = lset[pl.ds(hid, 1), :]
+            lrow = lse[pl.ds(hid, 1), :]
             qh = qs[:, cols]
             doh = dos[:, cols]
             delta = jnp.sum((doh.astype(F32) * os_[:, cols].astype(F32)).T, axis=0, keepdims=True)
@@ -1377,7 +1397,7 @@
         out_specs=(vm,) * 6 + (hbm,) * 8,
         scratch_shapes=[
             b(2 * R, D), b(nz, D, HC), b(nd, nz * HC, Dd), b(D, W2), b(S, W2), b(2 * R, nz * HC), b(2 * R, nz * HC), b(2 * R, nz * HC),
-            b(2 * R, D), f(2 * R, D), f(128, 2 * R), f(S, W2), f(2 * R, HD),
+            b(2 * R, D), f(2 * R, D), f(S, W2), f(2 * R, HD),
             b(2, F, Dd), b(ny, F, Dd), b(2, Fh, Dd), b(ny, Fh, Dd),
             b(1, F, Dd), b(hops, F, Dd), b(1, Fh, Dd), b(hops, Fh, Dd),
             b(2 * (ny - 1), F, Dd), b(ny, F, Dd), b(2 * (ny - 1), Fh, Dd), b(ny, Fh, Dd),
@@ -1454,10 +1474,11 @@
     cosine, sine = jnp.cos(angles), jnp.sin(angles)
     cosine_full = jnp.concatenate([cosine, cosine], axis=1)
     sine_full = jnp.concatenate([-sine, sine], axis=1)
+    first_rows = jnp.broadcast_to(first[None, :], (8, pair_rows))
     gain_rows = jnp.pad(low_gains.astype(F32), ((0, 6), (0, 0)))
 
     hidden_one, normed_two, gains_all, lse, normed_one, all_query, all_output, all_kv, kv_rows, queries, attended, grad_rows, gate_up = attend(
-        nd, nt, tokens, gain_rows, low_query, low_kv, low_output, cosine_full, sine_full, first[:, None],
+        nd, nt, tokens, gain_rows, low_query, low_kv, low_output, cosine_full, sine_full, first_rows,
         cotangent, low_gateup
     )
     grad_normed_two, *pieces, mlp_rows = mlp(nd, nt, normed_two, grad_rows, gate_up, low_down)
@@ -1467,7 +1488,7 @@
     tokens_grad, own_query, own_output, grad_keyvalue, gains_sum, norm_tile, *halves = grads(
         nd,
         nt,
-        (cotangent, tokens, gains_all, cosine_full, sine_full, jnp.broadcast_to(first[None, :], (8, pair_rows)), lse, kv_later),
+        (cotangent, tokens, gains_all, cosine_full, sine_full, first_rows, lse, kv_later),
         (hidden_one, grad_normed_two, normed_one, all_query, all_output, all_kv, kv_rows, queries, attended),
         pieces,
     )

time: 568 us -> 532 us (0.937)
  Pallas kernels: 499 us -> 462 us
    pallas_call x1, Pallas kernels: 182 us -> 140 us  [mlp(): pl.pallas_call(functools.partial(mlp_kernel, nd, nt), out_shape=(shape(R,...]
    pallas_call x1, Pallas kernels: 167 us -> 173 us  [grads(): pl.pallas_call(functools.partial(grads_kernel, nd, nt), out_shape=tuple([...]
  transfers between devices with their start and end apart: 1 -> 1, of which waited for: 0 -> 0; matrix products, arithmetic and copies ran while one was open for 4% -> 4% of each run, Pallas kernels for 30% -> 33%
where the time goes in v4:
time: 532 us; the launch traced here: 525 us
  Pallas kernels  462 us (87%)
  other arithmetic  37 us (7%)
  between operations  15.5 us (3%)
  local copies, waits for them, and re-layouts  10.7 us (2%)
    pallas_call x1, Pallas kernels, grads(): pl.pallas_call(functools.partial(grads_kernel, nd, nt), out_shape=tuple([...  173 us
    pallas_call x1, Pallas kernels, attend(): pl.pallas_call(functools.partial(attend_kernel, nd, nt), out_shape=tuple(...  150 us
    pallas_call x1, Pallas kernels, mlp(): pl.pallas_call(functools.partial(mlp_kernel, nd, nt), out_shape=(shape(R,...  140 us
    convert_element_type x6, other arithmetic, advance(): weight_new.astype(jnp.bfloat16)  11.1 us
  transfers between devices with their start and end apart: 1, of which 0 were waited for; matrix products, arithmetic and copies ran while one was open for 4% of the time, Pallas kernels for 33%

profile of v4, /device:TPU:0, one launch (start us, length us, event | category | flops | bytes accessed | tf_op | source)
XLA Modules:
  0.0 525.2 jit_solution(5405775525873427874)
XLA Ops:
  7.3 0.9 reduce-window.4
  8.2 0.7 fusion.4
  8.9 0.7 convert_element_type.76
  10.4 1.8 convert_element_type.77.wq_in
  12.1 1.8 convert_element_type.78.wkv_in
  13.9 1.9 convert_element_type.79.wo_in
  15.8 0.9 convert_element_type.84.w_in
  16.8 1.3 convert_bitcast_fusion.w_in
  18.1 1.0 fusion.3
  19.1 1.0 pad_maximum_fusion
  20.7 149.8 %attend.1 = (f32[256,2048]{1,0:T(8,128)}, bf16[256,2048]{1,0:T(8,128)(2,1)}, f32[4,8,512]{2,1,0:T(8,128)}, f32[8,512]{1,0:T(8,128)}, bf16[512,2048]{1,0:T(8,128)...) custom-call(bf16[256,2048]{1,0:T(8,128)(2,1)} %tok.3, ...), custom_call_target="tpu_custom_call" | custom-call | flops 21474836480 | bytes 41943040 | tf_op jit(solution)/shard_map/attend/pallas_call | solution.py:814
  170.5 139.6 %mlp.1 = (bf16[256,2048]{1,0:T(8,128)(2,1)}, bf16[2,704,512]{2,1,0:T(8,128)(2,1)}, bf16[2,704,512]{2,1,0:T(8,128)(2,1)}, bf16[2,704,512]{2,1,0:T(8,128)(2,1)}, b...) custom-call(bf16[256,2048]{1,0:T(8,128)(2,1)} %get-tuple-element.69.xn_in, ...), custom_call_target="tpu_custom_call" | custom-call | flops 35433480192 | bytes 41943040 | tf_op jit(solution)/shard_map/mlp/pallas_call | solution.py:493
  310.2 172.6 %grads.1 = (f32[256,2048]{1,0:T(8,128)}, f32[512,256]{1,0:T(8,128)}, f32[256,512]{1,0:T(8,128)}, f32[512,256]{1,0:T(8,128)}, f32[8,512]{1,0:T(8,128)}, /*index=5...) custom-call(bf16[256,2048]{1,0:T(8,128)(2,1)} %dy.1, ...), custom_call_target="tpu_custom_call" | custom-call | flops 32212254720 | bytes 41943040 | tf_op jit(solution)/shard_map/grads/pallas_call | solution.py:1393
  482.8 1.3 slice.6
  484.8 1.3 fusion.5
  486.7 1.3 convert_add_fusion.4
  488.3 1.2 fusion.10
  489.5 0.9 multiply_add_fusion.6
  491.2 1.2 fusion.9
  492.4 0.9 multiply_add_fusion.4
  494.1 1.2 fusion.11
  495.3 0.9 multiply_add_fusion.8
  497.2 0.9 copy-done.17
  498.6 1.1 copy-done.4
  500.1 2.3 fusion.6
  502.4 1.1 copy-done.5
  503.5 1.4 multiply_add_fusion.2
  505.0 1.1 copy-done.1
  506.0 3.9 fusion.7
  510.0 2.5 multiply_add_fusion
  512.5 4.1 fusion.12
  516.6 1.3 copy.57
  (82 shorter events, 5.9 us)
Async XLA Ops:
  7.2 8.6 %copy-start.3 = (f32[704,512]{1,0:T(8,128)S(1)}, f32[704,512]{1,0:T(8,128)}, u32[]{:S(2)}) copy-start(f32[704,512]{1,0:T(8,128)} %param.38) | copy-start | bytes 4325380
  7.2 505.3 %reduce-scatter.2.cloned.1.call-start = ((), (), s32[]{:S(2)}) async-start(), calls=%async_computation.1 | async-start | bytes 5242880 | tf_op jit(solution)/shard_map/reduce_scatter | solution.py:1486
  13.9 2.9 copy-start
  310.2 174.6 %copy-start.33 = (f32[2,512]{1,0:T(2,128)S(1)}, f32[2,512]{1,0:T(2,128)}, u32[]{:S(2)}) copy-start(f32[2,512]{1,0:T(2,128)} %param.41) | copy-start | bytes 12292
  310.2 174.6 %copy-start.35 = (f32[2,512]{1,0:T(2,128)S(1)}, f32[2,512]{1,0:T(2,128)}, u32[]{:S(2)}) copy-start(f32[2,512]{1,0:T(2,128)} %param.42) | copy-start | bytes 12292
  310.2 175.9 %copy-start.34 = (f32[2,512]{1,0:T(2,128)S(1)}, f32[2,512]{1,0:T(2,128)}, u32[]{:S(2)}) copy-start(f32[2,512]{1,0:T(2,128)} %param.43) | copy-start | bytes 12292
  482.8 5.2 copy-start.30
  482.8 5.2 copy-start.31
  486.1 2.1 copy-start.32
  486.7 1.5 copy-start.12
  486.7 1.5 copy-start.24
  486.7 1.6 copy-start.29
  489.5 2.9 copy-start.9
  489.5 1.4 copy-start.13
  489.5 1.6 copy-start.25
  489.5 1.7 copy-start.28
  492.4 2.9 copy-start.10
  492.4 1.4 copy-start.14
  492.4 1.6 copy-start.26
  492.4 1.7 copy-start.27
  495.3 1.9 copy-start.11
  495.3 1.5 copy-start.19
  495.3 1.7 copy-start.20
  497.0 1.3 copy-start.18
  498.3 1.4 copy-start.4
  498.3 1.8 copy-start.15
  500.1 3.4 copy-start.16
  500.1 4.8 copy-start.7
  503.5 2.5 copy-start.1
  506.0 3.9 copy-start.6
  510.0 2.5 copy-start.2
  512.5 4.1 copy-start.8
  (5 other events, 5.8 us)
Sparse Core Ops, SparseCore 0:
  310.3 86.7 reduce-scatter.1

commit v5 on v4

--- a/solution.py
+++ b/solution.py
@@ -1137,6 +1137,15 @@
     for zz in range(nz):
         wswap(zz).start()
     lax.fori_loop(max(nz - 2, 1), nz, lambda k, _: (sq(k).either("middle"), 0)[1], 0)
+    for s in range(1, nz + 1):
+        zz = lax.rem(at.z + s, nz)
+        r = slices(2 * zz + at.c)
+        remote(wd2.at[slices(0)], wcl.at[zz], wcs.at[zz], wcr.at[zz], at.dp, at.sibling()).wait_recv()
+        wd2[r, :] = (wd2[r, :].astype(F32) + wcl[zz].astype(F32)).astype(LOW)
+        if s < nz:
+            wpush(s).start()
+    o_total(k_last)
+
     big = []
     for n, (buf, got, second) in enumerate([(bg, tg, lg), (bu, tu, lu), (bd, td, ld), (be, te, le)]):
         if n < 2:
@@ -1166,15 +1175,6 @@
             total = total + got[slot].astype(F32)
         buf[keep] = total.astype(LOW)
         big.append((buf, keep, second, copies))
-
-    for s in range(1, nz + 1):
-        zz = lax.rem(at.z + s, nz)
-        r = slices(2 * zz + at.c)
-        remote(wd2.at[slices(0)], wcl.at[zz], wcs.at[zz], wcr.at[zz], at.dp, at.sibling()).wait_recv()
-        wd2[r, :] = (wd2[r, :].astype(F32) + wcl[zz].astype(F32)).astype(LOW)
-        if s < nz:
-            wpush(s).start()
-    o_total(k_last)
 
     xswap.wait_recv()
     for o in range(nd):

time: 532 us -> 532 us (level)
  no operation moved by 1% of the time
where the time goes in v5:
time: 532 us; the launch traced here: 526 us
  Pallas kernels  462 us (87%)
  other arithmetic  37 us (7%)
  between operations  15.5 us (3%)
  local copies, waits for them, and re-layouts  10.7 us (2%)
    pallas_call x1, Pallas kernels, grads(): pl.pallas_call(functools.partial(grads_kernel, nd, nt), out_shape=tuple([...  173 us
    pallas_call x1, Pallas kernels, attend(): pl.pallas_call(functools.partial(attend_kernel, nd, nt), out_shape=tuple(...  150 us
    pallas_call x1, Pallas kernels, mlp(): pl.pallas_call(functools.partial(mlp_kernel, nd, nt), out_shape=(shape(R,...  140 us
    convert_element_type x6, other arithmetic, advance(): weight_new.astype(jnp.bfloat16)  11.1 us
  transfers between devices with their start and end apart: 1, of which 0 were waited for; matrix products, arithmetic and copies ran while one was open for 4% of the time, Pallas kernels for 33%

profile of v5, /device:TPU:0, one launch (start us, length us, event | category | flops | bytes accessed | tf_op | source)
XLA Modules:
  0.0 525.6 jit_solution(17154551475583791263)
XLA Ops:
  7.3 0.9 reduce-window.4
  8.2 0.7 fusion.4
  8.9 0.7 convert_element_type.76
  10.4 1.8 convert_element_type.77.wq_in
  12.1 1.8 convert_element_type.78.wkv_in
  13.9 1.9 convert_element_type.79.wo_in
  15.8 0.9 convert_element_type.84.w_in
  16.8 1.3 convert_bitcast_fusion.w_in
  18.1 1.0 fusion.3
  19.1 1.0 pad_maximum_fusion
  20.7 149.8 %attend.1 = (f32[256,2048]{1,0:T(8,128)}, bf16[256,2048]{1,0:T(8,128)(2,1)}, f32[4,8,512]{2,1,0:T(8,128)}, f32[8,512]{1,0:T(8,128)}, bf16[512,2048]{1,0:T(8,128)...) custom-call(bf16[256,2048]{1,0:T(8,128)(2,1)} %tok.3, ...), custom_call_target="tpu_custom_call" | custom-call | flops 21474836480 | bytes 41943040 | tf_op jit(solution)/shard_map/attend/pallas_call | solution.py:814
  170.5 139.6 %mlp.1 = (bf16[256,2048]{1,0:T(8,128)(2,1)}, bf16[2,704,512]{2,1,0:T(8,128)(2,1)}, bf16[2,704,512]{2,1,0:T(8,128)(2,1)}, bf16[2,704,512]{2,1,0:T(8,128)(2,1)}, b...) custom-call(bf16[256,2048]{1,0:T(8,128)(2,1)} %get-tuple-element.69.xn_in, ...), custom_call_target="tpu_custom_call" | custom-call | flops 35433480192 | bytes 41943040 | tf_op jit(solution)/shard_map/mlp/pallas_call | solution.py:493
  310.2 172.9 %grads.1 = (f32[256,2048]{1,0:T(8,128)}, f32[512,256]{1,0:T(8,128)}, f32[256,512]{1,0:T(8,128)}, f32[512,256]{1,0:T(8,128)}, f32[8,512]{1,0:T(8,128)}, /*index=5...) custom-call(bf16[256,2048]{1,0:T(8,128)(2,1)} %dy.1, ...), custom_call_target="tpu_custom_call" | custom-call | flops 32212254720 | bytes 41943040 | tf_op jit(solution)/shard_map/grads/pallas_call | solution.py:1393
  483.2 1.3 slice.6
  485.1 1.3 fusion.5
  487.1 1.3 convert_add_fusion.4
  488.6 1.2 fusion.10
  489.8 0.9 multiply_add_fusion.6
  491.5 1.2 fusion.9
  492.8 0.9 multiply_add_fusion.4
  494.5 1.2 fusion.11
  495.7 0.9 multiply_add_fusion.8
  497.6 0.9 copy-done.17
  498.9 1.1 copy-done.4
  500.5 2.3 fusion.6
  502.8 1.1 copy-done.5
  503.9 1.4 multiply_add_fusion.2
  505.3 1.1 copy-done.1
  506.4 3.9 fusion.7
  510.3 2.5 multiply_add_fusion
  512.8 4.1 fusion.12
  517.0 1.3 copy.57
  (82 shorter events, 5.9 us)
Async XLA Ops:
  7.2 8.6 %copy-start.3 = (f32[704,512]{1,0:T(8,128)S(1)}, f32[704,512]{1,0:T(8,128)}, u32[]{:S(2)}) copy-start(f32[704,512]{1,0:T(8,128)} %param.38) | copy-start | bytes 4325380
  7.2 505.6 %reduce-scatter.2.cloned.1.call-start = ((), (), s32[]{:S(2)}) async-start(), calls=%async_computation.1 | async-start | bytes 5242880 | tf_op jit(solution)/shard_map/reduce_scatter | solution.py:1486
  13.9 2.9 copy-start
  310.2 174.9 %copy-start.33 = (f32[2,512]{1,0:T(2,128)S(1)}, f32[2,512]{1,0:T(2,128)}, u32[]{:S(2)}) copy-start(f32[2,512]{1,0:T(2,128)} %param.41) | copy-start | bytes 12292
  310.2 174.9 %copy-start.35 = (f32[2,512]{1,0:T(2,128)S(1)}, f32[2,512]{1,0:T(2,128)}, u32[]{:S(2)}) copy-start(f32[2,512]{1,0:T(2,128)} %param.42) | copy-start | bytes 12292
  310.2 176.3 %copy-start.34 = (f32[2,512]{1,0:T(2,128)S(1)}, f32[2,512]{1,0:T(2,128)}, u32[]{:S(2)}) copy-start(f32[2,512]{1,0:T(2,128)} %param.43) | copy-start | bytes 12292
  483.1 5.2 copy-start.30
  483.1 5.2 copy-start.31
  486.4 2.1 copy-start.32
  487.1 1.5 copy-start.12
  487.1 1.5 copy-start.24
  487.1 1.6 copy-start.29
  489.8 2.9 copy-start.9
  489.8 1.4 copy-start.13
  489.8 1.6 copy-start.25
  489.8 1.7 copy-start.28
  492.7 2.9 copy-start.10
  492.7 1.4 copy-start.14
  492.7 1.6 copy-start.26
  492.7 1.7 copy-start.27
  495.6 1.9 copy-start.11
  495.6 1.5 copy-start.19
  495.6 1.7 copy-start.20
  497.3 1.3 copy-start.18
  498.7 1.4 copy-start.4
  498.7 1.8 copy-start.15
  500.5 3.4 copy-start.16
  500.5 4.8 copy-start.7
  503.9 2.5 copy-start.1
  506.4 3.9 copy-start.6
  510.3 2.5 copy-start.2
  512.8 4.1 copy-start.8
  (5 other events, 5.8 us)
Sparse Core Ops, SparseCore 0:
  310.3 86.7 reduce-scatter.1
